TPU v7x, 256 devices: a whole 4x4x8 slice. The times are simulated.
256 devices in a mesh: phase: 4 (over x), ctx: 64 (over z, y, core).
Axes of the slice: x: 4, y: 4, z: 8, core: 2. Of those that a mesh axis runs over, the one named last changes fastest.
Arguments:
- tokens: bfloat16 [1, 8192, 4096], P(None, 'ctx', 'phase'), may hold values from -6 to 6
- queries: bfloat16 [4, 1, 8192, 4096], P('phase', None, 'ctx'), may hold values from -2 to 2
- keys_in: bfloat16 [4, 1, 8192, 4096], P('phase', None, 'ctx'), may hold values from -2 to 2
- values: bfloat16 [4, 1, 8192, 4096], P('phase', None, 'ctx'), may hold values from -6 to 6
- norm_gain: bfloat16 [4, 4096], P('phase'), may hold values from 0.5 to 1.5
- log_decay: float32 [4, 1, 32, 8192], P('phase', None, None, 'ctx'), may hold values from -1.2 to 0, as said below
- doc_ids: int32 [1, 8192], P(None, 'ctx'), may hold values from 0 to 7, never falling along the last dimension, each value on 1 to 4096 neighbouring positions
Outputs:
- phase_out: bfloat16 [4, 1, 8192, 4096], P('phase', None, 'ctx')
Inputs may be any that keep to these rules, and one draw needn't show every extreme that they name: `log_decay`: each entry is the log of one position's decay factor for one head.
All inputs are finite; a program needn't handle non-finite values.
Results may differ from a plain program's by a relative error of at most 0.006.
Values may be sent and summed in bfloat16 or wider, within the bound.
No kernel may reach another device: no remote copies, remote signals or barrier semaphores. Data moves between devices by JAX's collectives and lax.ppermute only.
A program may use at most 320 MiB of HBM per device.

v0:
```python
import jax
import jax.numpy as jnp
from jax import lax
from jax.sharding import PartitionSpec as P

EPSILON = 1e-05


def shifted(array, axis, by):
    size = lax.axis_size(axis)
    pairs = [(i, i + by) for i in range(size) if 0 <= i + by < size]
    return lax.ppermute(array, axis, pairs)


def local_terms(queries, keys_all, values, block_decay, block_document_ids):
    decay_sum = jnp.cumsum(block_decay, axis=1)
    length = block_document_ids.shape[0]
    steps = jnp.arange(length)
    allowed = (steps[None, :] <= steps[:, None]) & (
        block_document_ids[None, :] == block_document_ids[:, None]
    )
    spread = decay_sum[:, :, None] - decay_sum[:, None, :]
    weighting = jnp.where(allowed[None], jnp.exp(jnp.minimum(spread, 0.0)), 0.0)
    scores = jnp.einsum("thd,shd->hts", queries, keys_all, preferred_element_type=jnp.float32)
    attn = (scores * weighting).astype(jnp.bfloat16)
    intra = jnp.einsum("hts,shd->thd", attn, values, preferred_element_type=jnp.float32)
    same_doc = (block_document_ids == block_document_ids[-1]).astype(jnp.float32)
    carried = jnp.exp(decay_sum[:, -1:] - decay_sum) * same_doc[None, :]
    keyed = (keys_all * carried.T[:, :, None]).astype(jnp.bfloat16)
    summary = jnp.einsum("thi,thj->hij", keyed, values, preferred_element_type=jnp.float32)
    factor = jnp.exp(decay_sum[:, -1]) * (block_document_ids[0] == block_document_ids[-1]).astype(
        jnp.float32
    )
    return (decay_sum, intra, summary, factor)


def link(earlier, later):
    first_one, last_one, factor_one, state_one = earlier
    first_two, last_two, factor_two, state_two = later
    joined = ((last_one == first_two) | (last_one < 0.0) | (first_two < 0.0)).astype(jnp.float32)
    factor_new = factor_one * factor_two * joined
    state_new = factor_two * joined * state_one + state_two
    first_new = jnp.where(first_one < 0.0, first_two, first_one)
    last_new = jnp.where(last_two < 0.0, last_one, last_two)
    return (first_new, last_new, factor_new, state_new)


def incoming_state(summary, factor, block_document_ids):
    head_count = summary.shape[0]
    head_size = summary.shape[1]
    first_id = block_document_ids[0].astype(jnp.float32)
    last_id = block_document_ids[-1].astype(jnp.float32)
    members = lax.axis_size("ctx")
    total = head_count * head_size * head_size
    slab = total // members
    plane = head_size * head_size
    per_slab = max(1, slab // plane)
    span = slab // per_slab
    flat = summary.reshape(members, slab)
    meta = jnp.concatenate([factor, jnp.stack([first_id, last_id])])
    tiled = jnp.broadcast_to(meta[None, :], (members, head_count + 2))
    received, info = (
        lax.all_to_all(flat, "ctx", split_axis=0, concat_axis=0, tiled=True),
        lax.all_to_all(tiled, "ctx", split_axis=0, concat_axis=0, tiled=True),
    )
    head_start = lax.axis_index("ctx") * slab // plane
    factors_in = lax.dynamic_slice_in_dim(info[:, :head_count], head_start, per_slab, 1).reshape(
        members, per_slab, 1
    )
    firsts = info[:, head_count].reshape(members, 1, 1)
    lasts = info[:, head_count + 1].reshape(members, 1, 1)
    pieces = received.reshape(members, per_slab, span)
    inclusive = lax.associative_scan(link, (firsts, lasts, factors_in, pieces), axis=0)
    last_before = jnp.concatenate(
        [jnp.full((1, 1, 1), -1.0, jnp.float32), inclusive[1][:-1]], axis=0
    )
    state_before = jnp.concatenate(
        [jnp.zeros((1, per_slab, span), jnp.float32), inclusive[3][:-1]], axis=0
    )
    sending = (state_before * (last_before == firsts).astype(jnp.float32)).reshape(members, slab)
    returned = lax.all_to_all(
        sending.astype(jnp.bfloat16), "ctx", split_axis=0, concat_axis=0, tiled=True
    ).astype(sending.dtype)
    return returned.reshape(head_count, head_size, head_size)


def attention_term(query_rows, key_rows, value_rows, gain, block_decay, block_document_ids):
    length = query_rows.shape[0]
    width = query_rows.shape[1]
    head_count = block_decay.shape[0]
    head_size = width // head_count
    queries_split = query_rows.reshape(length, head_count, head_size)
    divided_key_tiles = key_rows.reshape(length, head_count, head_size)
    values_split = value_rows.reshape(length, head_count, head_size)
    decay_sum, intra, summary, factor = local_terms(
        queries_split, divided_key_tiles, values_split, block_decay, block_document_ids
    )
    prefix = incoming_state(summary, factor, block_document_ids)
    leading = (block_document_ids == block_document_ids[0]).astype(jnp.float32)
    inter = jnp.einsum(
        "thi,hij->thj",
        queries_split,
        prefix.astype(jnp.bfloat16),
        preferred_element_type=jnp.float32,
    )
    scaling = jnp.exp(decay_sum).T * leading[:, None]
    total = intra + inter * scaling[:, :, None]
    power = jnp.mean(total * total, axis=-1, keepdims=True)
    normed = (
        total * lax.rsqrt(power + EPSILON) * gain.reshape(head_count, head_size).astype(jnp.float32)
    )
    return normed.reshape(length, width)


def local(tokens, queries, keys_in, values, norm_gain, log_decay, doc_ids):
    phase_count = lax.axis_size("phase")
    phase_pos = lax.axis_index("phase")
    whole_input = lax.all_gather(tokens, "phase", axis=2, tiled=True)
    gain = norm_gain[0]
    normed = attention_term(
        queries[0, 0], keys_in[0, 0], values[0, 0], gain, log_decay[0, 0], doc_ids[0]
    )
    current = (whole_input[0].astype(jnp.float32) + normed).astype(jnp.bfloat16)
    for round_position in range(1, phase_count):
        arrived = shifted(current, "phase", 1)
        updated = (arrived.astype(jnp.float32) + normed).astype(jnp.bfloat16)
        current = jnp.where(phase_pos == round_position, updated, current)
    results = [current]
    return jnp.stack(results)[None]


def solution(mesh):
    return jax.shard_map(
        local,
        mesh=mesh,
        in_specs=(
            P(None, "ctx", "phase"),
            P("phase", None, "ctx", None),
            P("phase", None, "ctx", None),
            P("phase", None, "ctx", None),
            P("phase", None),
            P("phase", None, None, "ctx"),
            P(None, "ctx"),
        ),
        out_specs=P("phase", None, "ctx", None),
        check_vma=False,
    )
```

profile of v0, /device:TPU:34, one launch (start us, length us, event | category | flops | bytes accessed | tf_op | source)
XLA Modules:
  0.0 313.2 jit_solution(8627268717883827144)
XLA Ops:
  6.5 1.4 fusion.34
  10.4 1.0 reduce_window_sum.11
  11.7 0.6 broadcast_in_dim.9
  12.3 11.8 %all-to-all-start.1 = ((f32[64,1,34]{2,1,0:T(1,128)}), f32[64,1,34]{2,1,0:T(1,128)S(1)}, u32[]{:S(2)}, u32[]{:S(2)}) async-start(f32[64,1,34]{2,1,0:T(1,128)} %broadcast_in_dim.9), calls=%async_computation.1 | async-start | bytes 65536 | tf_op jit(solution)/shard_map/all_to_all | solution.py:64
  24.1 1.3 compare_convert_fusion
  25.5 1.2 fusion.24
  26.7 1.6 copy.38
  28.6 0.8 multiply_bitcast_fusion
  29.3 2.0 fusion.3
  31.4 1.3 all-to-all-done.1
  32.7 9.3 %all-to-all-start = ((f32[64,1,8192]{2,1,0:T(1,128)}), f32[64,1,8192]{2,1,0:T(1,128)S(1)}, u32[]{:S(2)}, u32[]{:S(2)}) async-start(f32[64,1,8192]{2,1,0:T(1,128)} %bitcast.74), calls=%async_computation | async-start | bytes 4194304 | tf_op jit(solution)/shard_map/all_to_all | solution.py:63
  45.6 0.6 slice.383
  49.3 0.6 slice.374
  51.8 0.7 pad_add_fusion.1
  53.8 0.7 slice.376
  55.8 0.6 slice.424
  59.0 0.7 pad_maximum_fusion.6
  62.8 0.7 pad_maximum_fusion.10
  65.0 0.6 compare_convert_fusion.1
  65.6 26.6 %all-to-all-done = f32[64,1,8192]{2,1,0:T(1,128)S(1)} async-done(((f32[64,1,8192]{2,1,0:T(1,128)}), f32[64,1,8192]{2,1,0:T(1,128)S(1)}, u32[]{:S(2)}, u32[]{:S(2)}) %all-to-all-start) | async-done | bytes 2097184 | tf_op jit(solution)/shard_map/all_to_all | solution.py:63
  92.3 1.3 slice_add_fusion
  93.6 1.0 copy-done.2
  94.5 0.6 slice_add_fusion.1
  95.2 0.6 slice.408
  96.1 0.6 slice.409
  98.0 0.7 fusion.21
  98.8 0.9 pad_maximum_fusion.3
  100.2 1.0 fusion.20
  102.8 0.8 copy-done.4
  103.6 1.4 add.167
  105.0 6.8 %pad.94 = f32[32,1,8192]{2,1,0:T(1,128)S(1)} pad(f32[16,1,8192]{2,1,0:T(1,128)} %add.167, f32[]{:T(128)} %constant.68.clone.1), padding=1_0_1x0_0_0x0_0_0 | pad | bytes 1572868 | tf_op jit(solution)/shard_map/pad | solution.py:73
  111.8 2.1 fusion.19
  113.9 1.3 pad_maximum_fusion.1
  115.2 9.6 %pad.93 = f32[32,1,8192]{2,1,0:T(1,128)} pad(f32[16,1,8192]{2,1,0:T(1,128)} %pad_maximum_fusion.1, f32[]{:T(128)} %constant.68.clone.1), padding=0_1_1x0_0_0x0_0_0 | pad | bytes 1572868 | tf_op jit(solution)/shard_map/pad | solution.py:73
  124.8 3.4 %add.169 = f32[32,1,8192]{2,1,0:T(1,128)} add(f32[32,1,8192]{2,1,0:T(1,128)} %pad.93, f32[32,1,8192]{2,1,0:T(1,128)S(1)} %pad.94) | non-fusion elementwise | flops 262144 | bytes 3145728 | tf_op jit(solution)/shard_map/add | solution.py:73
  128.2 2.5 fusion.13
  130.7 1.0 pad_maximum_fusion
  131.7 12.3 %pad.126 = f32[63,1,8192]{2,1,0:T(1,128)} pad(f32[32,1,8192]{2,1,0:T(1,128)S(1)} %pad_maximum_fusion, f32[]{:T(128)} %constant.68.clone.1), padding=0_0_1x0_0_0x0_0_0 | pad | bytes 3112964 | tf_op jit(solution)/shard_map/slice | solution.py:78
  143.9 2.6 pad.167
  146.6 5.7 %slice_add_fusion.7 = f32[63,1,8192]{2,1,0:T(1,128)S(1)} fusion(f32[63,1,8192]{2,1,0:T(1,128)} %pad.126, f32[64,1,8192]{2,1,0:T(1,128)S(1)} %pad.167), kind=kLoop, calls=%fused_computation.116 | loop fusion | flops 516096 | bytes 6193152 | tf_op jit(solution)/shard_map/add | solution.py:73
  152.4 3.5 %multiply_convert_fusion = bf16[64,1,8192]{2,1,0:T(2,128)(2,1)S(1)} fusion(f32[63,1,8192]{2,1,0:T(1,128)S(1)} %slice_add_fusion.7, f32[64]{0:T(128)S(1)} %copy-done.17), kind=kLoop, calls=%fused_computation.9 | loop fusion | flops 1048576 | bytes 3113216 | tf_op jit(solution)/shard_map/convert_element_type | solution.py:82
  156.4 7.2 %reduce.10 = bf16[64,8192]{1,0:T(8,128)(2,1)S(1)} reduce(bf16[64,1,8192]{2,1,0:T(2,128)(2,1)S(1)} %multiply_convert_fusion, bf16[]{:T(256)} %broadcast.226), dimensions={1}, to_apply=%multiply_convert_fusion.reduce_sub_computation | reduce | bytes 2097154 | tf_op jit(solution)/shard_map/convert_element_type | solution.py:82
  163.5 1.8 reshape.163
  165.3 6.4 %all-to-all-start.2 = ((bf16[64,2,4096]{2,1,0:T(2,128)(2,1)}), bf16[64,2,4096]{2,1,0:T(2,128)(2,1)S(1)}, u32[]{:S(2)}, u32[]{:S(2)}) async-start(bf16[64,2,4096]{2,1,0:T(2,128)(2,1)} %reshape.163), calls=%async_computation.2 | async-start | bytes 2097152 | tf_op jit(solution)/shard_map/all_to_all | solution.py:81
  171.8 0.7 all-gather.2.cloned.1.call-update
  172.5 2.4 copy.40
  175.1 4.1 %fusion.2 = f32[32,128,128]{1,2,0:T(8,128)} fusion(bf16[128,32,128]{0,2,1:T(8,128)(2,1)S(1)} %bitcast.77, f32[32,128]{1,0:T(8,128)S(1)} %reduce_window_sum.11, pred[128,128]{1,0:T(8,128)(4,1)S(1)} %fusion.22, bf16[128,32,128]{2,1,0:T(8,128)(2,1)S(1)} %bitcast.79, bf16[128,32,128]{2,1,0:T(8,128)(2,1)} %bitcast.80), kind=kOutput, calls=%fused_computation.12 | convolution fusion | flops 271056896 | bytes 5275648 | tf_op jit(solution)/shard_map/hts,shd->thd/dot_general | solution.py:26
  179.2 20.5 %all-to-all-done.2 = bf16[64,2,4096]{2,1,0:T(2,128)(2,1)S(1)} async-done(((bf16[64,2,4096]{2,1,0:T(2,128)(2,1)}), bf16[64,2,4096]{2,1,0:T(2,128)(2,1)S(1)}, u32[]{:S(2)}, u32[]{:S(2)}) %all-to-all-start.2) | async-done | bytes 1048608 | tf_op jit(solution)/shard_map/all_to_all | solution.py:81
  199.7 1.0 reshape.164
  200.8 6.5 %reduce.5 = bf16[64,8192]{1,0:T(8,128)(2,1)S(1)} reduce(bf16[64,1,8192]{2,1,0:T(2,128)(2,1)S(1)} %reshape.164, bf16[]{:T(256)} %constant.140), dimensions={1}, to_apply=%all_to_all.22.reduce_sub_computation | reduce | bytes 2097154 | tf_op jit(solution)/shard_map/all_to_all | solution.py:81
  207.3 1.3 all_to_all.23
  208.6 3.2 %multiply_reduce_fusion = (f32[128,32]{0,1:T(8,128)S(1)}, f32[128,32,128]{0,2,1:T(8,128)S(1)}) fusion(f32[128,32]{0,1:T(8,128)S(1)} %copy-done.12, bf16[32,128,128]{2,1,0:T(8,128)(2,1)} %all_to_all.23, bf16[128,32,128]{2,1,0:T(8,128)(2,1)} %bitcast.81, f32[32,128,128]{1,2,0:T(8,128)} %fusion.2), kind=kOutput, calls=%fused_computation.8 | convolution fusion | flops 136310784 | bytes 6324224 | tf_op jit(solution)/shard_map/thi,hij->thj/dot_general | solution.py:100
  211.8 1.7 multiply_multiply_fusion
  213.5 1.9 copy.33
  215.5 2.5 fusion
  218.0 3.4 %collective-permute-start = (bf16[128,4096]{1,0:T(8,128)(2,1)}, bf16[128,4096]{1,0:T(8,128)(2,1)}, u32[]{:S(2)}, u32[]{:S(2)}) collective-permute-start(bf16[128,4096]{1,0:T(8,128)(2,1)} %fusion), channel_id=1, source_target_pairs={{0,64},{64,128},{128,192},{1,65},{65,129},{129,193},{2,66},{66,130... | collective-permute-start | bytes 3145736 | tf_op jit(solution)/shard_map/ppermute | solution.py:12
  221.4 24.1 %collective-permute-done = bf16[128,4096]{1,0:T(8,128)(2,1)} collective-permute-done((bf16[128,4096]{1,0:T(8,128)(2,1)}, bf16[128,4096]{1,0:T(8,128)(2,1)}, u32[]{:S(2)}, u32[]{:S(2)}) %collective-permute-start) | collective-permute-done | bytes 1048608 | tf_op jit(solution)/shard_map/ppermute | solution.py:12
  245.5 2.6 fusion.4
  248.1 3.4 %collective-permute-start.1 = (bf16[128,4096]{1,0:T(8,128)(2,1)}, bf16[128,4096]{1,0:T(8,128)(2,1)}, u32[]{:S(2)}, u32[]{:S(2)}) collective-permute-start(bf16[128,4096]{1,0:T(8,128)(2,1)} %fusion.4), channel_id=1, source_target_pairs={{0,64},{64,128},{128,192},{1,65},{65,129},{129,193},{2,66},{66,130... | collective-permute-start | bytes 3145736 | tf_op jit(solution)/shard_map/ppermute | solution.py:12
  251.5 23.3 %collective-permute-done.1 = bf16[128,4096]{1,0:T(8,128)(2,1)} collective-permute-done((bf16[128,4096]{1,0:T(8,128)(2,1)}, bf16[128,4096]{1,0:T(8,128)(2,1)}, u32[]{:S(2)}, u32[]{:S(2)}) %collective-permute-start.1) | collective-permute-done | bytes 1048608 | tf_op jit(solution)/shard_map/ppermute | solution.py:12
  274.8 3.1 fusion.5
  277.9 3.4 %collective-permute-start.2 = (bf16[128,4096]{1,0:T(8,128)(2,1)}, bf16[128,4096]{1,0:T(8,128)(2,1)S(1)}, u32[]{:S(2)}, u32[]{:S(2)}) collective-permute-start(bf16[128,4096]{1,0:T(8,128)(2,1)} %fusion.5), channel_id=1, source_target_pairs={{0,64},{64,128},{128,192},{1,65},{65,129},{129,193},{2,66},{66,130... | collective-permute-start | bytes 3145736 | tf_op jit(solution)/shard_map/ppermute | solution.py:12
  281.3 22.3 %collective-permute-done.2 = bf16[128,4096]{1,0:T(8,128)(2,1)S(1)} collective-permute-done((bf16[128,4096]{1,0:T(8,128)(2,1)}, bf16[128,4096]{1,0:T(8,128)(2,1)S(1)}, u32[]{:S(2)}, u32[]{:S(2)}) %collective-permute-start.2) | collective-permute-done | bytes 1048608 | tf_op jit(solution)/shard_map/ppermute | solution.py:12
  303.6 2.6 fusion.7
  (138 shorter events, 14.8 us)
Async XLA Ops:
  6.5 21.8 %copy-start.10 = (bf16[1,1,128,4096]{3,2,1,0:T(8,128)(2,1)S(1)}, bf16[1,1,128,4096]{3,2,1,0:T(8,128)(2,1)}, u32[]{:S(2)}) copy-start(bf16[1,1,128,4096]{3,2,1,0:T(8,128)(2,1)} %param.10) | copy-start | bytes 3145732
  12.3 20.3 %all-to-all-start.1 = ((f32[64,1,34]{2,1,0:T(1,128)}), f32[64,1,34]{2,1,0:T(1,128)S(1)}, u32[]{:S(2)}, u32[]{:S(2)}) async-start(f32[64,1,34]{2,1,0:T(1,128)} %broadcast_in_dim.9), calls=%async_computation.1 | async-start | bytes 65536 | tf_op jit(solution)/shard_map/all_to_all | solution.py:64
  28.3 3.1 copy-start.6
  28.6 2.8 copy-start.8
  32.7 59.6 %all-to-all-start = ((f32[64,1,8192]{2,1,0:T(1,128)}), f32[64,1,8192]{2,1,0:T(1,128)S(1)}, u32[]{:S(2)}, u32[]{:S(2)}) async-start(f32[64,1,8192]{2,1,0:T(1,128)} %bitcast.74), calls=%async_computation | async-start | bytes 4194304 | tf_op jit(solution)/shard_map/all_to_all | solution.py:63
  93.6 1.0 copy-start.2
  98.0 3.2 %copy-start.11 = (f32[1,1,8192]{2,1,0:T(1,128)S(1)}, f32[1,1,8192]{2,1,0:T(1,128)}, u32[]{:S(2)}) copy-start(f32[1,1,8192]{2,1,0:T(1,128)} %slice.408) | copy-start | bytes 98308
  102.0 0.8 copy-start.3
  102.0 9.7 %copy-start.15 = (f32[15]{0:T(128)S(1)}, f32[15]{0:T(128)}, u32[]{:S(2)}) copy-start(f32[15]{0:T(128)} %get-tuple-element.26) | copy-start | bytes 184
  102.8 0.8 copy-start.4
  105.0 8.9 %slice-start = ((f32[32,1,8192]{2,1,0:T(1,128)}), f32[1,1,8192]{2,1,0:T(1,128)S(1)}, s32[]{:S(2)}) async-start(f32[32,1,8192]{2,1,0:T(1,128)} %copy-done.2), calls=%async_computation.4 | async-start | bytes 65536 | tf_op jit(solution)/shard_map/slice | solution.py:73
  115.2 13.0 %copy-start.16 = (f32[31]{0:T(128)S(1)}, f32[31]{0:T(128)}, u32[]{:S(2)}) copy-start(f32[31]{0:T(128)} %get-tuple-element.24) | copy-start | bytes 376
  124.8 3.4 %copy-start.1 = (f32[32,1,8192]{2,1,0:T(1,128)S(1)}, f32[32,1,8192]{2,1,0:T(1,128)}, u32[]{:S(2)}) copy-start(f32[32,1,8192]{2,1,0:T(1,128)} %pad.93) | copy-start | bytes 3145732
  130.7 13.2 %copy-start.5 = (f32[32,1,8192]{2,1,0:T(1,128)S(1)}, f32[32,1,8192]{2,1,0:T(1,128)}, u32[]{:S(2)}) copy-start(f32[32,1,8192]{2,1,0:T(1,128)} %add.169) | copy-start | bytes 3145732
  146.6 5.8 %copy-start.17 = (f32[64]{0:T(128)S(1)}, f32[64]{0:T(128)}, u32[]{:S(2)}) copy-start(f32[64]{0:T(128)} %compare_convert_fusion.1) | copy-start | bytes 772
  165.3 9.6 %copy-start.13 = (bf16[1,4096]{1,0:T(2,128)(2,1)S(1)}, bf16[1,4096]{1,0:T(2,128)(2,1)}, u32[]{:S(2)}) copy-start(bf16[1,4096]{1,0:T(2,128)(2,1)} %param.11) | copy-start | bytes 24580
  165.3 9.6 %copy-start.14 = (s32[1,128]{1,0:T(1,128)S(1)}, s32[1,128]{1,0:T(1,128)}, u32[]{:S(2)}) copy-start(s32[1,128]{1,0:T(1,128)} %param.13) | copy-start | bytes 1540
  165.3 9.7 %copy-start.7 = (bf16[1,1,128,4096]{2,3,1,0:T(8,128)(2,1)S(1)}, bf16[1,1,128,4096]{2,3,1,0:T(8,128)(2,1)}, u32[]{:S(2)}) copy-start(bf16[1,1,128,4096]{2,3,1,0:T(8,128)(2,1)} %copy-done.6) | copy-start | bytes 3145732
  165.3 9.7 %copy-start.9 = (bf16[16,8,32,128]{3,2,1,0:T(8,128)(2,1)S(1)}, bf16[16,8,32,128]{3,2,1,0:T(8,128)(2,1)}, u32[]{:S(2)}) copy-start(bf16[16,8,32,128]{3,2,1,0:T(8,128)(2,1)} %copy-done.8) | copy-start | bytes 3145732
  165.3 34.4 %all-to-all-start.2 = ((bf16[64,2,4096]{2,1,0:T(2,128)(2,1)}), bf16[64,2,4096]{2,1,0:T(2,128)(2,1)S(1)}, u32[]{:S(2)}, u32[]{:S(2)}) async-start(bf16[64,2,4096]{2,1,0:T(2,128)(2,1)} %reshape.163), calls=%async_computation.2 | async-start | bytes 2097152 | tf_op jit(solution)/shard_map/all_to_all | solution.py:81
  171.8 43.7 %all-gather.2.cloned.1.call-start = ((), (), s32[]{:S(2)}) async-start(), calls=%async_computation.3 | async-start | bytes 1310720 | tf_op jit(solution)/shard_map/all_gather | solution.py:118
  200.7 7.8 %copy-start.12 = (f32[128,32]{0,1:T(8,128)S(1)}, f32[128,32]{0,1:T(8,128)}, u32[]{:S(2)}) copy-start(f32[128,32]{0,1:T(8,128)} %get-tuple-element.11) | copy-start | bytes 49156
  215.5 30.0 %copy-start = (bf16[1,128,4096]{2,1,0:T(8,128)(2,1)S(1)}, bf16[1,128,4096]{2,1,0:T(8,128)(2,1)}, u32[]{:S(2)}) copy-start(bf16[1,128,4096]{2,1,0:T(8,128)(2,1)} %all-gather.2.cloned.1.call-done) | copy-start | bytes 3145732
  218.0 27.5 %collective-permute-start = (bf16[128,4096]{1,0:T(8,128)(2,1)}, bf16[128,4096]{1,0:T(8,128)(2,1)}, u32[]{:S(2)}, u32[]{:S(2)}) collective-permute-start(bf16[128,4096]{1,0:T(8,128)(2,1)} %fusion), channel_id=1, source_target_pairs={{0,64},{64,128},{128,192},{1,65},{65,129},{129,193},{2,66},{66,130... | collective-permute-start | bytes 3145736 | tf_op jit(solution)/shard_map/ppermute | solution.py:12
  248.1 26.7 %collective-permute-start.1 = (bf16[128,4096]{1,0:T(8,128)(2,1)}, bf16[128,4096]{1,0:T(8,128)(2,1)}, u32[]{:S(2)}, u32[]{:S(2)}) collective-permute-start(bf16[128,4096]{1,0:T(8,128)(2,1)} %fusion.4), channel_id=1, source_target_pairs={{0,64},{64,128},{128,192},{1,65},{65,129},{129,193},{2,66},{66,130... | collective-permute-start | bytes 3145736 | tf_op jit(solution)/shard_map/ppermute | solution.py:12
  277.9 25.7 %collective-permute-start.2 = (bf16[128,4096]{1,0:T(8,128)(2,1)}, bf16[128,4096]{1,0:T(8,128)(2,1)S(1)}, u32[]{:S(2)}, u32[]{:S(2)}) collective-permute-start(bf16[128,4096]{1,0:T(8,128)(2,1)} %fusion.5), channel_id=1, source_target_pairs={{0,64},{64,128},{128,192},{1,65},{65,129},{129,193},{2,66},{66,130... | collective-permute-start | bytes 3145736 | tf_op jit(solution)/shard_map/ppermute | solution.py:12
Sparse Core Ops, SparseCore 0:
  174.4 26.3 all-gather.1
where the time goes:
time: 319 us; the launch traced here: 313 us
  waiting for transfers between devices  119 us (37%)
  other arithmetic  62.7 us (20%)
  local copies, waits for them, and re-layouts  59.4 us (19%)
  starting transfers between devices  37.7 us (12%)
  between operations  25.1 us (8%)
  matrix products  9.4 us (3%)
    ppermute x3, waiting for transfers between devices, shifted(): return lax.ppermute(array, axis, pairs)  69.7 us
    all_to_all x1, waiting for transfers between devices, incoming_state(): lax.all_to_all(flat, 'ctx', split_axis=0, concat_axis=0, tiled=True)  26.6 us
    all_to_all x1, waiting for transfers between devices, incoming_state(): lax.all_to_all(sending.astype(jnp.bfloat16), 'ctx', split_axis=0, concat_...  20.5 us
    pad x18, local copies, waits for them, and re-layouts, incoming_state(): lax.associative_scan(link, (firsts, lasts, factors_in, pieces), axis=0)  19.2 us
    slice x1, local copies, waits for them, and re-layouts, incoming_state(): inclusive[3][:-1]  12.3 us
    all_to_all x1, starting transfers between devices, incoming_state(): lax.all_to_all(tiled, 'ctx', split_axis=0, concat_axis=0, tiled=True)  11.8 us
    add x12, other arithmetic, incoming_state(): lax.associative_scan(link, (firsts, lasts, factors_in, pieces), axis=0)  11.7 us
    convert_element_type x2, other arithmetic, incoming_state(): sending.astype(jnp.bfloat16)  10.7 us
  transfers between devices with their start and end apart: 7, of which 6 were waited for; matrix products, arithmetic and copies ran while one was open for 14% of the time, Pallas kernels for 0%

commit v1 on v0

v1 whole, which is shorter than its diff:
```python
import functools

import jax
import jax.numpy as jnp
from jax import lax
from jax.experimental import pallas as pl
from jax.experimental.pallas import tpu as pltpu
from jax.sharding import Mesh
from jax.sharding import PartitionSpec as P

EPSILON = 1e-05
F32, BF16 = jnp.float32, jnp.bfloat16
D = 128
HEADS = 32
HALF = HEADS // 2
GROUP = HALF // 4
NZ = 8
META = 32
ROWS = GROUP * D
PART = ROWS + META
HIGHEST = lax.Precision.HIGHEST
VMEM_LIMIT = 40 * 1024 * 1024


def nt(a, b, precision=None):
    return lax.dot_general(a, b, (((1,), (1,)), ((), ())), precision=precision, preferred_element_type=F32)


def tn(a, b):
    return lax.dot_general(a, b, (((0,), (0,)), ((), ())), preferred_element_type=F32)


def iota(shape, axis):
    return lax.broadcasted_iota(jnp.int32, shape, axis)


def lower():
    return (iota((D, D), 1) <= iota((D, D), 0)).astype(F32)


def rows_of(ids_row):
    return jnp.transpose(jnp.broadcast_to(ids_row, (D, D)))


def split3(x):
    hi = x.astype(BF16).astype(F32)
    mid = (x - hi).astype(BF16).astype(F32)
    return hi, mid, x - hi - mid


def pack_meta(decay, first, last):
    row = iota((8, D), 0)
    ids = jnp.where(row == 0, first, jnp.where(row == 1, last, 0.0))
    return jnp.concatenate([*split3(decay), ids], axis=0).astype(BF16)


def unpack_meta(meta):
    meta = meta.astype(F32)
    return meta[0:8] + meta[8:16] + meta[16:24], meta[24:25], meta[25:26]


def same(a, b):
    return (a == b).astype(F32)


def summary_kernel(index, k_ref, v_ref, decay_ref, ids_ref, out_ref, cut_ref):
    half = index[0]
    ids = ids_ref[...].astype(F32)
    first, last = ids[:, 0:1], ids[:, D - 1 : D]
    decay = decay_ref[pl.ds(pl.multiple_of(half * HALF, HALF), HALF), :]
    sums = nt(lower(), decay, HIGHEST)
    column = same(rows_of(ids)[:, 0:HALF], last)
    carried = jnp.exp(sums[D - 1 : D, :] - sums) * column
    total = lax.dot_general(
        decay, jnp.ones((D, D), F32), (((1,), (0,)), ((), ())), precision=HIGHEST, preferred_element_type=F32
    )
    for group in range(4):
        for i in range(GROUP):
            h = group * GROUP + i
            lanes = slice(h * D, (h + 1) * D)
            keyed = (k_ref[:, lanes].astype(F32) * carried[:, h : h + 1]).astype(BF16)
            out_ref[group, i * D : (i + 1) * D, :] = tn(keyed, v_ref[:, lanes]).astype(BF16)
        cut_ref[0:GROUP, :] = total[group * GROUP : (group + 1) * GROUP, :]
        cut_ref[GROUP:8, :] = jnp.zeros((8 - GROUP, D), F32)
        out_ref[group, ROWS:PART, :] = pack_meta(
            cut_ref[...], jnp.broadcast_to(first, (1, D)), jnp.broadcast_to(last, (1, D))
        )


def summaries(half, keys, values, decay, ids):
    whole = lambda shape: pl.BlockSpec(shape, lambda i, s: (0,) * len(shape))
    return pl.pallas_call(
        summary_kernel,
        out_shape=jax.ShapeDtypeStruct((4, PART, D), BF16),
        grid_spec=pltpu.PrefetchScalarGridSpec(
            num_scalar_prefetch=1,
            grid=(1,),
            in_specs=[
                pl.BlockSpec((D, HALF * D), lambda i, s: (0, s[0])),
                pl.BlockSpec((D, HALF * D), lambda i, s: (0, s[0])),
                whole((HEADS, D)),
                whole((1, D)),
            ],
            out_specs=whole((4, PART, D)),
            scratch_shapes=[pltpu.VMEM((8, D), F32)],
        ),
        compiler_params=pltpu.CompilerParams(vmem_limit_bytes=VMEM_LIMIT),
        cost_estimate=pl.CostEstimate(flops=2 * HALF * D**3, bytes_accessed=3 * HALF * D * D * 2, transcendentals=0),
    )(half, keys, values, decay, ids)


def intra_kernel(q_ref, k_ref, v_ref, decay_ref, ids_ref, out_ref):
    ids = ids_ref[...].astype(F32)
    heads = q_ref.shape[1] // D
    decay = decay_ref[...]
    sums_column = nt(lower(), decay, HIGHEST)
    sums_row = nt(decay, lower(), HIGHEST)
    allowed = (iota((D, D), 1) <= iota((D, D), 0)) & (rows_of(ids) == ids)
    for h in range(heads):
        lanes = slice(h * D, (h + 1) * D)
        spread = jnp.minimum(sums_column[:, h : h + 1] - sums_row[h : h + 1, :], 0.0)
        weighting = jnp.where(allowed, jnp.exp(spread), 0.0)
        attn = (nt(q_ref[:, lanes], k_ref[:, lanes]) * weighting).astype(BF16)
        out_ref[:, lanes] = jnp.dot(attn, v_ref[:, lanes], preferred_element_type=F32)


def intra_term(queries, keys, values, decay, ids):
    step = 8
    block = pl.BlockSpec((D, step * D), lambda i: (0, i))
    return pl.pallas_call(
        intra_kernel,
        out_shape=jax.ShapeDtypeStruct((D, HEADS * D), F32),
        grid=(HEADS // step,),
        in_specs=[block, block, block, pl.BlockSpec((step, D), lambda i: (i, 0)), pl.BlockSpec((1, D), lambda i: (0, 0))],
        out_specs=block,
        compiler_params=pltpu.CompilerParams(vmem_limit_bytes=VMEM_LIMIT),
        cost_estimate=pl.CostEstimate(
            flops=4 * HEADS * D**3, bytes_accessed=5 * HEADS * D * D * 2, transcendentals=HEADS * D * D
        ),
    )(queries, keys, values, decay, ids)


def chip_kernel(index, own_ref, other_ref, *out_refs):
    y, core = index[0], index[1]
    is_one = core == 1
    for step in range(4):
        group = lax.rem(y + step, 4)
        decay_own, first_own, last_own = unpack_meta(own_ref[group, ROWS:PART, :])
        decay_other, first_other, last_other = unpack_meta(other_ref[group, ROWS:PART, :])
        joined = same(last_own, last_other)
        later = jnp.where(is_one, decay_own, decay_other)
        passed = jnp.exp(later) * joined
        weight_own = jnp.where(is_one, 1.0, passed)
        weight_other = jnp.where(is_one, passed, 1.0)
        for i in range(GROUP):
            rows = slice(i * D, (i + 1) * D)
            out_refs[step][rows, :] = (
                weight_own[i : i + 1] * own_ref[group, rows, :].astype(F32)
                + weight_other[i : i + 1] * other_ref[group, rows, :].astype(F32)
            ).astype(BF16)
        out_refs[step][ROWS:PART, :] = pack_meta(
            decay_own + decay_other,
            jnp.where(is_one, first_other, first_own),
            jnp.where(is_one, last_own, last_other),
        )


def small_call(kernel, index, operands, outs, scratch=()):
    whole = lambda shape: pl.BlockSpec(shape, lambda i, s: (0,) * len(shape))
    size = sum(a.size * a.dtype.itemsize for a in operands)
    return pl.pallas_call(
        kernel,
        out_shape=[jax.ShapeDtypeStruct(shape, dtype) for shape, dtype in outs],
        grid_spec=pltpu.PrefetchScalarGridSpec(
            num_scalar_prefetch=1,
            grid=(1,),
            in_specs=[whole(a.shape) for a in operands],
            out_specs=[whole(shape) for shape, _ in outs],
            scratch_shapes=list(scratch),
        ),
        compiler_params=pltpu.CompilerParams(vmem_limit_bytes=VMEM_LIMIT),
        cost_estimate=pl.CostEstimate(flops=size, bytes_accessed=2 * size, transcendentals=0),
    )(index, *operands)


def in_order(y, slots, ordered_ref):
    for step in range(4):
        ordered_ref[lax.rem(y + 4 - step, 4)] = slots[step][...]


def row_kernel(index, *refs):
    *slots, out_ref, ordered_ref = refs
    in_order(index[0], slots, ordered_ref)
    metas = [unpack_meta(ordered_ref[c, ROWS:PART, :]) for c in range(4)]
    weights, after = [None] * 4, jnp.zeros((8, D), F32)
    for c in (3, 2, 1, 0):
        weights[c] = jnp.exp(after) * same(metas[c][2], metas[3][2])
        after = after + metas[c][0]
    row = iota((16, D), 0)
    for i in range(GROUP):
        rows = slice(i * D, (i + 1) * D)
        state = sum(weights[c][i : i + 1] * ordered_ref[c, rows, :].astype(F32) for c in range(4)).astype(BF16)
        out_ref[2 * i, 0 : D // 2, :] = state[0 : D // 2]
        out_ref[2 * i + 1, 0 : D // 2, :] = state[D // 2 :]
        hi, mid, low = split3(after[i : i + 1])
        meta = jnp.zeros((16, D), F32)
        for at, value in enumerate((hi, mid, low, metas[0][1], metas[3][2])):
            meta = jnp.where(row == at, value, meta)
        out_ref[2 * i, D // 2 :, :] = meta.astype(BF16)
        out_ref[2 * i + 1, D // 2 :, :] = meta.astype(BF16)


def scan_kernel(index, in_ref, out_ref):
    del index
    state = jnp.zeros((D // 2, D), F32)
    before = jnp.full((1, D), -1.0, F32)
    for z in range(NZ):
        meta = in_ref[z, D // 2 :, :].astype(F32)
        decay, first, last = meta[0:1] + meta[1:2] + meta[2:3], meta[3:4], meta[4:5]
        state = state * same(before, first)
        out_ref[z] = state.astype(BF16)
        state = jnp.exp(decay) * same(first, last) * state + in_ref[z, 0 : D // 2, :].astype(F32)
        before = last


def spread_kernel(index, state_ref, *refs):
    *slots, out0, out1, out2, out3, ordered_ref, result_ref = refs
    y = index[0]
    in_order(y, slots, ordered_ref)
    metas = [unpack_meta(ordered_ref[c, ROWS:PART, :]) for c in range(4)]
    passing = [jnp.exp(decay) * same(first, last) for decay, first, last in metas]
    joined = [None] + [same(metas[c - 1][2], metas[c][1]) for c in (1, 2, 3)]
    for i in range(GROUP):
        rows = slice(i * D, (i + 1) * D)
        state = state_ref[rows, :].astype(F32)
        result_ref[0, rows, :] = state.astype(BF16)
        for c in (1, 2, 3):
            state = passing[c - 1][i : i + 1] * state + ordered_ref[c - 1, rows, :].astype(F32)
            state = state * joined[c]
            result_ref[c, rows, :] = state.astype(BF16)
    for step, out_ref in enumerate((out0, out1, out2, out3)):
        out_ref[...] = result_ref[lax.rem(y + step, 4)]


def core_kernel(index, own_ref, other_ref, s0, s1, s2, s3, mine_ref, send_ref):
    y, core = index[0], index[1]
    is_one = core == 1
    for step, slot in enumerate((s0, s1, s2, s3)):
        group = lax.rem(y + 4 - step, 4)
        decay_own, first_own, last_own = unpack_meta(own_ref[group, ROWS:PART, :])
        decay_other, first_other, last_other = unpack_meta(other_ref[group, ROWS:PART, :])
        decay = jnp.where(is_one, decay_other, decay_own)
        first0 = jnp.where(is_one, first_other, first_own)
        last0 = jnp.where(is_one, last_other, last_own)
        first1 = jnp.where(is_one, first_own, first_other)
        joined = same(last0, first1)
        passing = jnp.exp(decay) * same(first0, last0) * joined
        for i in range(GROUP):
            rows = slice(i * D, (i + 1) * D)
            chip = slot[rows, :]
            earlier = jnp.where(is_one, other_ref[group, rows, :].astype(F32), own_ref[group, rows, :].astype(F32))
            later = (passing[i : i + 1] * chip.astype(F32) + joined * earlier).astype(BF16)
            mine_ref[group, rows, :] = jnp.where(is_one, later.astype(F32), chip.astype(F32)).astype(BF16)
            send_ref[group, rows, :] = jnp.where(is_one, chip.astype(F32), later.astype(F32)).astype(BF16)


def attend_kernel(index, q_ref, intra_ref, mine_ref, other_ref, decay_ref, ids_ref, gain_ref, *out_refs):
    step = pl.program_id(0)
    quarter = lax.rem(index[0] + step, 4)
    use_mine = (quarter // 2) == index[1]
    ids = ids_ref[...].astype(F32)
    decay = decay_ref[...]
    sums = nt(lower(), decay, HIGHEST)
    scaling = jnp.exp(sums) * same(rows_of(ids)[:, 0:8], ids[:, 0:1])
    for i in range(8):
        lanes = slice(i * D, (i + 1) * D)
        rows = slice((i % GROUP) * D, (i % GROUP + 1) * D)
        mine, other = mine_ref[i // GROUP, rows, :], other_ref[i // GROUP, rows, :]
        state = jnp.where(use_mine, mine.astype(F32), other.astype(F32)).astype(BF16)
        inter = jnp.dot(q_ref[:, lanes], state, preferred_element_type=F32)
        total = intra_ref[:, lanes] + inter * scaling[:, i : i + 1]
        power = jnp.sum(total * total, axis=1, keepdims=True) * (1.0 / D)
        normed = (total * lax.rsqrt(power + EPSILON) * gain_ref[:, lanes].astype(F32)).astype(BF16)
        for at, out_ref in enumerate(out_refs):

            @pl.when(step == at)
            def _(out_ref=out_ref, normed=normed, lanes=lanes):
                out_ref[:, lanes] = normed


def attend(index, queries, intra, mine, other, decay, ids, gain):
    quarter = lambda i, s: lax.rem(s[0] + i, 4)
    block = pl.BlockSpec((D, 8 * D), lambda i, s: (0, quarter(i, s)))
    states = pl.BlockSpec((2, ROWS, D), lambda i, s: (lax.rem(quarter(i, s), 2), 0, 0))
    return pl.pallas_call(
        attend_kernel,
        out_shape=[jax.ShapeDtypeStruct((D, 8 * D), BF16)] * 4,
        grid_spec=pltpu.PrefetchScalarGridSpec(
            num_scalar_prefetch=1,
            grid=(4,),
            in_specs=[
                block,
                block,
                states,
                states,
                pl.BlockSpec((8, D), lambda i, s: (quarter(i, s), 0)),
                pl.BlockSpec((1, D), lambda i, s: (0, 0)),
                pl.BlockSpec((1, 8 * D), lambda i, s: (0, quarter(i, s))),
            ],
            out_specs=[pl.BlockSpec((D, 8 * D), lambda i, s: (0, 0))] * 4,
        ),
        compiler_params=pltpu.CompilerParams(vmem_limit_bytes=VMEM_LIMIT),
        cost_estimate=pl.CostEstimate(
            flops=2 * HEADS * D**3, bytes_accessed=7 * HEADS * D * D * 2, transcendentals=HEADS * D
        ),
    )(index, queries, intra, mine, other, decay, ids, gain)


def layers_kernel(index, tokens_ref, *refs):
    *slots, out0, out1, out2, out3, ordered_ref = refs
    phase = index[0]
    in_order(phase, slots, ordered_ref)
    current = tokens_ref[...].astype(F32)
    for s in range(4):
        rounded = (current + ordered_ref[s].astype(F32)).astype(BF16)
        ordered_ref[s] = rounded
        current = rounded.astype(F32)
    for step, out_ref in enumerate((out0, out1, out2, out3)):
        out_ref[...] = ordered_ref[lax.rem(phase + step, 4)]


def place_kernel(index, *refs):
    *slots, out_ref = refs
    quarter = pl.program_id(0)
    source = lax.rem(index[0] + 4 - quarter, 4)
    for step, slot in enumerate(slots):

        @pl.when(source == step)
        def _(slot=slot):
            out_ref[...] = slot[...]


def place(index, slots):
    return pl.pallas_call(
        place_kernel,
        out_shape=jax.ShapeDtypeStruct((D, HEADS * D), BF16),
        grid_spec=pltpu.PrefetchScalarGridSpec(
            num_scalar_prefetch=1,
            grid=(4,),
            in_specs=[pl.BlockSpec((D, 8 * D), lambda i, s: (0, 0))] * 4,
            out_specs=pl.BlockSpec((D, 8 * D), lambda i, s: (0, i)),
        ),
        compiler_params=pltpu.CompilerParams(vmem_limit_bytes=VMEM_LIMIT),
        cost_estimate=pl.CostEstimate(flops=0, bytes_accessed=4 * HEADS * D * D, transcendentals=0),
    )(index, *slots)


def ring_exchange(slots, axis):
    size = lax.axis_size(axis)
    moved = [
        lax.ppermute(slots[d], axis, [(i, (i + d) % size) for i in range(size)]) for d in range(1, len(slots))
    ]
    return [slots[0], *moved]


def swap_cores(array):
    return lax.ppermute(array, "core", [(0, 1), (1, 0)])


def local(tokens, queries, keys_in, values, norm_gain, log_decay, doc_ids):
    phase, y, core = (lax.axis_index(name) for name in ("phase", "y", "core"))
    queries, keys, values, decay = queries[0, 0], keys_in[0, 0], values[0, 0], log_decay[0, 0]
    here = jnp.stack([y, core]).astype(jnp.int32)

    sending = summaries(jnp.stack([1 - core]), keys, values, decay, doc_ids)
    other = swap_cores(sending)
    own = summaries(jnp.stack([core]), keys, values, decay, doc_ids)

    group_out = ((PART, D), BF16)
    slots = ring_exchange(small_call(chip_kernel, here, [own, other], [group_out] * 4), "y")
    intra = intra_term(queries, keys, values, decay, doc_ids)

    (pieces,) = small_call(
        row_kernel, here, slots, [((NZ, D // 2 + 16, D), BF16)], [pltpu.VMEM((4, PART, D), BF16)]
    )
    pieces = lax.all_to_all(pieces, "z", split_axis=0, concat_axis=0, tiled=True)
    (states,) = small_call(scan_kernel, here, [pieces], [((NZ, D // 2, D), BF16)])
    states = lax.all_to_all(states, "z", split_axis=0, concat_axis=0, tiled=True)

    spread = small_call(
        spread_kernel,
        here,
        [states.reshape(ROWS, D), *slots],
        [((ROWS, D), BF16)] * 4,
        [pltpu.VMEM((4, PART, D), BF16), pltpu.VMEM((4, ROWS, D), BF16)],
    )
    spread = ring_exchange(spread, "y")
    mine, send = small_call(core_kernel, here, [own, other, *spread], [((4, ROWS, D), BF16)] * 2)
    theirs = swap_cores(send)

    at = jnp.stack([phase, core]).astype(jnp.int32)
    normed = ring_exchange(attend(at, queries, intra, mine, theirs, decay, doc_ids, norm_gain), "phase")
    quarter_out = ((D, 8 * D), BF16)
    sums = small_call(
        layers_kernel, at, [tokens[0], *normed], [quarter_out] * 4, [pltpu.VMEM((4, D, 8 * D), BF16)]
    )
    return place(at, ring_exchange(sums, "phase"))[None, None]


def solution(mesh):
    grid = Mesh(mesh.devices.reshape(4, NZ, 4, 2), ("phase", "z", "y", "core"))
    ctx = ("z", "y", "core")
    rows = P("phase", None, ctx, None)
    return jax.shard_map(
        local,
        mesh=grid,
        in_specs=(
            P(None, ctx, "phase"),
            rows,
            rows,
            rows,
            P("phase", None),
            P("phase", None, None, ctx),
            P(None, ctx),
        ),
        out_specs=rows,
        check_vma=False,
    )
```

time: 319 us -> 116 us (0.36)
  the two profiles are of different devices: /device:TPU:34 before, /device:TPU:8 now
where the time goes in v1:
time: 116 us; the launch traced here: 115 us
  waiting for transfers between devices  33 us (28%)
  blocking collectives  28.4 us (24%)
  Pallas kernels  27.1 us (23%)
  starting transfers between devices  20.6 us (18%)
  local copies, waits for them, and re-layouts  5.74 us (5%)
    ppermute x12, waiting for transfers between devices, ring_exchange(): lax.ppermute(slots[d], axis, [(i, (i + d) % size) for i in range(size)])  32.5 us
    ppermute x12, starting transfers between devices, ring_exchange(): lax.ppermute(slots[d], axis, [(i, (i + d) % size) for i in range(size)])  20.5 us
    all_to_all x1, blocking collectives, local(): lax.all_to_all(pieces, 'z', split_axis=0, concat_axis=0, tiled=True)  16.9 us
    all_to_all x1, blocking collectives, local(): lax.all_to_all(states, 'z', split_axis=0, concat_axis=0, tiled=True)  11.5 us
    pallas_call x1, Pallas kernels, attend(): pl.pallas_call(attend_kernel, out_shape=[jax.ShapeDtypeStruct((D, 8 * D),...  10.6 us
    pallas_call x1, Pallas kernels, intra_term(): pl.pallas_call(intra_kernel, out_shape=jax.ShapeDtypeStruct((D, HEADS * D...  6.52 us
    unnamed x30, local copies, waits for them, and re-layouts  5.74 us
    pallas_call x6, Pallas kernels, small_call(): pl.pallas_call(kernel, out_shape=[jax.ShapeDtypeStruct(shape, dtype) for...  5.68 us
  transfers between devices with their start and end apart: 14, of which 11 were waited for; matrix products, arithmetic and copies ran while one was open for 0% of the time, Pallas kernels for 7%

profile of v1, /device:TPU:8, one launch (start us, length us, event | category | flops | bytes accessed | tf_op | source)
XLA Modules:
  0.0 115.1 jit_solution(14977162542947459072)
XLA Ops:
  0.0 0.0 copy-start.14
  0.0 0.0 copy-start
  0.0 1.2 %copy-done = bf16[1,1,128,4096]{3,2,1,0:T(8,128)(2,1)S(1)} copy-done((bf16[1,1,128,4096]{3,2,1,0:T(8,128)(2,1)S(1)}, bf16[1,1,128,4096]{3,2,1,0:T(8,128)(2,1)}, u32[]{:S(2)}) %copy-start) | copy-done | bytes 1048600
  1.2 0.0 copy-start.2
  1.2 1.2 %copy-done.2 = bf16[1,1,128,4096]{3,2,1,0:T(8,128)(2,1)S(1)} copy-done((bf16[1,1,128,4096]{3,2,1,0:T(8,128)(2,1)S(1)}, bf16[1,1,128,4096]{3,2,1,0:T(8,128)(2,1)}, u32[]{:S(2)}) %copy-start.2) | copy-done | bytes 1048600
  2.5 0.0 copy-start.9
  2.5 0.7 copy-done.9
  3.2 0.7 copy-done.13
  3.8 1.1 shard_map.75
  5.0 0.1 collective-permute-start
  5.1 0.0 copy-done.14
  5.1 0.0 copy-done.1
  5.1 0.3 copy-done.3
  5.4 0.0 copy-done.10
  5.4 1.1 shard_map.74.own_ref
  6.5 0.1 pad_add_fusion.1.index
  6.6 0.4 collective-permute-done.other_ref
  7.0 0.8 shard_map.76
  7.8 0.0 copy-start.5
  7.8 0.8 copy-done.5
  8.6 1.6 %collective-permute-start.1 = (bf16[544,128]{1,0:T(8,128)(2,1)S(1)}, bf16[544,128]{1,0:T(8,128)(2,1)S(1)}, u32[]{:S(2)}, u32[]{:S(2)}) collective-permute-start(bf16[544,128]{1,0:T(8,128)(2,1)S(1)} %get-tuple-element.24), channel_id=1, source_target_pairs={{0,2},{2,4},{4,6},{6,0},{1,3},{3,5},{5,7},{7,1},{8,10},{10,12},{12... | collective-permute-start | bytes 417800 | tf_op jit(solution)/shard_map/ppermute | solution.py:361
  10.2 2.7 %collective-permute-start.2 = (bf16[544,128]{1,0:T(8,128)(2,1)S(1)}, bf16[544,128]{1,0:T(8,128)(2,1)S(1)}, u32[]{:S(2)}, u32[]{:S(2)}) collective-permute-start(bf16[544,128]{1,0:T(8,128)(2,1)S(1)} %get-tuple-element.25), channel_id=1, source_target_pairs={{0,4},{2,6},{4,0},{6,2},{1,5},{3,7},{5,1},{7,3},{8,12},{10,14},{12... | collective-permute-start | bytes 417800 | tf_op jit(solution)/shard_map/ppermute | solution.py:361
  12.9 0.7 collective-permute-start.3
  13.6 1.7 %collective-permute-done.1.refs_1_ = bf16[544,128]{1,0:T(8,128)(2,1)S(1)} collective-permute-done((bf16[544,128]{1,0:T(8,128)(2,1)S(1)}, bf16[544,128]{1,0:T(8,128)(2,1)S(1)}, u32[]{:S(2)}, u32[]{:S(2)}) %collective-permute-start.1) | collective-permute-done | bytes 139296 | tf_op jit(solution)/shard_map/ppermute | solution.py:361
  15.3 3.0 %collective-permute-done.2.refs_2_ = bf16[544,128]{1,0:T(8,128)(2,1)S(1)} collective-permute-done((bf16[544,128]{1,0:T(8,128)(2,1)S(1)}, bf16[544,128]{1,0:T(8,128)(2,1)S(1)}, u32[]{:S(2)}, u32[]{:S(2)}) %collective-permute-start.2) | collective-permute-done | bytes 139296 | tf_op jit(solution)/shard_map/ppermute | solution.py:361
  18.3 1.9 %collective-permute-done.3.refs_3_ = bf16[544,128]{1,0:T(8,128)(2,1)S(1)} collective-permute-done((bf16[544,128]{1,0:T(8,128)(2,1)S(1)}, bf16[544,128]{1,0:T(8,128)(2,1)S(1)}, u32[]{:S(2)}, u32[]{:S(2)}) %collective-permute-start.3) | collective-permute-done | bytes 139296 | tf_op jit(solution)/shard_map/ppermute | solution.py:361
  20.1 0.7 shard_map.77
  20.8 16.9 %all_to_all.10.in_ref = bf16[8,80,128]{2,1,0:T(8,128)(2,1)S(1)} all-to-all(bf16[8,80,128]{2,1,0:T(8,128)(2,1)S(1)} %shard_map.77), channel_id=1, replica_groups=mesh['phase'=4,'z'=8,'y'=4,'core'=2] {'z'}, dimensions={0} | all-to-all | bytes 327680 | tf_op jit(solution)/shard_map/all_to_all | solution.py:386
  37.7 0.6 shard_map.78
  38.3 11.5 %all_to_all.11 = bf16[8,64,128]{2,1,0:T(8,128)(2,1)S(1)} all-to-all(bf16[8,64,128]{2,1,0:T(8,128)(2,1)S(1)} %shard_map.78), channel_id=1, replica_groups=mesh['phase'=4,'z'=8,'y'=4,'core'=2] {'z'}, dimensions={0} | all-to-all | bytes 262144 | tf_op jit(solution)/shard_map/all_to_all | solution.py:388
  49.8 0.8 shard_map.79
  50.6 1.5 %collective-permute-start.4 = (bf16[512,128]{1,0:T(8,128)(2,1)S(1)}, bf16[512,128]{1,0:T(8,128)(2,1)S(1)}, u32[]{:S(2)}, u32[]{:S(2)}) collective-permute-start(bf16[512,128]{1,0:T(8,128)(2,1)S(1)} %get-tuple-element.28), channel_id=1, source_target_pairs={{0,2},{2,4},{4,6},{6,0},{1,3},{3,5},{5,7},{7,1},{8,10},{10,12},{12... | collective-permute-start | bytes 393224 | tf_op jit(solution)/shard_map/ppermute | solution.py:361
  52.0 1.6 %collective-permute-start.5 = (bf16[512,128]{1,0:T(8,128)(2,1)S(1)}, bf16[512,128]{1,0:T(8,128)(2,1)S(1)}, u32[]{:S(2)}, u32[]{:S(2)}) collective-permute-start(bf16[512,128]{1,0:T(8,128)(2,1)S(1)} %get-tuple-element.29), channel_id=1, source_target_pairs={{0,4},{2,6},{4,0},{6,2},{1,5},{3,7},{5,1},{7,3},{8,12},{10,14},{12... | collective-permute-start | bytes 393224 | tf_op jit(solution)/shard_map/ppermute | solution.py:361
  53.6 1.5 %collective-permute-start.6 = (bf16[512,128]{1,0:T(8,128)(2,1)S(1)}, bf16[512,128]{1,0:T(8,128)(2,1)S(1)}, u32[]{:S(2)}, u32[]{:S(2)}) collective-permute-start(bf16[512,128]{1,0:T(8,128)(2,1)S(1)} %get-tuple-element.30), channel_id=1, source_target_pairs={{0,6},{2,0},{4,2},{6,4},{1,7},{3,1},{5,3},{7,5},{8,14},{10,8},{12,... | collective-permute-start | bytes 393224 | tf_op jit(solution)/shard_map/ppermute | solution.py:361
  55.1 0.5 collective-permute-done.4.s1
  55.6 3.0 %collective-permute-done.5.s2 = bf16[512,128]{1,0:T(8,128)(2,1)S(1)} collective-permute-done((bf16[512,128]{1,0:T(8,128)(2,1)S(1)}, bf16[512,128]{1,0:T(8,128)(2,1)S(1)}, u32[]{:S(2)}, u32[]{:S(2)}) %collective-permute-start.5) | collective-permute-done | bytes 131104 | tf_op jit(solution)/shard_map/ppermute | solution.py:361
  58.6 1.3 %collective-permute-done.6.s3 = bf16[512,128]{1,0:T(8,128)(2,1)S(1)} collective-permute-done((bf16[512,128]{1,0:T(8,128)(2,1)S(1)}, bf16[512,128]{1,0:T(8,128)(2,1)S(1)}, u32[]{:S(2)}, u32[]{:S(2)}) %collective-permute-start.6) | collective-permute-done | bytes 131104 | tf_op jit(solution)/shard_map/ppermute | solution.py:361
  59.9 0.0 copy-done.6
  59.9 1.7 %shard_map.80 = (bf16[4,512,128]{2,1,0:T(8,128)(2,1)S(1)}, bf16[4,512,128]{2,1,0:T(8,128)(2,1)}) custom-call(s32[2]{0:T(128)S(1)} %pad_add_fusion.1.index, bf16[4,544,128]{2,1,0:T(8,128)(2,1)S(1)} %shard_map.74.own_ref, bf16[4,544,128]{2,1,0:T(8,128)(2,1)S(1)} %copy-done.6, bf16[512,128]{1,0:T(8,128)(2,1)S(1)} %get-tuple-element.27.s0, ...), custom_call_target="tpu_custom_call" | custom-call | flops 1638400 | bytes 3276800 | tf_op jit(solution)/shard_map/pallas_call | solution.py:171
  61.6 0.8 copy-done.7
  62.4 0.0 collective-permute-start.7
  62.4 0.0 copy-done.4
  62.4 6.5 %shard_map.73.intra_ref = f32[128,4096]{1,0:T(8,128)S(1)} custom-call(bf16[128,4096]{1,0:T(8,128)(2,1)S(1)} %bitcast.17, bf16[128,4096]{1,0:T(8,128)(2,1)S(1)} %bitcast.13, bf16[128,4096]{1,0:T(8,128)(2,1)S(1)} %bitcast.16, f32[32,128]{1,0:T(8,128)S(1)} %bitcast.22, s32[1,128]{1,0:T(1,128)S(1)} %copy-done.14), custom_call_target="tpu_custom_call" | custom-call | flops 268435456 | bytes 5242880 | tf_op jit(solution)/shard_map/pallas_call | solution.py:130
  69.0 0.1 pad_add_fusion.index
  69.0 0.0 collective-permute-done.7.other_ref
  69.0 0.0 copy-done.8
  69.0 0.0 copy-done.12
  69.0 0.0 copy-start.11
  69.1 10.6 %shard_map.81 = (bf16[128,1024]{1,0:T(8,128)(2,1)S(1)}, bf16[128,1024]{1,0:T(8,128)(2,1)S(1)}, bf16[128,1024]{1,0:T(8,128)(2,1)S(1)}, bf16[128,1024]{1,0:T(8,128)(2,1)S(1)}) custom-call(s32[2]{0:T(128)S(1)} %pad_add_fusion.index, bf16[128,4096]{1,0:T(8,128)(2,1)S(1)} %bitcast.18, f32[128,4096]{1,0:T(8,128)S(1)} %shard_map.73.intra_ref, ...), custom_call_target="tpu_custom_call" | custom-call | flops 134217728 | bytes 7340032 | tf_op jit(solution)/shard_map/pallas_call | solution.py:295
  79.6 1.6 %collective-permute-start.8 = (bf16[128,1024]{1,0:T(8,128)(2,1)S(1)}, bf16[128,1024]{1,0:T(8,128)(2,1)S(1)}, u32[]{:S(2)}, u32[]{:S(2)}) collective-permute-start(bf16[128,1024]{1,0:T(8,128)(2,1)S(1)} %get-tuple-element.34), channel_id=1, source_target_pairs={{0,64},{64,128},{128,192},{192,0},{1,65},{65,129},{129,193},{193,1... | collective-permute-start | bytes 786440 | tf_op jit(solution)/shard_map/ppermute | solution.py:361
  81.2 2.7 %collective-permute-start.9 = (bf16[128,1024]{1,0:T(8,128)(2,1)S(1)}, bf16[128,1024]{1,0:T(8,128)(2,1)S(1)}, u32[]{:S(2)}, u32[]{:S(2)}) collective-permute-start(bf16[128,1024]{1,0:T(8,128)(2,1)S(1)} %get-tuple-element.35), channel_id=1, source_target_pairs={{0,128},{64,192},{128,0},{192,64},{1,129},{65,193},{129,1},{193,65... | collective-permute-start | bytes 786440 | tf_op jit(solution)/shard_map/ppermute | solution.py:361
  83.9 1.4 %collective-permute-start.10 = (bf16[128,1024]{1,0:T(8,128)(2,1)S(1)}, bf16[128,1024]{1,0:T(8,128)(2,1)S(1)}, u32[]{:S(2)}, u32[]{:S(2)}) collective-permute-start(bf16[128,1024]{1,0:T(8,128)(2,1)S(1)} %get-tuple-element.36), channel_id=1, source_target_pairs={{0,192},{64,0},{128,64},{192,128},{1,193},{65,1},{129,65},{193,129... | collective-permute-start | bytes 786440 | tf_op jit(solution)/shard_map/ppermute | solution.py:361
  85.4 4.3 %collective-permute-done.8.refs_1_ = bf16[128,1024]{1,0:T(8,128)(2,1)S(1)} collective-permute-done((bf16[128,1024]{1,0:T(8,128)(2,1)S(1)}, bf16[128,1024]{1,0:T(8,128)(2,1)S(1)}, u32[]{:S(2)}, u32[]{:S(2)}) %collective-permute-start.8) | collective-permute-done | bytes 262176 | tf_op jit(solution)/shard_map/ppermute | solution.py:361
  89.6 6.6 %collective-permute-done.9.refs_2_ = bf16[128,1024]{1,0:T(8,128)(2,1)S(1)} collective-permute-done((bf16[128,1024]{1,0:T(8,128)(2,1)S(1)}, bf16[128,1024]{1,0:T(8,128)(2,1)S(1)}, u32[]{:S(2)}, u32[]{:S(2)}) %collective-permute-start.9) | collective-permute-done | bytes 262176 | tf_op jit(solution)/shard_map/ppermute | solution.py:361
  96.2 0.0 collective-permute-done.10.refs_3_
  96.2 0.0 copy-done.11
  96.2 1.1 shard_map.82
  97.4 1.4 %collective-permute-start.11 = (bf16[128,1024]{1,0:T(8,128)(2,1)S(1)}, bf16[128,1024]{1,0:T(8,128)(2,1)S(1)}, u32[]{:S(2)}, u32[]{:S(2)}) collective-permute-start(bf16[128,1024]{1,0:T(8,128)(2,1)S(1)} %get-tuple-element.38), channel_id=1, source_target_pairs={{0,64},{64,128},{128,192},{192,0},{1,65},{65,129},{129,193},{193,1... | collective-permute-start | bytes 786440 | tf_op jit(solution)/shard_map/ppermute | solution.py:361
  98.8 2.4 %collective-permute-start.12 = (bf16[128,1024]{1,0:T(8,128)(2,1)S(1)}, bf16[128,1024]{1,0:T(8,128)(2,1)S(1)}, u32[]{:S(2)}, u32[]{:S(2)}) collective-permute-start(bf16[128,1024]{1,0:T(8,128)(2,1)S(1)} %get-tuple-element.39), channel_id=1, source_target_pairs={{0,128},{64,192},{128,0},{192,64},{1,129},{65,193},{129,1},{193,65... | collective-permute-start | bytes 786440 | tf_op jit(solution)/shard_map/ppermute | solution.py:361
  101.2 1.6 %collective-permute-start.13 = (bf16[128,1024]{1,0:T(8,128)(2,1)S(1)}, bf16[128,1024]{1,0:T(8,128)(2,1)S(1)}, u32[]{:S(2)}, u32[]{:S(2)}) collective-permute-start(bf16[128,1024]{1,0:T(8,128)(2,1)S(1)} %get-tuple-element.40), channel_id=1, source_target_pairs={{0,192},{64,0},{128,64},{192,128},{1,193},{65,1},{129,65},{193,129... | collective-permute-start | bytes 786440 | tf_op jit(solution)/shard_map/ppermute | solution.py:361
  102.7 4.0 %collective-permute-done.11.refs_1_ = bf16[128,1024]{1,0:T(8,128)(2,1)S(1)} collective-permute-done((bf16[128,1024]{1,0:T(8,128)(2,1)S(1)}, bf16[128,1024]{1,0:T(8,128)(2,1)S(1)}, u32[]{:S(2)}, u32[]{:S(2)}) %collective-permute-start.11) | collective-permute-done | bytes 262176 | tf_op jit(solution)/shard_map/ppermute | solution.py:361
  106.7 6.3 %collective-permute-done.12.refs_2_ = bf16[128,1024]{1,0:T(8,128)(2,1)S(1)} collective-permute-done((bf16[128,1024]{1,0:T(8,128)(2,1)S(1)}, bf16[128,1024]{1,0:T(8,128)(2,1)S(1)}, u32[]{:S(2)}, u32[]{:S(2)}) %collective-permute-start.12) | collective-permute-done | bytes 262176 | tf_op jit(solution)/shard_map/ppermute | solution.py:361
  113.0 0.0 collective-permute-done.13.refs_3_
  113.0 2.1 %shard_map.83 = bf16[128,4096]{1,0:T(8,128)(2,1)} custom-call(s32[2]{0:T(128)S(1)} %pad_add_fusion.index, bf16[128,1024]{1,0:T(8,128)(2,1)S(1)} %get-tuple-element.37.refs_0_, bf16[128,1024]{1,0:T(8,128)(2,1)S(1)} %collective-permute-done.11.refs_1_, bf16[128,1024]{1,0:T(8,128)(2,1)S(1)} %collective-permute-done.12.refs_2_, ...), custom_call_target="tpu_custom_call" | custom-call | bytes 2097152 | tf_op jit(solution)/shard_map/pallas_call | solution.py:344
  (9 shorter events, 0.0 us)
Async XLA Ops:
  0.0 5.1 %copy-start.14 = (s32[1,128]{1,0:T(1,128)S(1)}, s32[1,128]{1,0:T(1,128)}, u32[]{:S(2)}) copy-start(s32[1,128]{1,0:T(1,128)} %ids_ref.7) | copy-start | bytes 1540
  0.0 1.2 %copy-start = (bf16[1,1,128,4096]{3,2,1,0:T(8,128)(2,1)S(1)}, bf16[1,1,128,4096]{3,2,1,0:T(8,128)(2,1)}, u32[]{:S(2)}) copy-start(bf16[1,1,128,4096]{3,2,1,0:T(8,128)(2,1)} %param.9) | copy-start | bytes 3145732
  1.2 1.2 %copy-start.2 = (bf16[1,1,128,4096]{3,2,1,0:T(8,128)(2,1)S(1)}, bf16[1,1,128,4096]{3,2,1,0:T(8,128)(2,1)}, u32[]{:S(2)}) copy-start(bf16[1,1,128,4096]{3,2,1,0:T(8,128)(2,1)} %param.10) | copy-start | bytes 3145732
  2.5 0.7 copy-start.9
  3.2 0.7 copy-start.13
  3.8 1.2 %copy-start.1 = (bf16[1,1,128,4096]{3,2,1,0:T(8,128)(2,1)S(1)}, bf16[1,1,128,4096]{3,2,1,0:T(8,128)(2,1)}, u32[]{:S(2)}) copy-start(bf16[1,1,128,4096]{3,2,1,0:T(8,128)(2,1)} %param.9) | copy-start | bytes 3145732
  3.8 1.5 %copy-start.3 = (bf16[1,1,128,4096]{3,2,1,0:T(8,128)(2,1)S(1)}, bf16[1,1,128,4096]{3,2,1,0:T(8,128)(2,1)}, u32[]{:S(2)}) copy-start(bf16[1,1,128,4096]{3,2,1,0:T(8,128)(2,1)} %param.10) | copy-start | bytes 3145732
  3.8 1.5 %copy-start.10 = (f32[1,1,32,128]{3,2,1,0:T(8,128)S(1)}, f32[1,1,32,128]{3,2,1,0:T(8,128)}, u32[]{:S(2)}) copy-start(f32[1,1,32,128]{3,2,1,0:T(8,128)} %param.12) | copy-start | bytes 49156
  5.0 2.0 %collective-permute-start = (bf16[4,544,128]{2,1,0:T(8,128)(2,1)S(1)}, bf16[4,544,128]{2,1,0:T(8,128)(2,1)S(1)}, u32[]{:S(2)}, u32[]{:S(2)}) collective-permute-start(bf16[4,544,128]{2,1,0:T(8,128)(2,1)S(1)} %shard_map.75), channel_id=1, source_target_pairs={{0,1},{1,0},{2,3},{3,2},{4,5},{5,4},{6,7},{7,6},{8,9},{9,8},{10,11... | collective-permute-start | bytes 1671176 | tf_op jit(solution)/shard_map/ppermute | solution.py:367
  7.8 0.8 copy-start.5
  8.6 53.8 %copy-start.4 = (bf16[1,1,128,4096]{3,2,1,0:T(8,128)(2,1)S(1)}, bf16[1,1,128,4096]{3,2,1,0:T(8,128)(2,1)}, u32[]{:S(2)}) copy-start(bf16[1,1,128,4096]{3,2,1,0:T(8,128)(2,1)} %param.8) | copy-start | bytes 3145732
  8.6 51.3 %copy-start.6 = (bf16[4,544,128]{2,1,0:T(8,128)(2,1)S(1)}, bf16[4,544,128]{2,1,0:T(8,128)(2,1)}, u32[]{:S(2)}) copy-start(bf16[4,544,128]{2,1,0:T(8,128)(2,1)} %copy-done.5) | copy-start | bytes 1671172
  8.6 6.6 %collective-permute-start.1 = (bf16[544,128]{1,0:T(8,128)(2,1)S(1)}, bf16[544,128]{1,0:T(8,128)(2,1)S(1)}, u32[]{:S(2)}, u32[]{:S(2)}) collective-permute-start(bf16[544,128]{1,0:T(8,128)(2,1)S(1)} %get-tuple-element.24), channel_id=1, source_target_pairs={{0,2},{2,4},{4,6},{6,0},{1,3},{3,5},{5,7},{7,1},{8,10},{10,12},{12... | collective-permute-start | bytes 417800 | tf_op jit(solution)/shard_map/ppermute | solution.py:361
  10.2 8.1 %collective-permute-start.2 = (bf16[544,128]{1,0:T(8,128)(2,1)S(1)}, bf16[544,128]{1,0:T(8,128)(2,1)S(1)}, u32[]{:S(2)}, u32[]{:S(2)}) collective-permute-start(bf16[544,128]{1,0:T(8,128)(2,1)S(1)} %get-tuple-element.25), channel_id=1, source_target_pairs={{0,4},{2,6},{4,0},{6,2},{1,5},{3,7},{5,1},{7,3},{8,12},{10,14},{12... | collective-permute-start | bytes 417800 | tf_op jit(solution)/shard_map/ppermute | solution.py:361
  12.9 7.2 %collective-permute-start.3 = (bf16[544,128]{1,0:T(8,128)(2,1)S(1)}, bf16[544,128]{1,0:T(8,128)(2,1)S(1)}, u32[]{:S(2)}, u32[]{:S(2)}) collective-permute-start(bf16[544,128]{1,0:T(8,128)(2,1)S(1)} %get-tuple-element.26), channel_id=1, source_target_pairs={{0,6},{2,0},{4,2},{6,4},{1,7},{3,1},{5,3},{7,5},{8,14},{10,8},{12,... | collective-permute-start | bytes 417800 | tf_op jit(solution)/shard_map/ppermute | solution.py:361
  50.6 5.0 %collective-permute-start.4 = (bf16[512,128]{1,0:T(8,128)(2,1)S(1)}, bf16[512,128]{1,0:T(8,128)(2,1)S(1)}, u32[]{:S(2)}, u32[]{:S(2)}) collective-permute-start(bf16[512,128]{1,0:T(8,128)(2,1)S(1)} %get-tuple-element.28), channel_id=1, source_target_pairs={{0,2},{2,4},{4,6},{6,0},{1,3},{3,5},{5,7},{7,1},{8,10},{10,12},{12... | collective-permute-start | bytes 393224 | tf_op jit(solution)/shard_map/ppermute | solution.py:361
  52.0 6.6 %collective-permute-start.5 = (bf16[512,128]{1,0:T(8,128)(2,1)S(1)}, bf16[512,128]{1,0:T(8,128)(2,1)S(1)}, u32[]{:S(2)}, u32[]{:S(2)}) collective-permute-start(bf16[512,128]{1,0:T(8,128)(2,1)S(1)} %get-tuple-element.29), channel_id=1, source_target_pairs={{0,4},{2,6},{4,0},{6,2},{1,5},{3,7},{5,1},{7,3},{8,12},{10,14},{12... | collective-permute-start | bytes 393224 | tf_op jit(solution)/shard_map/ppermute | solution.py:361
  53.6 6.3 %collective-permute-start.6 = (bf16[512,128]{1,0:T(8,128)(2,1)S(1)}, bf16[512,128]{1,0:T(8,128)(2,1)S(1)}, u32[]{:S(2)}, u32[]{:S(2)}) collective-permute-start(bf16[512,128]{1,0:T(8,128)(2,1)S(1)} %get-tuple-element.30), channel_id=1, source_target_pairs={{0,6},{2,0},{4,2},{6,4},{1,7},{3,1},{5,3},{7,5},{8,14},{10,8},{12,... | collective-permute-start | bytes 393224 | tf_op jit(solution)/shard_map/ppermute | solution.py:361
  61.6 0.8 copy-start.7
  62.4 6.6 %collective-permute-start.7 = (bf16[4,512,128]{2,1,0:T(8,128)(2,1)}, bf16[4,512,128]{2,1,0:T(8,128)(2,1)}, u32[]{:S(2)}, u32[]{:S(2)}) collective-permute-start(bf16[4,512,128]{2,1,0:T(8,128)(2,1)} %get-tuple-element.32), channel_id=1, source_target_pairs={{0,1},{1,0},{2,3},{3,2},{4,5},{5,4},{6,7},{7,6},{8,9},{9,8},{10,11... | collective-permute-start | bytes 1572872 | tf_op jit(solution)/shard_map/ppermute | solution.py:367
  62.4 6.6 %copy-start.8 = (bf16[4,512,128]{2,1,0:T(8,128)(2,1)S(1)}, bf16[4,512,128]{2,1,0:T(8,128)(2,1)}, u32[]{:S(2)}) copy-start(bf16[4,512,128]{2,1,0:T(8,128)(2,1)} %copy-done.7) | copy-start | bytes 1572868
  62.4 6.6 %copy-start.12 = (bf16[1,4096]{1,0:T(2,128)(2,1)S(1)}, bf16[1,4096]{1,0:T(2,128)(2,1)}, u32[]{:S(2)}) copy-start(bf16[1,4096]{1,0:T(2,128)(2,1)} %gain_ref.1) | copy-start | bytes 24580
  69.0 27.2 %copy-start.11 = (bf16[1,128,1024]{2,1,0:T(8,128)(2,1)S(1)}, bf16[1,128,1024]{2,1,0:T(8,128)(2,1)}, u32[]{:S(2)}) copy-start(bf16[1,128,1024]{2,1,0:T(8,128)(2,1)} %param.7) | copy-start | bytes 786436
  79.6 10.0 %collective-permute-start.8 = (bf16[128,1024]{1,0:T(8,128)(2,1)S(1)}, bf16[128,1024]{1,0:T(8,128)(2,1)S(1)}, u32[]{:S(2)}, u32[]{:S(2)}) collective-permute-start(bf16[128,1024]{1,0:T(8,128)(2,1)S(1)} %get-tuple-element.34), channel_id=1, source_target_pairs={{0,64},{64,128},{128,192},{192,0},{1,65},{65,129},{129,193},{193,1... | collective-permute-start | bytes 786440 | tf_op jit(solution)/shard_map/ppermute | solution.py:361
  81.2 15.0 %collective-permute-start.9 = (bf16[128,1024]{1,0:T(8,128)(2,1)S(1)}, bf16[128,1024]{1,0:T(8,128)(2,1)S(1)}, u32[]{:S(2)}, u32[]{:S(2)}) collective-permute-start(bf16[128,1024]{1,0:T(8,128)(2,1)S(1)} %get-tuple-element.35), channel_id=1, source_target_pairs={{0,128},{64,192},{128,0},{192,64},{1,129},{65,193},{129,1},{193,65... | collective-permute-start | bytes 786440 | tf_op jit(solution)/shard_map/ppermute | solution.py:361
  83.9 12.3 %collective-permute-start.10 = (bf16[128,1024]{1,0:T(8,128)(2,1)S(1)}, bf16[128,1024]{1,0:T(8,128)(2,1)S(1)}, u32[]{:S(2)}, u32[]{:S(2)}) collective-permute-start(bf16[128,1024]{1,0:T(8,128)(2,1)S(1)} %get-tuple-element.36), channel_id=1, source_target_pairs={{0,192},{64,0},{128,64},{192,128},{1,193},{65,1},{129,65},{193,129... | collective-permute-start | bytes 786440 | tf_op jit(solution)/shard_map/ppermute | solution.py:361
  97.4 9.3 %collective-permute-start.11 = (bf16[128,1024]{1,0:T(8,128)(2,1)S(1)}, bf16[128,1024]{1,0:T(8,128)(2,1)S(1)}, u32[]{:S(2)}, u32[]{:S(2)}) collective-permute-start(bf16[128,1024]{1,0:T(8,128)(2,1)S(1)} %get-tuple-element.38), channel_id=1, source_target_pairs={{0,64},{64,128},{128,192},{192,0},{1,65},{65,129},{129,193},{193,1... | collective-permute-start | bytes 786440 | tf_op jit(solution)/shard_map/ppermute | solution.py:361
  98.8 14.2 %collective-permute-start.12 = (bf16[128,1024]{1,0:T(8,128)(2,1)S(1)}, bf16[128,1024]{1,0:T(8,128)(2,1)S(1)}, u32[]{:S(2)}, u32[]{:S(2)}) collective-permute-start(bf16[128,1024]{1,0:T(8,128)(2,1)S(1)} %get-tuple-element.39), channel_id=1, source_target_pairs={{0,128},{64,192},{128,0},{192,64},{1,129},{65,193},{129,1},{193,65... | collective-permute-start | bytes 786440 | tf_op jit(solution)/shard_map/ppermute | solution.py:361
  101.2 11.8 %collective-permute-start.13 = (bf16[128,1024]{1,0:T(8,128)(2,1)S(1)}, bf16[128,1024]{1,0:T(8,128)(2,1)S(1)}, u32[]{:S(2)}, u32[]{:S(2)}) collective-permute-start(bf16[128,1024]{1,0:T(8,128)(2,1)S(1)} %get-tuple-element.40), channel_id=1, source_target_pairs={{0,192},{64,0},{128,64},{192,128},{1,193},{65,1},{129,65},{193,129... | collective-permute-start | bytes 786440 | tf_op jit(solution)/shard_map/ppermute | solution.py:361

commit v2 on v1

v2 whole, which is shorter than its diff:
```python
import functools

import jax
import jax.numpy as jnp
from jax import lax
from jax.experimental import pallas as pl
from jax.experimental.pallas import tpu as pltpu
from jax.sharding import Mesh
from jax.sharding import PartitionSpec as P

EPSILON = 1e-05
F32, BF16 = jnp.float32, jnp.bfloat16
D = 128
HEADS = 32
HALF = HEADS // 2
GROUP = HALF // 4
NZ = 8
META = 32
ROWS = GROUP * D
PART = ROWS + META
VMEM_LIMIT = 16 * 1024 * 1024
ATTEND_LIMIT = 52 * 1024 * 1024
INTRA_LIMIT = 60 * 1024 * 1024


def nt(a, b):
    return lax.dot_general(a, b, (((1,), (1,)), ((), ())), preferred_element_type=F32)


def iota(shape, axis):
    return lax.broadcasted_iota(jnp.int32, shape, axis)


def split3(x):
    hi = x.astype(BF16).astype(F32)
    mid = (x - hi).astype(BF16).astype(F32)
    return hi, mid, x - hi - mid


def three_parts(x):
    return jnp.concatenate([part.astype(BF16) for part in split3(x)], axis=1)


def running_sums(decay):
    shape = (D, 3 * D)
    lower = (lax.rem(iota(shape, 1), D) <= iota(shape, 0)).astype(F32).astype(BF16)
    return nt(three_parts(decay), lower)


def rows_of(ids_row):
    return jnp.transpose(jnp.broadcast_to(ids_row, (D, D)))


def pack_meta(decay, first, last):
    row = iota((8, D), 0)
    ids = jnp.where(row == 0, first, jnp.where(row == 1, last, 0.0))
    return jnp.concatenate([*split3(decay), ids], axis=0).astype(BF16)


def unpack_meta(meta):
    meta = meta.astype(F32)
    return meta[0:8] + meta[8:16] + meta[16:24], meta[24:25], meta[25:26]


def same(a, b):
    return (a == b).astype(F32)


def summarise(ids, decay, head_rows, out_ref, cut_ref):
    first, last = ids[:, 0:1], ids[:, D - 1 : D]
    total = nt(three_parts(decay), jnp.ones((D, 3 * D), BF16))
    carried = jnp.exp(total - running_sums(decay)) * same(ids, last)
    for group in range(4):
        keys, values = head_rows(group)
        for i in range(GROUP):
            h = group * GROUP + i
            lanes = slice(i * D, (i + 1) * D)
            keyed = (jnp.transpose(keys[:, lanes].astype(F32)) * carried[h : h + 1]).astype(BF16)
            state = jnp.dot(keyed, values[:, lanes], preferred_element_type=F32)
            out_ref[group, i * D : (i + 1) * D, :] = state.astype(BF16)
        cut_ref[0:GROUP, :] = total[group * GROUP : (group + 1) * GROUP, :]
        cut_ref[GROUP:8, :] = jnp.zeros((8 - GROUP, D), F32)
        out_ref[group, ROWS:PART, :] = pack_meta(
            cut_ref[...], jnp.broadcast_to(first, (1, D)), jnp.broadcast_to(last, (1, D))
        )


def summary_kernel(index, k_ref, v_ref, decay_ref, ids_ref, out_ref, cut_ref):
    decay = decay_ref[pl.ds(pl.multiple_of(index[0] * HALF, HALF), HALF), :]

    def head_rows(group):
        lanes = slice(group * ROWS, (group + 1) * ROWS)
        return k_ref[:, lanes], v_ref[:, lanes]

    summarise(ids_ref[...].astype(F32), decay, head_rows, out_ref, cut_ref)


SUMMARY_COST = pl.CostEstimate(flops=2 * HALF * D**3, bytes_accessed=3 * HALF * D * D * 2, transcendentals=0)


def summaries(half, keys, values, decay, ids):
    whole = lambda shape: pl.BlockSpec(shape, lambda i, s: (0,) * len(shape))
    return pl.pallas_call(
        summary_kernel,
        out_shape=jax.ShapeDtypeStruct((4, PART, D), BF16),
        grid_spec=pltpu.PrefetchScalarGridSpec(
            num_scalar_prefetch=1,
            grid=(1,),
            in_specs=[
                pl.BlockSpec((D, HALF * D), lambda i, s: (0, s[0])),
                pl.BlockSpec((D, HALF * D), lambda i, s: (0, s[0])),
                whole((HEADS, D)),
                whole((1, D)),
            ],
            out_specs=whole((4, PART, D)),
            scratch_shapes=[pltpu.VMEM((8, D), F32)],
        ),
        compiler_params=pltpu.CompilerParams(vmem_limit_bytes=VMEM_LIMIT),
        cost_estimate=SUMMARY_COST,
    )(half, keys, values, decay, ids)


def two_parts(x):
    hi = x.astype(BF16)
    return hi, (x - hi.astype(F32)).astype(BF16)


def intra_kernel(wave, q_ref, k_ref, v_ref, decay_ref, ids_ref, out_ref, factor_ref, column_ref, row_ref, allowed_ref):
    step = pl.program_id(0)

    @pl.when(step == 0)
    def _():
        ids = ids_ref[...].astype(F32)
        row_ref[0:HEADS, :] = running_sums(decay_ref[...])
        row_ref[HEADS:D, :] = jnp.zeros((D - HEADS, D), F32)
        sums = jnp.transpose(row_ref[...])
        documents = rows_of(ids)
        scaling = jnp.exp(sums) * same(documents, ids[:, 0:1])
        for quarter in range(4):
            heads = slice(8 * quarter + GROUP * wave, 8 * quarter + GROUP * (wave + 1))
            column_ref[quarter, :, 0:GROUP] = sums[:, heads]
            factor_ref[quarter] = jnp.concatenate(two_parts(scaling[:, heads]), axis=1)
        allowed_ref[...] = ((iota((D, D), 1) <= iota((D, D), 0)) & (documents == ids)).astype(F32)

    allowed = allowed_ref[...] > 0.0
    columns = column_ref[step]
    rows = row_ref[pl.ds(pl.multiple_of(8 * step, 8), 8), :]
    for i in range(GROUP):
        h = GROUP * wave + i
        lanes = slice(i * D, (i + 1) * D)
        spread = jnp.minimum(columns[:, i : i + 1] - rows[h : h + 1, :], 0.0)
        weighting = jnp.where(allowed, jnp.exp(spread), 0.0)
        keys = jnp.transpose(k_ref[:, lanes].astype(F32)).astype(BF16)
        attn = (jnp.dot(q_ref[:, lanes], keys, preferred_element_type=F32) * weighting).astype(BF16)
        out_ref[0, :, lanes] = jnp.dot(attn, v_ref[:, lanes], preferred_element_type=F32)


def intra_term(wave, queries, keys, values, decay, ids):
    block = pl.BlockSpec((D, ROWS), lambda i: (0, 2 * i + wave))
    return pl.pallas_call(
        functools.partial(intra_kernel, wave),
        out_shape=[jax.ShapeDtypeStruct((4, D, ROWS), F32), jax.ShapeDtypeStruct((4, D, 2 * GROUP), BF16)],
        grid=(4,),
        in_specs=[
            block,
            block,
            block,
            pl.BlockSpec((HEADS, D), lambda i: (0, 0)),
            pl.BlockSpec((1, D), lambda i: (0, 0)),
        ],
        out_specs=[
            pl.BlockSpec((1, D, ROWS), lambda i: (i, 0, 0)),
            pl.BlockSpec((4, D, 2 * GROUP), lambda i: (0, 0, 0)),
        ],
        scratch_shapes=[pltpu.VMEM((4, D, 8), F32), pltpu.VMEM((D, D), F32), pltpu.VMEM((D, D), F32)],
        compiler_params=pltpu.CompilerParams(vmem_limit_bytes=INTRA_LIMIT),
        cost_estimate=pl.CostEstimate(
            flops=2 * HEADS * D**3, bytes_accessed=5 * HALF * D * D * 2, transcendentals=HALF * D * D
        ),
    )(queries, keys, values, decay, ids)


def chip_kernel(index, own_ref, other_ref, *out_refs):
    y, core = index[0], index[1]
    is_one = core == 1
    for step in range(4):
        group = lax.rem(y + step, 4)
        decay_own, first_own, last_own = unpack_meta(own_ref[group, ROWS:PART, :])
        decay_other, first_other, last_other = unpack_meta(other_ref[group, ROWS:PART, :])
        joined = same(last_own, last_other)
        later = jnp.where(is_one, decay_own, decay_other)
        passed = jnp.exp(later) * joined
        weight_own = jnp.where(is_one, 1.0, passed)
        weight_other = jnp.where(is_one, passed, 1.0)
        for i in range(GROUP):
            rows = slice(i * D, (i + 1) * D)
            out_refs[step][rows, :] = (
                weight_own[i : i + 1] * own_ref[group, rows, :].astype(F32)
                + weight_other[i : i + 1] * other_ref[group, rows, :].astype(F32)
            ).astype(BF16)
        out_refs[step][ROWS:PART, :] = pack_meta(
            decay_own + decay_other,
            jnp.where(is_one, first_other, first_own),
            jnp.where(is_one, last_own, last_other),
        )


def small_call(kernel, index, operands, outs, scratch=(), after=()):
    whole = lambda shape: pl.BlockSpec(shape, lambda i, s: (0,) * len(shape))
    size = sum(a.size * a.dtype.itemsize for a in operands)
    many, extra = len(operands), len(after)

    def body(index, *refs):
        kernel(index, *refs[:many], *refs[many + extra :])

    return pl.pallas_call(
        body,
        out_shape=[jax.ShapeDtypeStruct(shape, dtype) for shape, dtype in outs],
        grid_spec=pltpu.PrefetchScalarGridSpec(
            num_scalar_prefetch=1,
            grid=(1,),
            in_specs=[whole(a.shape) for a in operands] + [pl.BlockSpec(memory_space=pl.ANY)] * extra,
            out_specs=[whole(shape) for shape, _ in outs],
            scratch_shapes=list(scratch),
        ),
        compiler_params=pltpu.CompilerParams(vmem_limit_bytes=VMEM_LIMIT),
        cost_estimate=pl.CostEstimate(flops=size, bytes_accessed=2 * size, transcendentals=0),
    )(index, *operands, *after)


def in_order(y, slots, ordered_ref):
    for step in range(4):
        ordered_ref[lax.rem(y + 4 - step, 4)] = slots[step][...]


def row_kernel(index, *refs):
    *slots, out_ref, ordered_ref = refs
    in_order(index[0], slots, ordered_ref)
    metas = [unpack_meta(ordered_ref[c, ROWS:PART, :]) for c in range(4)]
    weights, after = [None] * 4, jnp.zeros((8, D), F32)
    for c in (3, 2, 1, 0):
        weights[c] = jnp.exp(after) * same(metas[c][2], metas[3][2])
        after = after + metas[c][0]
    row = iota((16, D), 0)
    for i in range(GROUP):
        rows = slice(i * D, (i + 1) * D)
        state = sum(weights[c][i : i + 1] * ordered_ref[c, rows, :].astype(F32) for c in range(4)).astype(BF16)
        out_ref[2 * i, 0 : D // 2, :] = state[0 : D // 2]
        out_ref[2 * i + 1, 0 : D // 2, :] = state[D // 2 :]
        hi, mid, low = split3(after[i : i + 1])
        meta = jnp.zeros((16, D), F32)
        for at, value in enumerate((hi, mid, low, metas[0][1], metas[3][2])):
            meta = jnp.where(row == at, value, meta)
        out_ref[2 * i, D // 2 :, :] = meta.astype(BF16)
        out_ref[2 * i + 1, D // 2 :, :] = meta.astype(BF16)


def scan_kernel(index, in_ref, out_ref):
    del index
    state = jnp.zeros((D // 2, D), F32)
    before = jnp.full((1, D), -1.0, F32)
    for z in range(NZ):
        meta = in_ref[z, D // 2 :, :].astype(F32)
        decay, first, last = meta[0:1] + meta[1:2] + meta[2:3], meta[3:4], meta[4:5]
        state = state * same(before, first)
        out_ref[z] = state.astype(BF16)
        state = jnp.exp(decay) * same(first, last) * state + in_ref[z, 0 : D // 2, :].astype(F32)
        before = last


def spread_kernel(index, state_ref, *refs):
    *slots, out0, out1, out2, out3, ordered_ref, result_ref = refs
    y = index[0]
    in_order(y, slots, ordered_ref)
    metas = [unpack_meta(ordered_ref[c, ROWS:PART, :]) for c in range(4)]
    passing = [jnp.exp(decay) * same(first, last) for decay, first, last in metas]
    joined = [None] + [same(metas[c - 1][2], metas[c][1]) for c in (1, 2, 3)]
    for i in range(GROUP):
        rows = slice(i * D, (i + 1) * D)
        state = state_ref[rows, :].astype(F32)
        result_ref[0, rows, :] = state.astype(BF16)
        for c in (1, 2, 3):
            state = passing[c - 1][i : i + 1] * state + ordered_ref[c - 1, rows, :].astype(F32)
            state = state * joined[c]
            result_ref[c, rows, :] = state.astype(BF16)
    for step, out_ref in enumerate((out0, out1, out2, out3)):
        out_ref[...] = result_ref[lax.rem(y + step, 4)]


def core_kernel(index, own_ref, other_ref, s0, s1, s2, s3, out_ref):
    y, core, target = index[0], index[1], index[2]
    is_one = core == 1

    @pl.when(target == 0)
    def _():
        for step, slot in enumerate((s0, s1, s2, s3)):
            out_ref[lax.rem(y + 4 - step, 4)] = slot[...]

    @pl.when(target == 1)
    def _():
        for step, slot in enumerate((s0, s1, s2, s3)):
            group = lax.rem(y + 4 - step, 4)
            decay_own, first_own, last_own = unpack_meta(own_ref[group, ROWS:PART, :])
            decay_other, first_other, last_other = unpack_meta(other_ref[group, ROWS:PART, :])
            decay = jnp.where(is_one, decay_other, decay_own)
            first0 = jnp.where(is_one, first_other, first_own)
            last0 = jnp.where(is_one, last_other, last_own)
            first1 = jnp.where(is_one, first_own, first_other)
            joined = same(last0, first1)
            passing = jnp.exp(decay) * same(first0, last0) * joined
            for i in range(GROUP):
                rows = slice(i * D, (i + 1) * D)
                earlier = jnp.where(is_one, other_ref[group, rows, :], own_ref[group, rows, :]).astype(F32)
                later = passing[i : i + 1] * slot[rows, :].astype(F32) + joined * earlier
                out_ref[group, rows, :] = later.astype(BF16)


def attend_kernel(
    wave, index, q_ref, intra_ref, mine_ref, other_ref, factor_ref, gain_ref, *refs
):
    *out_refs, queries, intra, sem = refs
    copies = []
    for step in range(4):
        quarter = lax.rem(index[0] + step, 4)
        lanes = pl.ds(pl.multiple_of((2 * quarter + wave) * ROWS, ROWS), ROWS)
        copies.append(
            [
                pltpu.make_async_copy(q_ref.at[:, lanes], queries.at[step], sem.at[0, step]),
                pltpu.make_async_copy(intra_ref.at[quarter], intra.at[step], sem.at[1, step]),
            ]
        )
    for pair in copies:
        for copy in pair:
            copy.start()
    shape = (2 * GROUP, ROWS)
    spreading = (lax.rem(iota(shape, 0), GROUP) == iota(shape, 1) // D).astype(F32).astype(BF16)
    for step in range(4):
        quarter = lax.rem(index[0] + step, 4)
        group = 2 * quarter + wave
        use_mine = (quarter // 2) == index[1]
        factors = jnp.dot(factor_ref[quarter], spreading, preferred_element_type=F32)
        gain = gain_ref[group]
        for copy in copies[step]:
            copy.wait()
        for i in range(GROUP):
            lanes = slice(i * D, (i + 1) * D)
            at = lax.rem(group, 4)
            state = jnp.where(use_mine, mine_ref[at, lanes, :], other_ref[at, lanes, :])
            inter = jnp.dot(queries[step, :, lanes], state, preferred_element_type=F32)
            total = intra[step, :, lanes] + inter * factors[:, lanes]
            power = jnp.mean(total * total, axis=1, keepdims=True)
            out_refs[step][:, lanes] = (
                total * lax.rsqrt(power + EPSILON) * gain[:, lanes].astype(F32)
            ).astype(BF16)


def attend(wave, index, queries, intra, factors, mine, other, gain):
    whole = lambda shape: pl.BlockSpec(shape, lambda i, s: (0,) * len(shape))
    anywhere = pl.BlockSpec(memory_space=pl.ANY)
    return pl.pallas_call(
        functools.partial(attend_kernel, wave),
        out_shape=[jax.ShapeDtypeStruct((D, ROWS), BF16)] * 4,
        grid_spec=pltpu.PrefetchScalarGridSpec(
            num_scalar_prefetch=1,
            grid=(1,),
            in_specs=[
                anywhere,
                anywhere,
                whole(mine.shape),
                whole(other.shape),
                whole(factors.shape),
                whole(gain.shape),
            ],
            out_specs=[whole((D, ROWS))] * 4,
            scratch_shapes=[
                pltpu.VMEM((4, D, ROWS), BF16),
                pltpu.VMEM((4, D, ROWS), F32),
                pltpu.SemaphoreType.DMA((2, 4)),
            ],
        ),
        compiler_params=pltpu.CompilerParams(vmem_limit_bytes=ATTEND_LIMIT),
        cost_estimate=pl.CostEstimate(
            flops=HEADS * D**3, bytes_accessed=4 * HEADS * D * D * 2, transcendentals=HEADS * D
        ),
    )(index, queries, intra, mine, other, factors, gain)


def layers_kernel(wave, index, tokens_ref, *refs):
    *slots, out0, out1, out2, out3, ordered_ref = refs
    phase = index[0]
    in_order(phase, slots, ordered_ref)
    current = tokens_ref[:, wave * ROWS : (wave + 1) * ROWS].astype(F32)
    for s in range(4):
        rounded = (current + ordered_ref[s].astype(F32)).astype(BF16)
        ordered_ref[s] = rounded
        current = rounded.astype(F32)
    for step, out_ref in enumerate((out0, out1, out2, out3)):
        out_ref[...] = ordered_ref[lax.rem(phase + step, 4)]


def place_kernel(index, *refs):
    *slots, out_ref, sem = refs
    copies = []
    for n, slot in enumerate(slots):
        wave, step = n // 4, n % 4
        quarter = lax.rem(index[0] + 4 - step, 4)
        lanes = pl.ds(pl.multiple_of((2 * quarter + wave) * ROWS, ROWS), ROWS)
        copies.append(pltpu.make_async_copy(slot, out_ref.at[:, lanes], sem.at[n]))
    for copy in copies:
        copy.start()
    for copy in copies:
        copy.wait()


def place(index, slots):
    return pl.pallas_call(
        place_kernel,
        out_shape=jax.ShapeDtypeStruct((D, HEADS * D), BF16),
        grid_spec=pltpu.PrefetchScalarGridSpec(
            num_scalar_prefetch=1,
            grid=(1,),
            in_specs=[pl.BlockSpec(memory_space=pl.ANY)] * 8,
            out_specs=pl.BlockSpec(memory_space=pl.ANY),
            scratch_shapes=[pltpu.SemaphoreType.DMA((8,))],
        ),
        compiler_params=pltpu.CompilerParams(vmem_limit_bytes=VMEM_LIMIT),
        cost_estimate=pl.CostEstimate(flops=0, bytes_accessed=4 * HEADS * D * D, transcendentals=0),
    )(index, *slots)


def ring_exchange(slots, axis):
    size = lax.axis_size(axis)
    moved = [
        lax.ppermute(slots[d], axis, [(i, (i + d) % size) for i in range(size)]) for d in range(1, len(slots))
    ]
    return [slots[0], *moved]


def swap_cores(array):
    return lax.ppermute(array, "core", [(0, 1), (1, 0)])


def local(tokens, queries, keys_in, values, norm_gain, log_decay, doc_ids):
    phase, z, y, core = (lax.axis_index(name) for name in ("phase", "z", "y", "core"))
    queries, keys, values, decay = queries[0, 0], keys_in[0, 0], values[0, 0], log_decay[0, 0]
    here = jnp.stack([y, core, z]).astype(jnp.int32)

    sending = summaries(jnp.stack([1 - core]), keys, values, decay, doc_ids)
    other = swap_cores(sending)
    own = summaries(jnp.stack([core]), keys, values, decay, doc_ids)

    part = ((PART, D), BF16)
    slots = ring_exchange(small_call(chip_kernel, here, [own, other], [part] * 4), "y")
    intra = [intra_term(wave, queries, keys, values, decay, doc_ids) for wave in range(2)]

    (parts,) = small_call(
        row_kernel, here, slots, [((NZ, D // 2 + 16, D), BF16)], [pltpu.VMEM((4, PART, D), BF16)], intra[0][1:]
    )
    parts = lax.all_to_all(parts, "z", split_axis=0, concat_axis=0, tiled=True)
    (states,) = small_call(scan_kernel, here, [parts], [((NZ, D // 2, D), BF16)])
    states = lax.all_to_all(states, "z", split_axis=0, concat_axis=0, tiled=True)
    spread = small_call(
        spread_kernel,
        here,
        [states.reshape(ROWS, D), *slots],
        [((ROWS, D), BF16)] * 4,
        [pltpu.VMEM((4, PART, D), BF16), pltpu.VMEM((4, ROWS, D), BF16)],
    )
    spread = ring_exchange(spread, "y")
    out = [((4, ROWS, D), BF16)]
    to_other = jnp.stack([y, core, 1 - core]).astype(jnp.int32)
    (send,) = small_call(core_kernel, to_other, [own, other, *spread], out, after=intra[1][1:])
    theirs = swap_cores(send)
    (mine,) = small_call(core_kernel, jnp.stack([y, core, core]).astype(jnp.int32), [own, other, *spread], out)

    at = jnp.stack([phase, core]).astype(jnp.int32)
    gain = norm_gain.reshape(8, 1, ROWS)
    pieces = []
    for wave in range(2):
        normed = ring_exchange(attend(wave, at, queries, *intra[wave], mine, theirs, gain), "phase")
        sums = small_call(
            functools.partial(layers_kernel, wave),
            at,
            [tokens[0], *normed],
            [((D, ROWS), BF16)] * 4,
            [pltpu.VMEM((4, D, ROWS), BF16)],
        )
        pieces += ring_exchange(sums, "phase")
    return place(at, pieces)[None, None]


def solution(mesh):
    grid = Mesh(mesh.devices.reshape(4, NZ, 4, 2), ("phase", "z", "y", "core"))
    ctx = ("z", "y", "core")
    rows = P("phase", None, ctx, None)
    return jax.shard_map(
        local,
        mesh=grid,
        in_specs=(
            P(None, ctx, "phase"),
            rows,
            rows,
            rows,
            P("phase", None),
            P("phase", None, None, ctx),
            P(None, ctx),
        ),
        out_specs=rows,
        check_vma=False,
    )
```

time: 116 us -> 99.9 us (0.86)
  waiting for transfers between devices: 33 us -> 13.2 us
  starting transfers between devices: 20.6 us -> 25.9 us
  Pallas kernels: 27.1 us -> 24.4 us
    ppermute x12 -> x18, waiting for transfers between devices: 32.5 us -> 10.9 us  [ring_exchange(): lax.ppermute(slots[d], axis, [(i, (i + d) % size) for i in range(size)])]
    ppermute x12 -> x18, starting transfers between devices: 20.5 us -> 25.8 us  [ring_exchange(): lax.ppermute(slots[d], axis, [(i, (i + d) % size) for i in range(size)])]
    ppermute x2, waiting for transfers between devices: 0.44 us -> 2.29 us  [swap_cores(): return lax.ppermute(array, 'core', [(0, 1), (1, 0)])]
    pallas_call x8 -> x12, Pallas kernels: 22.8 us -> 21 us  [the longest x2 9.45 us: intra_term(): pl.pallas_call(functools.partial(intra_kernel, wave), out_shape=[jax.Shap...]
    unnamed x30 -> x26, local copies, waits for them, and re-layouts: 5.74 us -> 6.08 us
  transfers between devices with their start and end apart: 14 -> 20, of which waited for: 11 -> 8; matrix products, arithmetic and copies ran while one was open for 0% -> 0% of each run, Pallas kernels for 7% -> 15%
where the time goes in v2:
time: 99.9 us; the launch traced here: 98.6 us
  blocking collectives  28.5 us (29%)
  starting transfers between devices  25.9 us (26%)
  Pallas kernels  24.4 us (24%)
  waiting for transfers between devices  13.2 us (13%)
  local copies, waits for them, and re-layouts  6.08 us (6%)
    ppermute x18, starting transfers between devices, ring_exchange(): lax.ppermute(slots[d], axis, [(i, (i + d) % size) for i in range(size)])  25.8 us
    all_to_all x1, blocking collectives, local(): parts = lax.all_to_all(parts, 'z', split_axis=0, concat_axis=0, tiled=True)  17 us
    all_to_all x1, blocking collectives, local(): lax.all_to_all(states, 'z', split_axis=0, concat_axis=0, tiled=True)  11.5 us
    ppermute x18, waiting for transfers between devices, ring_exchange(): lax.ppermute(slots[d], axis, [(i, (i + d) % size) for i in range(size)])  10.9 us
    pallas_call x2, Pallas kernels, intra_term(): pl.pallas_call(functools.partial(intra_kernel, wave), out_shape=[jax.Shap...  9.45 us
    unnamed x26, local copies, waits for them, and re-layouts  6.08 us
    pallas_call x8, Pallas kernels, small_call(): pl.pallas_call(body, out_shape=[jax.ShapeDtypeStruct(shape, dtype) for sh...  5.82 us
    pallas_call x2, Pallas kernels, attend(): pl.pallas_call(functools.partial(attend_kernel, wave), out_shape=[jax.Sha...  5.76 us
  transfers between devices with their start and end apart: 20, of which 8 were waited for; matrix products, arithmetic and copies ran while one was open for 0% of the time, Pallas kernels for 15%

profile of v2, /device:TPU:8, one launch (start us, length us, event | category | flops | bytes accessed | tf_op | source)
XLA Modules:
  0.0 98.6 jit_solution(9223506518157613082)
XLA Ops:
  0.0 0.7 copy-done.12
  0.7 1.2 %copy-done = bf16[1,1,128,4096]{3,2,1,0:T(8,128)(2,1)S(1)} copy-done((bf16[1,1,128,4096]{3,2,1,0:T(8,128)(2,1)S(1)}, bf16[1,1,128,4096]{3,2,1,0:T(8,128)(2,1)}, u32[]{:S(2)}) %copy-start) | copy-done | bytes 1048600
  1.9 1.2 %copy-done.2 = bf16[1,1,128,4096]{3,2,1,0:T(8,128)(2,1)S(1)} copy-done((bf16[1,1,128,4096]{3,2,1,0:T(8,128)(2,1)S(1)}, bf16[1,1,128,4096]{3,2,1,0:T(8,128)(2,1)}, u32[]{:S(2)}) %copy-start.2) | copy-done | bytes 1048600
  3.1 0.7 copy-done.9
  3.8 1.3 %shard_map.75 = bf16[4,544,128]{2,1,0:T(8,128)(2,1)} custom-call(s32[1]{0:T(128)} %bitcast.8.index, bf16[128,4096]{1,0:T(8,128)(2,1)S(1)} %bitcast.15, bf16[128,4096]{1,0:T(8,128)(2,1)S(1)} %bitcast.19, f32[32,128]{1,0:T(8,128)S(1)} %bitcast.26, s32[1,128]{1,0:T(1,128)S(1)} %copy-done.12), custom_call_target="tpu_custom_call" | custom-call | flops 67108864 | bytes 1572864 | tf_op jit(solution)/shard_map/pallas_call | solution.py:103
  5.1 0.4 copy-done.3
  5.6 0.5 shard_map.74.refs_0_
  6.1 0.1 pad_add_fusion.3.index
  6.1 1.1 %collective-permute-done.refs_1_ = bf16[4,544,128]{2,1,0:T(8,128)(2,1)S(1)} collective-permute-done((bf16[4,544,128]{2,1,0:T(8,128)(2,1)}, bf16[4,544,128]{2,1,0:T(8,128)(2,1)S(1)}, u32[]{:S(2)}, u32[]{:S(2)}) %collective-permute-start) | collective-permute-done | bytes 557088 | tf_op jit(solution)/shard_map/ppermute | solution.py:440
  7.3 0.8 shard_map.76
  8.1 1.7 %collective-permute-start.1 = (bf16[544,128]{1,0:T(8,128)(2,1)S(1)}, bf16[544,128]{1,0:T(8,128)(2,1)S(1)}, u32[]{:S(2)}, u32[]{:S(2)}) collective-permute-start(bf16[544,128]{1,0:T(8,128)(2,1)S(1)} %get-tuple-element.35), channel_id=1, source_target_pairs={{0,2},{2,4},{4,6},{6,0},{1,3},{3,5},{5,7},{7,1},{8,10},{10,12},{12... | collective-permute-start | bytes 417800 | tf_op jit(solution)/shard_map/ppermute | solution.py:434
  9.7 2.7 %collective-permute-start.2 = (bf16[544,128]{1,0:T(8,128)(2,1)S(1)}, bf16[544,128]{1,0:T(8,128)(2,1)S(1)}, u32[]{:S(2)}, u32[]{:S(2)}) collective-permute-start(bf16[544,128]{1,0:T(8,128)(2,1)S(1)} %get-tuple-element.36), channel_id=1, source_target_pairs={{0,4},{2,6},{4,0},{6,2},{1,5},{3,7},{5,1},{7,3},{8,12},{10,14},{12... | collective-permute-start | bytes 417800 | tf_op jit(solution)/shard_map/ppermute | solution.py:434
  12.4 0.7 collective-permute-start.3
  13.1 4.7 %shard_map.73 = (f32[4,128,512]{2,1,0:T(8,128)}, bf16[4,128,8]{2,1,0:T(8,128)(2,1)}) custom-call(bf16[128,4096]{1,0:T(8,128)(2,1)} %bitcast.30, bf16[128,4096]{1,0:T(8,128)(2,1)} %bitcast.13, bf16[128,4096]{1,0:T(8,128)(2,1)} %bitcast.17, f32[32,128]{1,0:T(8,128)} %bitcast.24, s32[1,128]{1,0:T(1,128)} %ids_ref.7), custom_call_target="tpu_custom_call" | custom-call | flops 134217728 | bytes 2621440 | tf_op jit(solution)/shard_map/pallas_call | solution.py:160
  17.8 0.0 collective-permute-done.1.refs_1_.refs_2_
  17.8 0.0 collective-permute-done.2.refs_2_.refs_3_
  17.8 1.8 %collective-permute-done.3.refs_3_.refs_4_ = bf16[544,128]{1,0:T(8,128)(2,1)S(1)} collective-permute-done((bf16[544,128]{1,0:T(8,128)(2,1)S(1)}, bf16[544,128]{1,0:T(8,128)(2,1)S(1)}, u32[]{:S(2)}, u32[]{:S(2)}) %collective-permute-start.3) | collective-permute-done | bytes 139296 | tf_op jit(solution)/shard_map/ppermute | solution.py:434
  19.7 0.9 copy-done.7
  20.6 0.7 shard_map.77
  21.3 17.0 %all_to_all.10.refs_0_ = bf16[8,80,128]{2,1,0:T(8,128)(2,1)S(1)} all-to-all(bf16[8,80,128]{2,1,0:T(8,128)(2,1)S(1)} %shard_map.77), channel_id=1, replica_groups=mesh['phase'=4,'z'=8,'y'=4,'core'=2] {'z'}, dimensions={0} | all-to-all | bytes 327680 | tf_op jit(solution)/shard_map/all_to_all | solution.py:459
  38.3 0.6 shard_map.78
  38.9 11.5 %all_to_all.11 = bf16[8,64,128]{2,1,0:T(8,128)(2,1)S(1)} all-to-all(bf16[8,64,128]{2,1,0:T(8,128)(2,1)S(1)} %shard_map.78), channel_id=1, replica_groups=mesh['phase'=4,'z'=8,'y'=4,'core'=2] {'z'}, dimensions={0} | all-to-all | bytes 262144 | tf_op jit(solution)/shard_map/all_to_all | solution.py:461
  50.4 0.8 shard_map.79
  51.1 1.4 %collective-permute-start.4 = (bf16[512,128]{1,0:T(8,128)(2,1)S(1)}, bf16[512,128]{1,0:T(8,128)(2,1)S(1)}, u32[]{:S(2)}, u32[]{:S(2)}) collective-permute-start(bf16[512,128]{1,0:T(8,128)(2,1)S(1)} %get-tuple-element.40), channel_id=1, source_target_pairs={{0,2},{2,4},{4,6},{6,0},{1,3},{3,5},{5,7},{7,1},{8,10},{10,12},{12... | collective-permute-start | bytes 393224 | tf_op jit(solution)/shard_map/ppermute | solution.py:434
  52.5 1.6 %collective-permute-start.5 = (bf16[512,128]{1,0:T(8,128)(2,1)S(1)}, bf16[512,128]{1,0:T(8,128)(2,1)S(1)}, u32[]{:S(2)}, u32[]{:S(2)}) collective-permute-start(bf16[512,128]{1,0:T(8,128)(2,1)S(1)} %get-tuple-element.41), channel_id=1, source_target_pairs={{0,4},{2,6},{4,0},{6,2},{1,5},{3,7},{5,1},{7,3},{8,12},{10,14},{12... | collective-permute-start | bytes 393224 | tf_op jit(solution)/shard_map/ppermute | solution.py:434
  54.1 1.6 %collective-permute-start.6 = (bf16[512,128]{1,0:T(8,128)(2,1)S(1)}, bf16[512,128]{1,0:T(8,128)(2,1)S(1)}, u32[]{:S(2)}, u32[]{:S(2)}) collective-permute-start(bf16[512,128]{1,0:T(8,128)(2,1)S(1)} %get-tuple-element.42), channel_id=1, source_target_pairs={{0,6},{2,0},{4,2},{6,4},{1,7},{3,1},{5,3},{7,5},{8,14},{10,8},{12,... | collective-permute-start | bytes 393224 | tf_op jit(solution)/shard_map/ppermute | solution.py:434
  55.6 4.7 %shard_map.81 = (f32[4,128,512]{2,1,0:T(8,128)}, bf16[4,128,8]{2,1,0:T(8,128)(2,1)}) custom-call(bf16[128,4096]{1,0:T(8,128)(2,1)} %bitcast.31, bf16[128,4096]{1,0:T(8,128)(2,1)} %bitcast.14, bf16[128,4096]{1,0:T(8,128)(2,1)} %bitcast.18, f32[32,128]{1,0:T(8,128)} %bitcast.25, s32[1,128]{1,0:T(1,128)} %ids_ref.7), custom_call_target="tpu_custom_call" | custom-call | flops 134217728 | bytes 2621440 | tf_op jit(solution)/shard_map/pallas_call | solution.py:160
  60.4 0.1 pad_add_fusion.4.index
  60.4 0.0 collective-permute-done.4.refs_3_
  60.4 0.0 collective-permute-done.5.refs_4_
  60.5 0.9 copy-done.5
  61.4 0.8 shard_map.82
  62.2 0.1 collective-permute-start.7
  62.3 0.1 pad_add_fusion.1.index
  62.3 0.1 pad_add_fusion.index
  62.4 0.6 shard_map.80.mine_ref
  63.0 1.1 %collective-permute-done.7.other_ref = bf16[4,512,128]{2,1,0:T(8,128)(2,1)S(1)} collective-permute-done((bf16[4,512,128]{2,1,0:T(8,128)(2,1)S(1)}, bf16[4,512,128]{2,1,0:T(8,128)(2,1)S(1)}, u32[]{:S(2)}, u32[]{:S(2)}) %collective-permute-start.7) | collective-permute-done | bytes 524320 | tf_op jit(solution)/shard_map/ppermute | solution.py:440
  64.2 2.9 %shard_map.85 = (bf16[128,512]{1,0:T(8,128)(2,1)S(1)}, bf16[128,512]{1,0:T(8,128)(2,1)S(1)}, bf16[128,512]{1,0:T(8,128)(2,1)S(1)}, bf16[128,512]{1,0:T(8,128)(2,1)S(1)}) custom-call(s32[2]{0:T(128)S(1)} %pad_add_fusion.index, bf16[128,4096]{1,0:T(8,128)(2,1)} %bitcast.32, f32[4,128,512]{2,1,0:T(8,128)} %get-tuple-element.52.intra_ref, ...), custom_call_target="tpu_custom_call" | custom-call | flops 67108864 | bytes 4194304 | tf_op jit(solution)/shard_map/pallas_call | solution.py:360
  67.0 1.6 %collective-permute-start.14 = (bf16[128,512]{1,0:T(8,128)(2,1)S(1)}, bf16[128,512]{1,0:T(8,128)(2,1)S(1)}, u32[]{:S(2)}, u32[]{:S(2)}) collective-permute-start(bf16[128,512]{1,0:T(8,128)(2,1)S(1)} %get-tuple-element.54), channel_id=1, source_target_pairs={{0,64},{64,128},{128,192},{192,0},{1,65},{65,129},{129,193},{193,1... | collective-permute-start | bytes 393224 | tf_op jit(solution)/shard_map/ppermute | solution.py:434
  68.6 2.7 %collective-permute-start.15 = (bf16[128,512]{1,0:T(8,128)(2,1)S(1)}, bf16[128,512]{1,0:T(8,128)(2,1)S(1)}, u32[]{:S(2)}, u32[]{:S(2)}) collective-permute-start(bf16[128,512]{1,0:T(8,128)(2,1)S(1)} %get-tuple-element.55), channel_id=1, source_target_pairs={{0,128},{64,192},{128,0},{192,64},{1,129},{65,193},{129,1},{193,65... | collective-permute-start | bytes 393224 | tf_op jit(solution)/shard_map/ppermute | solution.py:434
  71.3 1.4 %collective-permute-start.16 = (bf16[128,512]{1,0:T(8,128)(2,1)S(1)}, bf16[128,512]{1,0:T(8,128)(2,1)S(1)}, u32[]{:S(2)}, u32[]{:S(2)}) collective-permute-start(bf16[128,512]{1,0:T(8,128)(2,1)S(1)} %get-tuple-element.56), channel_id=1, source_target_pairs={{0,192},{64,0},{128,64},{192,128},{1,193},{65,1},{129,65},{193,129... | collective-permute-start | bytes 393224 | tf_op jit(solution)/shard_map/ppermute | solution.py:434
  72.8 2.9 %shard_map.83 = (bf16[128,512]{1,0:T(8,128)(2,1)S(1)}, bf16[128,512]{1,0:T(8,128)(2,1)S(1)}, bf16[128,512]{1,0:T(8,128)(2,1)S(1)}, bf16[128,512]{1,0:T(8,128)(2,1)S(1)}) custom-call(s32[2]{0:T(128)S(1)} %pad_add_fusion.index, bf16[128,4096]{1,0:T(8,128)(2,1)} %bitcast.33, f32[4,128,512]{2,1,0:T(8,128)} %get-tuple-element.33.intra_ref, ...), custom_call_target="tpu_custom_call" | custom-call | flops 67108864 | bytes 4194304 | tf_op jit(solution)/shard_map/pallas_call | solution.py:360
  75.7 0.7 collective-permute-start.8
  76.3 0.9 collective-permute-start.9
  77.2 1.9 %collective-permute-start.10 = (bf16[128,512]{1,0:T(8,128)(2,1)S(1)}, bf16[128,512]{1,0:T(8,128)(2,1)S(1)}, u32[]{:S(2)}, u32[]{:S(2)}) collective-permute-start(bf16[128,512]{1,0:T(8,128)(2,1)S(1)} %get-tuple-element.47), channel_id=1, source_target_pairs={{0,192},{64,0},{128,64},{192,128},{1,193},{65,1},{129,65},{193,129... | collective-permute-start | bytes 393224 | tf_op jit(solution)/shard_map/ppermute | solution.py:434
  79.1 0.0 collective-permute-done.15.refs_3_
  79.1 0.0 collective-permute-done.16.refs_4_
  79.1 0.8 shard_map.86
  79.9 0.8 collective-permute-start.17
  80.8 2.2 %collective-permute-start.18 = (bf16[128,512]{1,0:T(8,128)(2,1)S(1)}, bf16[128,512]{1,0:T(8,128)(2,1)S(1)}, u32[]{:S(2)}, u32[]{:S(2)}) collective-permute-start(bf16[128,512]{1,0:T(8,128)(2,1)S(1)} %get-tuple-element.59), channel_id=1, source_target_pairs={{0,128},{64,192},{128,0},{192,64},{1,129},{65,193},{129,1},{193,65... | collective-permute-start | bytes 393224 | tf_op jit(solution)/shard_map/ppermute | solution.py:434
  82.9 2.9 %collective-permute-done.8.refs_2_ = bf16[128,512]{1,0:T(8,128)(2,1)S(1)} collective-permute-done((bf16[128,512]{1,0:T(8,128)(2,1)S(1)}, bf16[128,512]{1,0:T(8,128)(2,1)S(1)}, u32[]{:S(2)}, u32[]{:S(2)}) %collective-permute-start.8) | collective-permute-done | bytes 131104 | tf_op jit(solution)/shard_map/ppermute | solution.py:434
  85.8 0.0 collective-permute-start.19
  85.8 0.0 collective-permute-done.9.refs_3_
  85.8 1.2 %collective-permute-done.10.refs_4_ = bf16[128,512]{1,0:T(8,128)(2,1)S(1)} collective-permute-done((bf16[128,512]{1,0:T(8,128)(2,1)S(1)}, bf16[128,512]{1,0:T(8,128)(2,1)S(1)}, u32[]{:S(2)}, u32[]{:S(2)}) %collective-permute-start.10) | collective-permute-done | bytes 131104 | tf_op jit(solution)/shard_map/ppermute | solution.py:434
  87.0 0.8 shard_map.84
  87.8 0.9 collective-permute-start.11
  88.7 3.2 %collective-permute-start.12 = (bf16[128,512]{1,0:T(8,128)(2,1)S(1)}, bf16[128,512]{1,0:T(8,128)(2,1)S(1)}, u32[]{:S(2)}, u32[]{:S(2)}) collective-permute-start(bf16[128,512]{1,0:T(8,128)(2,1)S(1)} %get-tuple-element.50), channel_id=1, source_target_pairs={{0,128},{64,192},{128,0},{192,64},{1,129},{65,193},{129,1},{193,65... | collective-permute-start | bytes 393224 | tf_op jit(solution)/shard_map/ppermute | solution.py:434
  91.9 0.0 collective-permute-done.17.refs_5_
  91.9 0.0 collective-permute-start.13
  91.9 0.0 collective-permute-done.18.refs_6_
  91.9 3.3 %collective-permute-done.11.refs_1_ = bf16[128,512]{1,0:T(8,128)(2,1)S(1)} collective-permute-done((bf16[128,512]{1,0:T(8,128)(2,1)S(1)}, bf16[128,512]{1,0:T(8,128)(2,1)S(1)}, u32[]{:S(2)}, u32[]{:S(2)}) %collective-permute-start.11) | collective-permute-done | bytes 131104 | tf_op jit(solution)/shard_map/ppermute | solution.py:434
  95.2 1.4 %collective-permute-done.12.refs_2_ = bf16[128,512]{1,0:T(8,128)(2,1)S(1)} collective-permute-done((bf16[128,512]{1,0:T(8,128)(2,1)S(1)}, bf16[128,512]{1,0:T(8,128)(2,1)S(1)}, u32[]{:S(2)}, u32[]{:S(2)}) %collective-permute-start.12) | collective-permute-done | bytes 131104 | tf_op jit(solution)/shard_map/ppermute | solution.py:434
  96.6 0.2 collective-permute-done.13.refs_3_
  96.9 1.6 %shard_map.87 = bf16[128,4096]{1,0:T(8,128)(2,1)} custom-call(s32[2]{0:T(128)S(1)} %pad_add_fusion.index, bf16[128,512]{1,0:T(8,128)(2,1)S(1)} %get-tuple-element.48.refs_0_, bf16[128,512]{1,0:T(8,128)(2,1)S(1)} %collective-permute-done.11.refs_1_, bf16[128,512]{1,0:T(8,128)(2,1)S(1)} %collective-permute-done.12.refs_2_, ...), custom_call_target="tpu_custom_call" | custom-call | bytes 2097152 | tf_op jit(solution)/shard_map/pallas_call | solution.py:416
  (23 shorter events, 0.0 us)
Async XLA Ops:
  0.0 0.7 copy-start.12
  0.7 1.2 %copy-start = (bf16[1,1,128,4096]{3,2,1,0:T(8,128)(2,1)S(1)}, bf16[1,1,128,4096]{3,2,1,0:T(8,128)(2,1)}, u32[]{:S(2)}) copy-start(bf16[1,1,128,4096]{3,2,1,0:T(8,128)(2,1)} %param.9) | copy-start | bytes 3145732
  1.9 1.2 %copy-start.2 = (bf16[1,1,128,4096]{3,2,1,0:T(8,128)(2,1)S(1)}, bf16[1,1,128,4096]{3,2,1,0:T(8,128)(2,1)}, u32[]{:S(2)}) copy-start(bf16[1,1,128,4096]{3,2,1,0:T(8,128)(2,1)} %param.10) | copy-start | bytes 3145732
  3.1 0.7 copy-start.9
  3.8 1.3 %copy-start.1 = (bf16[1,1,128,4096]{3,2,1,0:T(8,128)(2,1)S(1)}, bf16[1,1,128,4096]{3,2,1,0:T(8,128)(2,1)}, u32[]{:S(2)}) copy-start(bf16[1,1,128,4096]{3,2,1,0:T(8,128)(2,1)} %param.9) | copy-start | bytes 3145732
  3.8 1.7 %copy-start.3 = (bf16[1,1,128,4096]{3,2,1,0:T(8,128)(2,1)S(1)}, bf16[1,1,128,4096]{3,2,1,0:T(8,128)(2,1)}, u32[]{:S(2)}) copy-start(bf16[1,1,128,4096]{3,2,1,0:T(8,128)(2,1)} %param.10) | copy-start | bytes 3145732
  3.8 1.7 %copy-start.10 = (f32[1,1,32,128]{3,2,1,0:T(8,128)S(1)}, f32[1,1,32,128]{3,2,1,0:T(8,128)}, u32[]{:S(2)}) copy-start(f32[1,1,32,128]{3,2,1,0:T(8,128)} %param.12) | copy-start | bytes 49156
  5.1 2.2 %collective-permute-start = (bf16[4,544,128]{2,1,0:T(8,128)(2,1)}, bf16[4,544,128]{2,1,0:T(8,128)(2,1)S(1)}, u32[]{:S(2)}, u32[]{:S(2)}) collective-permute-start(bf16[4,544,128]{2,1,0:T(8,128)(2,1)} %shard_map.75), channel_id=1, source_target_pairs={{0,1},{1,0},{2,3},{3,2},{4,5},{5,4},{6,7},{7,6},{8,9},{9,8},{10,11... | collective-permute-start | bytes 1671176 | tf_op jit(solution)/shard_map/ppermute | solution.py:440
  8.1 9.7 %collective-permute-start.1 = (bf16[544,128]{1,0:T(8,128)(2,1)S(1)}, bf16[544,128]{1,0:T(8,128)(2,1)S(1)}, u32[]{:S(2)}, u32[]{:S(2)}) collective-permute-start(bf16[544,128]{1,0:T(8,128)(2,1)S(1)} %get-tuple-element.35), channel_id=1, source_target_pairs={{0,2},{2,4},{4,6},{6,0},{1,3},{3,5},{5,7},{7,1},{8,10},{10,12},{12... | collective-permute-start | bytes 417800 | tf_op jit(solution)/shard_map/ppermute | solution.py:434
  9.7 8.1 %collective-permute-start.2 = (bf16[544,128]{1,0:T(8,128)(2,1)S(1)}, bf16[544,128]{1,0:T(8,128)(2,1)S(1)}, u32[]{:S(2)}, u32[]{:S(2)}) collective-permute-start(bf16[544,128]{1,0:T(8,128)(2,1)S(1)} %get-tuple-element.36), channel_id=1, source_target_pairs={{0,4},{2,6},{4,0},{6,2},{1,5},{3,7},{5,1},{7,3},{8,12},{10,14},{12... | collective-permute-start | bytes 417800 | tf_op jit(solution)/shard_map/ppermute | solution.py:434
  12.4 7.2 %collective-permute-start.3 = (bf16[544,128]{1,0:T(8,128)(2,1)S(1)}, bf16[544,128]{1,0:T(8,128)(2,1)S(1)}, u32[]{:S(2)}, u32[]{:S(2)}) collective-permute-start(bf16[544,128]{1,0:T(8,128)(2,1)S(1)} %get-tuple-element.37), channel_id=1, source_target_pairs={{0,6},{2,0},{4,2},{6,4},{1,7},{3,1},{5,3},{7,5},{8,14},{10,8},{12,... | collective-permute-start | bytes 417800 | tf_op jit(solution)/shard_map/ppermute | solution.py:434
  19.7 0.9 copy-start.7
  51.1 9.3 %collective-permute-start.4 = (bf16[512,128]{1,0:T(8,128)(2,1)S(1)}, bf16[512,128]{1,0:T(8,128)(2,1)S(1)}, u32[]{:S(2)}, u32[]{:S(2)}) collective-permute-start(bf16[512,128]{1,0:T(8,128)(2,1)S(1)} %get-tuple-element.40), channel_id=1, source_target_pairs={{0,2},{2,4},{4,6},{6,0},{1,3},{3,5},{5,7},{7,1},{8,10},{10,12},{12... | collective-permute-start | bytes 393224 | tf_op jit(solution)/shard_map/ppermute | solution.py:434
  52.5 7.9 %collective-permute-start.5 = (bf16[512,128]{1,0:T(8,128)(2,1)S(1)}, bf16[512,128]{1,0:T(8,128)(2,1)S(1)}, u32[]{:S(2)}, u32[]{:S(2)}) collective-permute-start(bf16[512,128]{1,0:T(8,128)(2,1)S(1)} %get-tuple-element.41), channel_id=1, source_target_pairs={{0,4},{2,6},{4,0},{6,2},{1,5},{3,7},{5,1},{7,3},{8,12},{10,14},{12... | collective-permute-start | bytes 393224 | tf_op jit(solution)/shard_map/ppermute | solution.py:434
  54.1 6.4 %collective-permute-start.6 = (bf16[512,128]{1,0:T(8,128)(2,1)S(1)}, bf16[512,128]{1,0:T(8,128)(2,1)S(1)}, u32[]{:S(2)}, u32[]{:S(2)}) collective-permute-start(bf16[512,128]{1,0:T(8,128)(2,1)S(1)} %get-tuple-element.42), channel_id=1, source_target_pairs={{0,6},{2,0},{4,2},{6,4},{1,7},{3,1},{5,3},{7,5},{8,14},{10,8},{12,... | collective-permute-start | bytes 393224 | tf_op jit(solution)/shard_map/ppermute | solution.py:434
  60.4 0.9 copy-start.5
  62.2 2.0 %collective-permute-start.7 = (bf16[4,512,128]{2,1,0:T(8,128)(2,1)S(1)}, bf16[4,512,128]{2,1,0:T(8,128)(2,1)S(1)}, u32[]{:S(2)}, u32[]{:S(2)}) collective-permute-start(bf16[4,512,128]{2,1,0:T(8,128)(2,1)S(1)} %shard_map.82), channel_id=1, source_target_pairs={{0,1},{1,0},{2,3},{3,2},{4,5},{5,4},{6,7},{7,6},{8,9},{9,8},{10,11... | collective-permute-start | bytes 1572872 | tf_op jit(solution)/shard_map/ppermute | solution.py:440
  62.4 1.7 %copy-start.6 = (bf16[4,128,8]{2,1,0:T(8,128)(2,1)S(1)}, bf16[4,128,8]{2,1,0:T(8,128)(2,1)}, u32[]{:S(2)}) copy-start(bf16[4,128,8]{2,1,0:T(8,128)(2,1)} %get-tuple-element.43.refs_6_.factor_ref) | copy-start | bytes 24580
  62.4 1.7 %copy-start.11 = (bf16[1,4096]{1,0:T(2,128)(2,1)S(1)}, bf16[1,4096]{1,0:T(2,128)(2,1)}, u32[]{:S(2)}) copy-start(bf16[1,4096]{1,0:T(2,128)(2,1)} %param.11) | copy-start | bytes 24580
  64.2 8.6 %copy-start.8 = (bf16[4,128,8]{2,1,0:T(8,128)(2,1)S(1)}, bf16[4,128,8]{2,1,0:T(8,128)(2,1)}, u32[]{:S(2)}) copy-start(bf16[4,128,8]{2,1,0:T(8,128)(2,1)} %get-tuple-element.38.refs_4_.factor_ref) | copy-start | bytes 24580
  67.0 10.2 %collective-permute-start.14 = (bf16[128,512]{1,0:T(8,128)(2,1)S(1)}, bf16[128,512]{1,0:T(8,128)(2,1)S(1)}, u32[]{:S(2)}, u32[]{:S(2)}) collective-permute-start(bf16[128,512]{1,0:T(8,128)(2,1)S(1)} %get-tuple-element.54), channel_id=1, source_target_pairs={{0,64},{64,128},{128,192},{192,0},{1,65},{65,129},{129,193},{193,1... | collective-permute-start | bytes 393224 | tf_op jit(solution)/shard_map/ppermute | solution.py:434
  68.6 10.5 %collective-permute-start.15 = (bf16[128,512]{1,0:T(8,128)(2,1)S(1)}, bf16[128,512]{1,0:T(8,128)(2,1)S(1)}, u32[]{:S(2)}, u32[]{:S(2)}) collective-permute-start(bf16[128,512]{1,0:T(8,128)(2,1)S(1)} %get-tuple-element.55), channel_id=1, source_target_pairs={{0,128},{64,192},{128,0},{192,64},{1,129},{65,193},{129,1},{193,65... | collective-permute-start | bytes 393224 | tf_op jit(solution)/shard_map/ppermute | solution.py:434
  71.3 7.8 %collective-permute-start.16 = (bf16[128,512]{1,0:T(8,128)(2,1)S(1)}, bf16[128,512]{1,0:T(8,128)(2,1)S(1)}, u32[]{:S(2)}, u32[]{:S(2)}) collective-permute-start(bf16[128,512]{1,0:T(8,128)(2,1)S(1)} %get-tuple-element.56), channel_id=1, source_target_pairs={{0,192},{64,0},{128,64},{192,128},{1,193},{65,1},{129,65},{193,129... | collective-permute-start | bytes 393224 | tf_op jit(solution)/shard_map/ppermute | solution.py:434
  72.8 6.3 %copy-start.4 = (bf16[1,128,1024]{2,1,0:T(8,128)(2,1)S(1)}, bf16[1,128,1024]{2,1,0:T(8,128)(2,1)}, u32[]{:S(2)}) copy-start(bf16[1,128,1024]{2,1,0:T(8,128)(2,1)} %param.7) | copy-start | bytes 786436
  75.7 10.1 %collective-permute-start.8 = (bf16[128,512]{1,0:T(8,128)(2,1)S(1)}, bf16[128,512]{1,0:T(8,128)(2,1)S(1)}, u32[]{:S(2)}, u32[]{:S(2)}) collective-permute-start(bf16[128,512]{1,0:T(8,128)(2,1)S(1)} %get-tuple-element.45), channel_id=1, source_target_pairs={{0,64},{64,128},{128,192},{192,0},{1,65},{65,129},{129,193},{193,1... | collective-permute-start | bytes 393224 | tf_op jit(solution)/shard_map/ppermute | solution.py:434
  76.3 9.5 %collective-permute-start.9 = (bf16[128,512]{1,0:T(8,128)(2,1)S(1)}, bf16[128,512]{1,0:T(8,128)(2,1)S(1)}, u32[]{:S(2)}, u32[]{:S(2)}) collective-permute-start(bf16[128,512]{1,0:T(8,128)(2,1)S(1)} %get-tuple-element.46), channel_id=1, source_target_pairs={{0,128},{64,192},{128,0},{192,64},{1,129},{65,193},{129,1},{193,65... | collective-permute-start | bytes 393224 | tf_op jit(solution)/shard_map/ppermute | solution.py:434
  77.2 9.8 %collective-permute-start.10 = (bf16[128,512]{1,0:T(8,128)(2,1)S(1)}, bf16[128,512]{1,0:T(8,128)(2,1)S(1)}, u32[]{:S(2)}, u32[]{:S(2)}) collective-permute-start(bf16[128,512]{1,0:T(8,128)(2,1)S(1)} %get-tuple-element.47), channel_id=1, source_target_pairs={{0,192},{64,0},{128,64},{192,128},{1,193},{65,1},{129,65},{193,129... | collective-permute-start | bytes 393224 | tf_op jit(solution)/shard_map/ppermute | solution.py:434
  79.9 12.0 %collective-permute-start.17 = (bf16[128,512]{1,0:T(8,128)(2,1)S(1)}, bf16[128,512]{1,0:T(8,128)(2,1)S(1)}, u32[]{:S(2)}, u32[]{:S(2)}) collective-permute-start(bf16[128,512]{1,0:T(8,128)(2,1)S(1)} %get-tuple-element.58), channel_id=1, source_target_pairs={{0,64},{64,128},{128,192},{192,0},{1,65},{65,129},{129,193},{193,1... | collective-permute-start | bytes 393224 | tf_op jit(solution)/shard_map/ppermute | solution.py:434
  80.8 11.2 %collective-permute-start.18 = (bf16[128,512]{1,0:T(8,128)(2,1)S(1)}, bf16[128,512]{1,0:T(8,128)(2,1)S(1)}, u32[]{:S(2)}, u32[]{:S(2)}) collective-permute-start(bf16[128,512]{1,0:T(8,128)(2,1)S(1)} %get-tuple-element.59), channel_id=1, source_target_pairs={{0,128},{64,192},{128,0},{192,64},{1,129},{65,193},{129,1},{193,65... | collective-permute-start | bytes 393224 | tf_op jit(solution)/shard_map/ppermute | solution.py:434
  85.8 6.1 %collective-permute-start.19 = (bf16[128,512]{1,0:T(8,128)(2,1)S(1)}, bf16[128,512]{1,0:T(8,128)(2,1)S(1)}, u32[]{:S(2)}, u32[]{:S(2)}) collective-permute-start(bf16[128,512]{1,0:T(8,128)(2,1)S(1)} %get-tuple-element.60), channel_id=1, source_target_pairs={{0,192},{64,0},{128,64},{192,128},{1,193},{65,1},{129,65},{193,129... | collective-permute-start | bytes 393224 | tf_op jit(solution)/shard_map/ppermute | solution.py:434
  87.8 7.5 %collective-permute-start.11 = (bf16[128,512]{1,0:T(8,128)(2,1)S(1)}, bf16[128,512]{1,0:T(8,128)(2,1)S(1)}, u32[]{:S(2)}, u32[]{:S(2)}) collective-permute-start(bf16[128,512]{1,0:T(8,128)(2,1)S(1)} %get-tuple-element.49), channel_id=1, source_target_pairs={{0,64},{64,128},{128,192},{192,0},{1,65},{65,129},{129,193},{193,1... | collective-permute-start | bytes 393224 | tf_op jit(solution)/shard_map/ppermute | solution.py:434
  88.7 7.9 %collective-permute-start.12 = (bf16[128,512]{1,0:T(8,128)(2,1)S(1)}, bf16[128,512]{1,0:T(8,128)(2,1)S(1)}, u32[]{:S(2)}, u32[]{:S(2)}) collective-permute-start(bf16[128,512]{1,0:T(8,128)(2,1)S(1)} %get-tuple-element.50), channel_id=1, source_target_pairs={{0,128},{64,192},{128,0},{192,64},{1,129},{65,193},{129,1},{193,65... | collective-permute-start | bytes 393224 | tf_op jit(solution)/shard_map/ppermute | solution.py:434
  91.9 5.0 %collective-permute-start.13 = (bf16[128,512]{1,0:T(8,128)(2,1)S(1)}, bf16[128,512]{1,0:T(8,128)(2,1)S(1)}, u32[]{:S(2)}, u32[]{:S(2)}) collective-permute-start(bf16[128,512]{1,0:T(8,128)(2,1)S(1)} %get-tuple-element.51), channel_id=1, source_target_pairs={{0,192},{64,0},{128,64},{192,128},{1,193},{65,1},{129,65},{193,129... | collective-permute-start | bytes 393224 | tf_op jit(solution)/shard_map/ppermute | solution.py:434

commit v3 on v2

--- a/solution.py
+++ b/solution.py
@@ -18,9 +18,8 @@
 META = 32
 ROWS = GROUP * D
 PART = ROWS + META
+PHASE, Y, CORE = 0, 1, 2
 VMEM_LIMIT = 16 * 1024 * 1024
-ATTEND_LIMIT = 52 * 1024 * 1024
-INTRA_LIMIT = 60 * 1024 * 1024
 
 
 def nt(a, b):
@@ -66,17 +65,19 @@
     return (a == b).astype(F32)
 
 
-def summarise(ids, decay, head_rows, out_ref, cut_ref):
+def summary_kernel(of_other, index, k_ref, v_ref, decay_ref, ids_ref, out_ref, cut_ref):
+    half = 1 - index[CORE] if of_other else index[CORE]
+    ids = ids_ref[...].astype(F32)
     first, last = ids[:, 0:1], ids[:, D - 1 : D]
+    decay = decay_ref[pl.ds(pl.multiple_of(half * HALF, HALF), HALF), :]
     total = nt(three_parts(decay), jnp.ones((D, 3 * D), BF16))
     carried = jnp.exp(total - running_sums(decay)) * same(ids, last)
     for group in range(4):
-        keys, values = head_rows(group)
         for i in range(GROUP):
             h = group * GROUP + i
-            lanes = slice(i * D, (i + 1) * D)
-            keyed = (jnp.transpose(keys[:, lanes].astype(F32)) * carried[h : h + 1]).astype(BF16)
-            state = jnp.dot(keyed, values[:, lanes], preferred_element_type=F32)
+            lanes = slice(h * D, (h + 1) * D)
+            keyed = (jnp.transpose(k_ref[:, lanes].astype(F32)) * carried[h : h + 1]).astype(BF16)
+            state = jnp.dot(keyed, v_ref[:, lanes], preferred_element_type=F32)
             out_ref[group, i * D : (i + 1) * D, :] = state.astype(BF16)
         cut_ref[0:GROUP, :] = total[group * GROUP : (group + 1) * GROUP, :]
         cut_ref[GROUP:8, :] = jnp.zeros((8 - GROUP, D), F32)
@@ -85,39 +86,22 @@
         )
 
 
-def summary_kernel(index, k_ref, v_ref, decay_ref, ids_ref, out_ref, cut_ref):
-    decay = decay_ref[pl.ds(pl.multiple_of(index[0] * HALF, HALF), HALF), :]
-
-    def head_rows(group):
-        lanes = slice(group * ROWS, (group + 1) * ROWS)
-        return k_ref[:, lanes], v_ref[:, lanes]
-
-    summarise(ids_ref[...].astype(F32), decay, head_rows, out_ref, cut_ref)
-
-
-SUMMARY_COST = pl.CostEstimate(flops=2 * HALF * D**3, bytes_accessed=3 * HALF * D * D * 2, transcendentals=0)
-
-
-def summaries(half, keys, values, decay, ids):
+def summaries(of_other, index, keys, values, decay, ids):
     whole = lambda shape: pl.BlockSpec(shape, lambda i, s: (0,) * len(shape))
+    block = pl.BlockSpec((D, HALF * D), lambda i, s: (0, 1 - s[CORE] if of_other else s[CORE]))
     return pl.pallas_call(
-        summary_kernel,
+        functools.partial(summary_kernel, of_other),
         out_shape=jax.ShapeDtypeStruct((4, PART, D), BF16),
         grid_spec=pltpu.PrefetchScalarGridSpec(
             num_scalar_prefetch=1,
             grid=(1,),
-            in_specs=[
-                pl.BlockSpec((D, HALF * D), lambda i, s: (0, s[0])),
-                pl.BlockSpec((D, HALF * D), lambda i, s: (0, s[0])),
-                whole((HEADS, D)),
-                whole((1, D)),
-            ],
+            in_specs=[block, block, whole((HEADS, D)), whole((1, D))],
             out_specs=whole((4, PART, D)),
             scratch_shapes=[pltpu.VMEM((8, D), F32)],
         ),
         compiler_params=pltpu.CompilerParams(vmem_limit_bytes=VMEM_LIMIT),
-        cost_estimate=SUMMARY_COST,
-    )(half, keys, values, decay, ids)
+        cost_estimate=pl.CostEstimate(flops=HEADS * D**3, bytes_accessed=3 * HALF * D * D * 2, transcendentals=0),
+    )(index, keys, values, decay, ids)
 
 
 def two_parts(x):
@@ -125,7 +109,9 @@
     return hi, (x - hi.astype(F32)).astype(BF16)
 
 
-def intra_kernel(wave, q_ref, k_ref, v_ref, decay_ref, ids_ref, out_ref, factor_ref, column_ref, row_ref, allowed_ref):
+def intra_kernel(
+    wave, q_ref, k_ref, v_ref, decay_ref, ids_ref, out_ref, factor_ref, column_ref, row_ref, allowed_ref
+):
     step = pl.program_id(0)
 
     @pl.when(step == 0)
@@ -173,7 +159,7 @@
             pl.BlockSpec((4, D, 2 * GROUP), lambda i: (0, 0, 0)),
         ],
         scratch_shapes=[pltpu.VMEM((4, D, 8), F32), pltpu.VMEM((D, D), F32), pltpu.VMEM((D, D), F32)],
-        compiler_params=pltpu.CompilerParams(vmem_limit_bytes=INTRA_LIMIT),
+        compiler_params=pltpu.CompilerParams(vmem_limit_bytes=VMEM_LIMIT),
         cost_estimate=pl.CostEstimate(
             flops=2 * HEADS * D**3, bytes_accessed=5 * HALF * D * D * 2, transcendentals=HALF * D * D
         ),
@@ -181,7 +167,7 @@
 
 
 def chip_kernel(index, own_ref, other_ref, *out_refs):
-    y, core = index[0], index[1]
+    y, core = index[Y], index[CORE]
     is_one = core == 1
     for step in range(4):
         group = lax.rem(y + step, 4)
@@ -235,7 +221,7 @@
 
 def row_kernel(index, *refs):
     *slots, out_ref, ordered_ref = refs
-    in_order(index[0], slots, ordered_ref)
+    in_order(index[Y], slots, ordered_ref)
     metas = [unpack_meta(ordered_ref[c, ROWS:PART, :]) for c in range(4)]
     weights, after = [None] * 4, jnp.zeros((8, D), F32)
     for c in (3, 2, 1, 0):
@@ -270,7 +256,7 @@
 
 def spread_kernel(index, state_ref, *refs):
     *slots, out0, out1, out2, out3, ordered_ref, result_ref = refs
-    y = index[0]
+    y = index[Y]
     in_order(y, slots, ordered_ref)
     metas = [unpack_meta(ordered_ref[c, ROWS:PART, :]) for c in range(4)]
     passing = [jnp.exp(decay) * same(first, last) for decay, first, last in metas]
@@ -287,9 +273,10 @@
         out_ref[...] = result_ref[lax.rem(y + step, 4)]
 
 
-def core_kernel(index, own_ref, other_ref, s0, s1, s2, s3, out_ref):
-    y, core, target = index[0], index[1], index[2]
+def core_kernel(of_other, index, own_ref, other_ref, s0, s1, s2, s3, out_ref):
+    y, core = index[Y], index[CORE]
     is_one = core == 1
+    target = 1 - core if of_other else core
 
     @pl.when(target == 0)
     def _():
@@ -315,79 +302,35 @@
                 out_ref[group, rows, :] = later.astype(BF16)
 
 
-def attend_kernel(
-    wave, index, q_ref, intra_ref, mine_ref, other_ref, factor_ref, gain_ref, *refs
-):
-    *out_refs, queries, intra, sem = refs
-    copies = []
-    for step in range(4):
-        quarter = lax.rem(index[0] + step, 4)
-        lanes = pl.ds(pl.multiple_of((2 * quarter + wave) * ROWS, ROWS), ROWS)
-        copies.append(
-            [
-                pltpu.make_async_copy(q_ref.at[:, lanes], queries.at[step], sem.at[0, step]),
-                pltpu.make_async_copy(intra_ref.at[quarter], intra.at[step], sem.at[1, step]),
-            ]
-        )
-    for pair in copies:
-        for copy in pair:
-            copy.start()
+def attend_kernel(wave, index, q_ref, intra_ref, factor_ref, mine_ref, other_ref, gain_ref, *out_refs):
     shape = (2 * GROUP, ROWS)
     spreading = (lax.rem(iota(shape, 0), GROUP) == iota(shape, 1) // D).astype(F32).astype(BF16)
     for step in range(4):
-        quarter = lax.rem(index[0] + step, 4)
+        quarter = lax.rem(index[PHASE] + step, 4)
         group = 2 * quarter + wave
-        use_mine = (quarter // 2) == index[1]
+        at = lax.rem(group, 4)
+        use_mine = (quarter // 2) == index[CORE]
         factors = jnp.dot(factor_ref[quarter], spreading, preferred_element_type=F32)
         gain = gain_ref[group]
-        for copy in copies[step]:
-            copy.wait()
         for i in range(GROUP):
             lanes = slice(i * D, (i + 1) * D)
-            at = lax.rem(group, 4)
             state = jnp.where(use_mine, mine_ref[at, lanes, :], other_ref[at, lanes, :])
-            inter = jnp.dot(queries[step, :, lanes], state, preferred_element_type=F32)
-            total = intra[step, :, lanes] + inter * factors[:, lanes]
+            queries = q_ref[:, pl.ds(pl.multiple_of(group * ROWS + i * D, D), D)]
+            inter = jnp.dot(queries, state, preferred_element_type=F32)
+            total = intra_ref[quarter, :, lanes] + inter * factors[:, lanes]
             power = jnp.mean(total * total, axis=1, keepdims=True)
             out_refs[step][:, lanes] = (
                 total * lax.rsqrt(power + EPSILON) * gain[:, lanes].astype(F32)
             ).astype(BF16)
 
 
-def attend(wave, index, queries, intra, factors, mine, other, gain):
-    whole = lambda shape: pl.BlockSpec(shape, lambda i, s: (0,) * len(shape))
-    anywhere = pl.BlockSpec(memory_space=pl.ANY)
-    return pl.pallas_call(
-        functools.partial(attend_kernel, wave),
-        out_shape=[jax.ShapeDtypeStruct((D, ROWS), BF16)] * 4,
-        grid_spec=pltpu.PrefetchScalarGridSpec(
-            num_scalar_prefetch=1,
-            grid=(1,),
-            in_specs=[
-                anywhere,
-                anywhere,
-                whole(mine.shape),
-                whole(other.shape),
-                whole(factors.shape),
-                whole(gain.shape),
-            ],
-            out_specs=[whole((D, ROWS))] * 4,
-            scratch_shapes=[
-                pltpu.VMEM((4, D, ROWS), BF16),
-                pltpu.VMEM((4, D, ROWS), F32),
-                pltpu.SemaphoreType.DMA((2, 4)),
-            ],
-        ),
-        compiler_params=pltpu.CompilerParams(vmem_limit_bytes=ATTEND_LIMIT),
-        cost_estimate=pl.CostEstimate(
-            flops=HEADS * D**3, bytes_accessed=4 * HEADS * D * D * 2, transcendentals=HEADS * D
-        ),
-    )(index, queries, intra, mine, other, factors, gain)
+def attend(wave, index, *operands):
+    return small_call(functools.partial(attend_kernel, wave), index, operands, [((D, ROWS), BF16)] * 4)
 
 
 def layers_kernel(wave, index, tokens_ref, *refs):
     *slots, out0, out1, out2, out3, ordered_ref = refs
-    phase = index[0]
+    phase = index[PHASE]
     in_order(phase, slots, ordered_ref)
     current = tokens_ref[:, wave * ROWS : (wave + 1) * ROWS].astype(F32)
     for s in range(4):
@@ -398,34 +341,35 @@
         out_ref[...] = ordered_ref[lax.rem(phase + step, 4)]
 
 
-def place_kernel(index, *refs):
-    *slots, out_ref, sem = refs
+def place_kernel(wave, index, *refs):
+    slots, out_ref, sem = refs[:4], refs[-2], refs[-1]
     copies = []
-    for n, slot in enumerate(slots):
-        wave, step = n // 4, n % 4
-        quarter = lax.rem(index[0] + 4 - step, 4)
+    for step, slot in enumerate(slots):
+        quarter = lax.rem(index[PHASE] + 4 - step, 4)
         lanes = pl.ds(pl.multiple_of((2 * quarter + wave) * ROWS, ROWS), ROWS)
-        copies.append(pltpu.make_async_copy(slot, out_ref.at[:, lanes], sem.at[n]))
+        copies.append(pltpu.make_async_copy(slot, out_ref.at[:, lanes], sem.at[step]))
     for copy in copies:
         copy.start()
     for copy in copies:
         copy.wait()
 
 
-def place(index, slots):
+def place(wave, index, slots, out=None):
+    given = [] if out is None else [out]
     return pl.pallas_call(
-        place_kernel,
+        functools.partial(place_kernel, wave),
         out_shape=jax.ShapeDtypeStruct((D, HEADS * D), BF16),
         grid_spec=pltpu.PrefetchScalarGridSpec(
             num_scalar_prefetch=1,
             grid=(1,),
-            in_specs=[pl.BlockSpec(memory_space=pl.ANY)] * 8,
+            in_specs=[pl.BlockSpec(memory_space=pl.ANY)] * (4 + len(given)),
             out_specs=pl.BlockSpec(memory_space=pl.ANY),
-            scratch_shapes=[pltpu.SemaphoreType.DMA((8,))],
+            scratch_shapes=[pltpu.SemaphoreType.DMA((4,))],
         ),
+        input_output_aliases={5: 0} if given else {},
         compiler_params=pltpu.CompilerParams(vmem_limit_bytes=VMEM_LIMIT),
-        cost_estimate=pl.CostEstimate(flops=0, bytes_accessed=4 * HEADS * D * D, transcendentals=0),
-    )(index, *slots)
+        cost_estimate=pl.CostEstimate(flops=0, bytes_accessed=2 * HEADS * D * D, transcendentals=0),
+    )(index, *slots, *given)
 
 
 def ring_exchange(slots, axis):
@@ -441,52 +385,49 @@
 
 
 def local(tokens, queries, keys_in, values, norm_gain, log_decay, doc_ids):
-    phase, z, y, core = (lax.axis_index(name) for name in ("phase", "z", "y", "core"))
+    index = jnp.stack([lax.axis_index(name) for name in ("phase", "y", "core")]).astype(jnp.int32)
     queries, keys, values, decay = queries[0, 0], keys_in[0, 0], values[0, 0], log_decay[0, 0]
-    here = jnp.stack([y, core, z]).astype(jnp.int32)
-
-    sending = summaries(jnp.stack([1 - core]), keys, values, decay, doc_ids)
-    other = swap_cores(sending)
-    own = summaries(jnp.stack([core]), keys, values, decay, doc_ids)
-
-    part = ((PART, D), BF16)
-    slots = ring_exchange(small_call(chip_kernel, here, [own, other], [part] * 4), "y")
+    gain = norm_gain.reshape(8, 1, ROWS)
+
+    other = swap_cores(summaries(True, index, keys, values, decay, doc_ids))
+    own = summaries(False, index, keys, values, decay, doc_ids)
+
+    part, group_states = ((PART, D), BF16), ((ROWS, D), BF16)
+    slots = ring_exchange(small_call(chip_kernel, index, [own, other], [part] * 4), "y")
     intra = [intra_term(wave, queries, keys, values, decay, doc_ids) for wave in range(2)]
 
     (parts,) = small_call(
-        row_kernel, here, slots, [((NZ, D // 2 + 16, D), BF16)], [pltpu.VMEM((4, PART, D), BF16)], intra[0][1:]
+        row_kernel, index, slots, [((NZ, D // 2 + 16, D), BF16)], [pltpu.VMEM((4, PART, D), BF16)], intra[0][:1]
     )
     parts = lax.all_to_all(parts, "z", split_axis=0, concat_axis=0, tiled=True)
-    (states,) = small_call(scan_kernel, here, [parts], [((NZ, D // 2, D), BF16)])
+    (states,) = small_call(scan_kernel, index, [parts], [((NZ, D // 2, D), BF16)])
     states = lax.all_to_all(states, "z", split_axis=0, concat_axis=0, tiled=True)
     spread = small_call(
         spread_kernel,
-        here,
+        index,
         [states.reshape(ROWS, D), *slots],
-        [((ROWS, D), BF16)] * 4,
+        [group_states] * 4,
         [pltpu.VMEM((4, PART, D), BF16), pltpu.VMEM((4, ROWS, D), BF16)],
     )
     spread = ring_exchange(spread, "y")
-    out = [((4, ROWS, D), BF16)]
-    to_other = jnp.stack([y, core, 1 - core]).astype(jnp.int32)
-    (send,) = small_call(core_kernel, to_other, [own, other, *spread], out, after=intra[1][1:])
-    theirs = swap_cores(send)
-    (mine,) = small_call(core_kernel, jnp.stack([y, core, core]).astype(jnp.int32), [own, other, *spread], out)
-
-    at = jnp.stack([phase, core]).astype(jnp.int32)
-    gain = norm_gain.reshape(8, 1, ROWS)
-    pieces = []
+    for_core = lambda of_other, after: small_call(
+        functools.partial(core_kernel, of_other), index, [own, other, *spread], [((4, ROWS, D), BF16)], after=after
+    )[0]
+    theirs = swap_cores(for_core(True, intra[1][:1]))
+    mine = for_core(False, ())
+
+    result = None
     for wave in range(2):
-        normed = ring_exchange(attend(wave, at, queries, *intra[wave], mine, theirs, gain), "phase")
+        normed = ring_exchange(attend(wave, index, queries, *intra[wave], mine, theirs, gain), "phase")
         sums = small_call(
             functools.partial(layers_kernel, wave),
-            at,
+            index,
             [tokens[0], *normed],
             [((D, ROWS), BF16)] * 4,
             [pltpu.VMEM((4, D, ROWS), BF16)],
         )
-        pieces += ring_exchange(sums, "phase")
-    return place(at, pieces)[None, None]
+        result = place(wave, index, ring_exchange(sums, "phase"), result)
+    return result[None, None]
 
 
 def solution(mesh):

time: 99.9 us -> 92.2 us (0.923)
  Pallas kernels: 24.4 us -> 17.6 us
  starting transfers between devices: 25.9 us -> 28.9 us
  local copies, waits for them, and re-layouts: 6.08 us -> 3.14 us
    pallas_call x2, Pallas kernels: 9.45 us -> 4.45 us  [intra_term(): pl.pallas_call(functools.partial(intra_kernel, wave), out_shape=[jax.Shap...]
    pallas_call x5 -> x4, Pallas kernels: 9.12 us -> 4.84 us  [the longest x2 2.73 us: place(): pl.pallas_call(functools.partial(place_kernel, wave), out_shape=jax.Shape...]
    ppermute x18, starting transfers between devices: 25.8 us -> 28.8 us  [ring_exchange(): lax.ppermute(slots[d], axis, [(i, (i + d) % size) for i in range(size)])]
    unnamed x26 -> x18, local copies, waits for them, and re-layouts: 6.08 us -> 3.14 us
    pallas_call x8 -> x10, Pallas kernels: 5.82 us -> 8.27 us  [small_call(): pl.pallas_call(body, out_shape=[jax.ShapeDtypeStruct(shape, dtype) for sh...]
  transfers between devices with their start and end apart: 20 -> 20, of which waited for: 8 -> 11; matrix products, arithmetic and copies ran while one was open for 0% -> 0% of each run, Pallas kernels for 15% -> 11%
where the time goes in v3:
time: 92.2 us; the launch traced here: 91.9 us
  starting transfers between devices  28.9 us (31%)
  blocking collectives  28.5 us (31%)
  Pallas kernels  17.6 us (19%)
  waiting for transfers between devices  13.4 us (15%)
  local copies, waits for them, and re-layouts  3.14 us (3%)
    ppermute x18, starting transfers between devices, ring_exchange(): lax.ppermute(slots[d], axis, [(i, (i + d) % size) for i in range(size)])  28.8 us
    all_to_all x1, blocking collectives, local(): parts = lax.all_to_all(parts, 'z', split_axis=0, concat_axis=0, tiled=True)  17 us
    all_to_all x1, blocking collectives, local(): lax.all_to_all(states, 'z', split_axis=0, concat_axis=0, tiled=True)  11.5 us
    ppermute x18, waiting for transfers between devices, ring_exchange(): lax.ppermute(slots[d], axis, [(i, (i + d) % size) for i in range(size)])  11.2 us
    pallas_call x10, Pallas kernels, small_call(): pl.pallas_call(body, out_shape=[jax.ShapeDtypeStruct(shape, dtype) for sh...  8.27 us
    pallas_call x2, Pallas kernels, intra_term(): pl.pallas_call(functools.partial(intra_kernel, wave), out_shape=[jax.Shap...  4.45 us
    unnamed x18, local copies, waits for them, and re-layouts  3.14 us
    pallas_call x2, Pallas kernels, place(): pl.pallas_call(functools.partial(place_kernel, wave), out_shape=jax.Shape...  2.73 us
  transfers between devices with their start and end apart: 20, of which 11 were waited for; matrix products, arithmetic and copies ran while one was open for 0% of the time, Pallas kernels for 11%

profile of v3, /device:TPU:8, one launch (start us, length us, event | category | flops | bytes accessed | tf_op | source)
XLA Modules:
  0.0 91.9 jit_solution(13008003560500546831)
XLA Ops:
  0.0 0.1 pad_add_fusion.index
  0.1 0.6 copy-done.6
  0.7 0.0 copy-done.8
  0.7 1.2 %copy-done = bf16[1,1,128,4096]{3,2,1,0:T(8,128)(2,1)S(1)} copy-done((bf16[1,1,128,4096]{3,2,1,0:T(8,128)(2,1)S(1)}, bf16[1,1,128,4096]{3,2,1,0:T(8,128)(2,1)}, u32[]{:S(2)}) %copy-start) | copy-done | bytes 1048600
  2.0 1.2 %copy-done.2 = bf16[1,1,128,4096]{3,2,1,0:T(8,128)(2,1)S(1)} copy-done((bf16[1,1,128,4096]{3,2,1,0:T(8,128)(2,1)S(1)}, bf16[1,1,128,4096]{3,2,1,0:T(8,128)(2,1)}, u32[]{:S(2)}) %copy-start.2) | copy-done | bytes 1048600
  3.2 1.1 %shard_map.75 = bf16[4,544,128]{2,1,0:T(8,128)(2,1)S(1)} custom-call(s32[3]{0:T(128)S(1)} %pad_add_fusion.index, bf16[128,4096]{1,0:T(8,128)(2,1)S(1)} %bitcast.11, bf16[128,4096]{1,0:T(8,128)(2,1)S(1)} %bitcast.15, f32[32,128]{1,0:T(8,128)S(1)} %bitcast.26, s32[1,128]{1,0:T(1,128)S(1)} %copy-done.8), custom_call_target="tpu_custom_call" | custom-call | flops 67108864 | bytes 1572864 | tf_op jit(solution)/shard_map/pallas_call | solution.py:92
  4.3 0.1 collective-permute-start
  4.4 0.0 copy-start.3
  4.4 0.0 copy-start.4
  4.4 1.1 %shard_map.74.refs_0_ = bf16[4,544,128]{2,1,0:T(8,128)(2,1)S(1)} custom-call(s32[3]{0:T(128)S(1)} %pad_add_fusion.index, bf16[128,4096]{1,0:T(8,128)(2,1)S(1)} %bitcast.12, bf16[128,4096]{1,0:T(8,128)(2,1)S(1)} %bitcast.16, f32[32,128]{1,0:T(8,128)S(1)} %bitcast.27, s32[1,128]{1,0:T(1,128)S(1)} %copy-done.8), custom_call_target="tpu_custom_call" | custom-call | flops 67108864 | bytes 1572864 | tf_op jit(solution)/shard_map/pallas_call | solution.py:92
  5.4 0.0 copy-start.1
  5.5 0.8 collective-permute-done.refs_1_
  6.3 0.8 shard_map.76
  7.1 1.7 %collective-permute-start.1 = (bf16[544,128]{1,0:T(8,128)(2,1)S(1)}, bf16[544,128]{1,0:T(8,128)(2,1)S(1)}, u32[]{:S(2)}, u32[]{:S(2)}) collective-permute-start(bf16[544,128]{1,0:T(8,128)(2,1)S(1)} %get-tuple-element.36), channel_id=1, source_target_pairs={{0,2},{2,4},{4,6},{6,0},{1,3},{3,5},{5,7},{7,1},{8,10},{10,12},{12... | collective-permute-start | bytes 417800 | tf_op jit(solution)/shard_map/ppermute | solution.py:378
  8.7 2.7 %collective-permute-start.2 = (bf16[544,128]{1,0:T(8,128)(2,1)S(1)}, bf16[544,128]{1,0:T(8,128)(2,1)S(1)}, u32[]{:S(2)}, u32[]{:S(2)}) collective-permute-start(bf16[544,128]{1,0:T(8,128)(2,1)S(1)} %get-tuple-element.37), channel_id=1, source_target_pairs={{0,4},{2,6},{4,0},{6,2},{1,5},{3,7},{5,1},{7,3},{8,12},{10,14},{12... | collective-permute-start | bytes 417800 | tf_op jit(solution)/shard_map/ppermute | solution.py:378
  11.4 0.7 collective-permute-start.3
  12.1 2.2 %shard_map.77 = (f32[4,128,512]{2,1,0:T(8,128)S(1)}, bf16[4,128,8]{2,1,0:T(8,128)(2,1)S(1)}) custom-call(bf16[128,4096]{1,0:T(8,128)(2,1)S(1)} %bitcast.19, bf16[128,4096]{1,0:T(8,128)(2,1)S(1)} %bitcast.13, bf16[128,4096]{1,0:T(8,128)(2,1)S(1)} %bitcast.17, f32[32,128]{1,0:T(8,128)S(1)} %bitcast.28, s32[1,128]{1,0:T(1,128)S(1)} %copy-done.8), custom_call_target="tpu_custom_call" | custom-call | flops 134217728 | bytes 2621440 | tf_op jit(solution)/shard_map/pallas_call | solution.py:146
  14.3 0.0 collective-permute-done.1.refs_1_.refs_2_
  14.3 2.5 %collective-permute-done.2.refs_2_.refs_3_ = bf16[544,128]{1,0:T(8,128)(2,1)S(1)} collective-permute-done((bf16[544,128]{1,0:T(8,128)(2,1)S(1)}, bf16[544,128]{1,0:T(8,128)(2,1)S(1)}, u32[]{:S(2)}, u32[]{:S(2)}) %collective-permute-start.2) | collective-permute-done | bytes 139296 | tf_op jit(solution)/shard_map/ppermute | solution.py:378
  16.8 1.9 %collective-permute-done.3.refs_3_.refs_4_ = bf16[544,128]{1,0:T(8,128)(2,1)S(1)} collective-permute-done((bf16[544,128]{1,0:T(8,128)(2,1)S(1)}, bf16[544,128]{1,0:T(8,128)(2,1)S(1)}, u32[]{:S(2)}, u32[]{:S(2)}) %collective-permute-start.3) | collective-permute-done | bytes 139296 | tf_op jit(solution)/shard_map/ppermute | solution.py:378
  18.7 0.7 shard_map.78
  19.4 17.0 %all_to_all.10.refs_0_ = bf16[8,80,128]{2,1,0:T(8,128)(2,1)S(1)} all-to-all(bf16[8,80,128]{2,1,0:T(8,128)(2,1)S(1)} %shard_map.78), channel_id=1, replica_groups=mesh['phase'=4,'z'=8,'y'=4,'core'=2] {'z'}, dimensions={0} | all-to-all | bytes 327680 | tf_op jit(solution)/shard_map/all_to_all | solution.py:402
  36.4 0.6 shard_map.79
  37.0 11.5 %all_to_all.11 = bf16[8,64,128]{2,1,0:T(8,128)(2,1)S(1)} all-to-all(bf16[8,64,128]{2,1,0:T(8,128)(2,1)S(1)} %shard_map.79), channel_id=1, replica_groups=mesh['phase'=4,'z'=8,'y'=4,'core'=2] {'z'}, dimensions={0} | all-to-all | bytes 262144 | tf_op jit(solution)/shard_map/all_to_all | solution.py:404
  48.5 0.8 shard_map.80
  49.2 1.4 %collective-permute-start.4 = (bf16[512,128]{1,0:T(8,128)(2,1)S(1)}, bf16[512,128]{1,0:T(8,128)(2,1)S(1)}, u32[]{:S(2)}, u32[]{:S(2)}) collective-permute-start(bf16[512,128]{1,0:T(8,128)(2,1)S(1)} %get-tuple-element.41), channel_id=1, source_target_pairs={{0,2},{2,4},{4,6},{6,0},{1,3},{3,5},{5,7},{7,1},{8,10},{10,12},{12... | collective-permute-start | bytes 393224 | tf_op jit(solution)/shard_map/ppermute | solution.py:378
  50.6 1.6 %collective-permute-start.5 = (bf16[512,128]{1,0:T(8,128)(2,1)S(1)}, bf16[512,128]{1,0:T(8,128)(2,1)S(1)}, u32[]{:S(2)}, u32[]{:S(2)}) collective-permute-start(bf16[512,128]{1,0:T(8,128)(2,1)S(1)} %get-tuple-element.42), channel_id=1, source_target_pairs={{0,4},{2,6},{4,0},{6,2},{1,5},{3,7},{5,1},{7,3},{8,12},{10,14},{12... | collective-permute-start | bytes 393224 | tf_op jit(solution)/shard_map/ppermute | solution.py:378
  52.2 1.6 %collective-permute-start.6 = (bf16[512,128]{1,0:T(8,128)(2,1)S(1)}, bf16[512,128]{1,0:T(8,128)(2,1)S(1)}, u32[]{:S(2)}, u32[]{:S(2)}) collective-permute-start(bf16[512,128]{1,0:T(8,128)(2,1)S(1)} %get-tuple-element.43), channel_id=1, source_target_pairs={{0,6},{2,0},{4,2},{6,4},{1,7},{3,1},{5,3},{7,5},{8,14},{10,8},{12,... | collective-permute-start | bytes 393224 | tf_op jit(solution)/shard_map/ppermute | solution.py:378
  53.7 2.2 %shard_map.73 = (f32[4,128,512]{2,1,0:T(8,128)S(1)}, bf16[4,128,8]{2,1,0:T(8,128)(2,1)S(1)}) custom-call(bf16[128,4096]{1,0:T(8,128)(2,1)S(1)} %bitcast.20, bf16[128,4096]{1,0:T(8,128)(2,1)S(1)} %bitcast.14, bf16[128,4096]{1,0:T(8,128)(2,1)S(1)} %bitcast.18, f32[32,128]{1,0:T(8,128)S(1)} %bitcast.29, s32[1,128]{1,0:T(1,128)S(1)} %copy-done.8), custom_call_target="tpu_custom_call" | custom-call | flops 134217728 | bytes 2621440 | tf_op jit(solution)/shard_map/pallas_call | solution.py:146
  56.0 0.0 collective-permute-done.4.refs_3_
  56.0 1.2 %collective-permute-done.5.refs_4_ = bf16[512,128]{1,0:T(8,128)(2,1)S(1)} collective-permute-done((bf16[512,128]{1,0:T(8,128)(2,1)S(1)}, bf16[512,128]{1,0:T(8,128)(2,1)S(1)}, u32[]{:S(2)}, u32[]{:S(2)}) %collective-permute-start.5) | collective-permute-done | bytes 131104 | tf_op jit(solution)/shard_map/ppermute | solution.py:378
  57.2 1.3 %collective-permute-done.6.refs_5_ = bf16[512,128]{1,0:T(8,128)(2,1)S(1)} collective-permute-done((bf16[512,128]{1,0:T(8,128)(2,1)S(1)}, bf16[512,128]{1,0:T(8,128)(2,1)S(1)}, u32[]{:S(2)}, u32[]{:S(2)}) %collective-permute-start.6) | collective-permute-done | bytes 131104 | tf_op jit(solution)/shard_map/ppermute | solution.py:378
  58.5 0.8 shard_map.82
  59.3 0.0 copy-start.7
  59.3 0.1 collective-permute-start.7
  59.4 0.6 shard_map.81.refs_3_
  60.0 1.3 %collective-permute-done.7.refs_4_ = bf16[4,512,128]{2,1,0:T(8,128)(2,1)S(1)} collective-permute-done((bf16[4,512,128]{2,1,0:T(8,128)(2,1)S(1)}, bf16[4,512,128]{2,1,0:T(8,128)(2,1)S(1)}, u32[]{:S(2)}, u32[]{:S(2)}) %collective-permute-start.7) | collective-permute-done | bytes 524320 | tf_op jit(solution)/shard_map/ppermute | solution.py:384
  61.3 1.2 %shard_map.85 = (bf16[128,512]{1,0:T(8,128)(2,1)S(1)}, bf16[128,512]{1,0:T(8,128)(2,1)S(1)}, bf16[128,512]{1,0:T(8,128)(2,1)S(1)}, bf16[128,512]{1,0:T(8,128)(2,1)S(1)}) custom-call(s32[3]{0:T(128)S(1)} %pad_add_fusion.index, bf16[128,4096]{1,0:T(8,128)(2,1)S(1)} %bitcast.21, f32[4,128,512]{2,1,0:T(8,128)S(1)} %get-tuple-element.39.refs_4_.refs_1_, ...), custom_call_target="tpu_custom_call" | custom-call | flops 3162112 | bytes 6324224 | tf_op jit(solution)/shard_map/pallas_call | solution.py:202
  62.5 1.6 %collective-permute-start.14 = (bf16[128,512]{1,0:T(8,128)(2,1)S(1)}, bf16[128,512]{1,0:T(8,128)(2,1)S(1)}, u32[]{:S(2)}, u32[]{:S(2)}) collective-permute-start(bf16[128,512]{1,0:T(8,128)(2,1)S(1)} %get-tuple-element.54), channel_id=1, source_target_pairs={{0,64},{64,128},{128,192},{192,0},{1,65},{65,129},{129,193},{193,1... | collective-permute-start | bytes 393224 | tf_op jit(solution)/shard_map/ppermute | solution.py:378
  64.1 2.7 %collective-permute-start.15 = (bf16[128,512]{1,0:T(8,128)(2,1)S(1)}, bf16[128,512]{1,0:T(8,128)(2,1)S(1)}, u32[]{:S(2)}, u32[]{:S(2)}) collective-permute-start(bf16[128,512]{1,0:T(8,128)(2,1)S(1)} %get-tuple-element.55), channel_id=1, source_target_pairs={{0,128},{64,192},{128,0},{192,64},{1,129},{65,193},{129,1},{193,65... | collective-permute-start | bytes 393224 | tf_op jit(solution)/shard_map/ppermute | solution.py:378
  66.8 1.4 %collective-permute-start.16 = (bf16[128,512]{1,0:T(8,128)(2,1)S(1)}, bf16[128,512]{1,0:T(8,128)(2,1)S(1)}, u32[]{:S(2)}, u32[]{:S(2)}) collective-permute-start(bf16[128,512]{1,0:T(8,128)(2,1)S(1)} %get-tuple-element.56), channel_id=1, source_target_pairs={{0,192},{64,0},{128,64},{192,128},{1,193},{65,1},{129,65},{193,129... | collective-permute-start | bytes 393224 | tf_op jit(solution)/shard_map/ppermute | solution.py:378
  68.3 1.2 %shard_map.83 = (bf16[128,512]{1,0:T(8,128)(2,1)S(1)}, bf16[128,512]{1,0:T(8,128)(2,1)S(1)}, bf16[128,512]{1,0:T(8,128)(2,1)S(1)}, bf16[128,512]{1,0:T(8,128)(2,1)S(1)}) custom-call(s32[3]{0:T(128)S(1)} %pad_add_fusion.index, bf16[128,4096]{1,0:T(8,128)(2,1)S(1)} %bitcast.22, f32[4,128,512]{2,1,0:T(8,128)S(1)} %get-tuple-element.33.refs_6_.refs_1_, ...), custom_call_target="tpu_custom_call" | custom-call | flops 3162112 | bytes 6324224 | tf_op jit(solution)/shard_map/pallas_call | solution.py:202
  69.5 0.7 collective-permute-start.8
  70.2 0.9 collective-permute-start.9
  71.0 0.0 collective-permute-done.14.refs_2_
  71.0 1.9 %collective-permute-start.10 = (bf16[128,512]{1,0:T(8,128)(2,1)S(1)}, bf16[128,512]{1,0:T(8,128)(2,1)S(1)}, u32[]{:S(2)}, u32[]{:S(2)}) collective-permute-start(bf16[128,512]{1,0:T(8,128)(2,1)S(1)} %get-tuple-element.47), channel_id=1, source_target_pairs={{0,192},{64,0},{128,64},{192,128},{1,193},{65,1},{129,65},{193,129... | collective-permute-start | bytes 393224 | tf_op jit(solution)/shard_map/ppermute | solution.py:378
  72.9 1.0 %collective-permute-done.15.refs_3_ = bf16[128,512]{1,0:T(8,128)(2,1)S(1)} collective-permute-done((bf16[128,512]{1,0:T(8,128)(2,1)S(1)}, bf16[128,512]{1,0:T(8,128)(2,1)S(1)}, u32[]{:S(2)}, u32[]{:S(2)}) %collective-permute-start.15) | collective-permute-done | bytes 131104 | tf_op jit(solution)/shard_map/ppermute | solution.py:378
  73.9 0.0 collective-permute-done.16.refs_4_
  73.9 0.8 shard_map.86
  74.7 0.9 %collective-permute-start.17 = (bf16[128,512]{1,0:T(8,128)(2,1)S(1)}, bf16[128,512]{1,0:T(8,128)(2,1)S(1)}, u32[]{:S(2)}, u32[]{:S(2)}) collective-permute-start(bf16[128,512]{1,0:T(8,128)(2,1)S(1)} %get-tuple-element.58), channel_id=1, source_target_pairs={{0,64},{64,128},{128,192},{192,0},{1,65},{65,129},{129,193},{193,1... | collective-permute-start | bytes 393224 | tf_op jit(solution)/shard_map/ppermute | solution.py:378
  75.7 2.2 %collective-permute-start.18 = (bf16[128,512]{1,0:T(8,128)(2,1)S(1)}, bf16[128,512]{1,0:T(8,128)(2,1)S(1)}, u32[]{:S(2)}, u32[]{:S(2)}) collective-permute-start(bf16[128,512]{1,0:T(8,128)(2,1)S(1)} %get-tuple-element.59), channel_id=1, source_target_pairs={{0,128},{64,192},{128,0},{192,64},{1,129},{65,193},{129,1},{193,65... | collective-permute-start | bytes 393224 | tf_op jit(solution)/shard_map/ppermute | solution.py:378
  77.9 0.4 collective-permute-done.8.refs_2_
  78.2 2.1 %collective-permute-start.19 = (bf16[128,512]{1,0:T(8,128)(2,1)S(1)}, bf16[128,512]{1,0:T(8,128)(2,1)S(1)}, u32[]{:S(2)}, u32[]{:S(2)}) collective-permute-start(bf16[128,512]{1,0:T(8,128)(2,1)S(1)} %get-tuple-element.60), channel_id=1, source_target_pairs={{0,192},{64,0},{128,64},{192,128},{1,193},{65,1},{129,65},{193,129... | collective-permute-start | bytes 393224 | tf_op jit(solution)/shard_map/ppermute | solution.py:378
  80.4 0.0 collective-permute-done.9.refs_3_
  80.4 0.0 collective-permute-done.10.refs_4_
  80.4 0.8 shard_map.84
  81.2 1.6 %collective-permute-start.11 = (bf16[128,512]{1,0:T(8,128)(2,1)S(1)}, bf16[128,512]{1,0:T(8,128)(2,1)S(1)}, u32[]{:S(2)}, u32[]{:S(2)}) collective-permute-start(bf16[128,512]{1,0:T(8,128)(2,1)S(1)} %get-tuple-element.49), channel_id=1, source_target_pairs={{0,64},{64,128},{128,192},{192,0},{1,65},{65,129},{129,193},{193,1... | collective-permute-start | bytes 393224 | tf_op jit(solution)/shard_map/ppermute | solution.py:378
  82.8 2.6 %collective-permute-start.12 = (bf16[128,512]{1,0:T(8,128)(2,1)S(1)}, bf16[128,512]{1,0:T(8,128)(2,1)S(1)}, u32[]{:S(2)}, u32[]{:S(2)}) collective-permute-start(bf16[128,512]{1,0:T(8,128)(2,1)S(1)} %get-tuple-element.50), channel_id=1, source_target_pairs={{0,128},{64,192},{128,0},{192,64},{1,129},{65,193},{129,1},{193,65... | collective-permute-start | bytes 393224 | tf_op jit(solution)/shard_map/ppermute | solution.py:378
  85.4 0.6 collective-permute-start.13
  86.0 1.4 %shard_map.87.refs_4_ = bf16[128,4096]{1,0:T(8,128)(2,1)} custom-call(s32[3]{0:T(128)S(1)} %pad_add_fusion.index, bf16[128,512]{1,0:T(8,128)(2,1)S(1)} %get-tuple-element.57.refs_0_, bf16[128,512]{1,0:T(8,128)(2,1)S(1)} %collective-permute-done.17.refs_1_, bf16[128,512]{1,0:T(8,128)(2,1)S(1)} %collective-permute-done.18.refs_2_, ...), custom_call_target="tpu_custom_call" | custom-call | bytes 1048576 | tf_op jit(solution)/shard_map/pallas_call | solution.py:359
  87.4 1.4 %collective-permute-done.11.refs_1_ = bf16[128,512]{1,0:T(8,128)(2,1)S(1)} collective-permute-done((bf16[128,512]{1,0:T(8,128)(2,1)S(1)}, bf16[128,512]{1,0:T(8,128)(2,1)S(1)}, u32[]{:S(2)}, u32[]{:S(2)}) %collective-permute-start.11) | collective-permute-done | bytes 131104 | tf_op jit(solution)/shard_map/ppermute | solution.py:378
  88.8 1.4 %collective-permute-done.12.refs_2_ = bf16[128,512]{1,0:T(8,128)(2,1)S(1)} collective-permute-done((bf16[128,512]{1,0:T(8,128)(2,1)S(1)}, bf16[128,512]{1,0:T(8,128)(2,1)S(1)}, u32[]{:S(2)}, u32[]{:S(2)}) %collective-permute-start.12) | collective-permute-done | bytes 131104 | tf_op jit(solution)/shard_map/ppermute | solution.py:378
  90.2 0.2 collective-permute-done.13.refs_3_
  90.4 1.4 %shard_map.88 = bf16[128,4096]{1,0:T(8,128)(2,1)} custom-call(s32[3]{0:T(128)S(1)} %pad_add_fusion.index, bf16[128,512]{1,0:T(8,128)(2,1)S(1)} %get-tuple-element.48.refs_0_, bf16[128,512]{1,0:T(8,128)(2,1)S(1)} %collective-permute-done.11.refs_1_, bf16[128,512]{1,0:T(8,128)(2,1)S(1)} %collective-permute-done.12.refs_2_, ...), custom_call_target="tpu_custom_call", output_to_operand_aliasing={{}: (5, {})} | custom-call | bytes 1048576 | tf_op jit(solution)/shard_map/pallas_call | solution.py:359
  (13 shorter events, 0.0 us)
Async XLA Ops:
  0.0 0.7 copy-start.6
  0.1 0.7 copy-start.8
  0.7 1.2 %copy-start = (bf16[1,1,128,4096]{3,2,1,0:T(8,128)(2,1)S(1)}, bf16[1,1,128,4096]{3,2,1,0:T(8,128)(2,1)}, u32[]{:S(2)}) copy-start(bf16[1,1,128,4096]{3,2,1,0:T(8,128)(2,1)} %param.9) | copy-start | bytes 3145732
  2.0 1.2 %copy-start.2 = (bf16[1,1,128,4096]{3,2,1,0:T(8,128)(2,1)S(1)}, bf16[1,1,128,4096]{3,2,1,0:T(8,128)(2,1)}, u32[]{:S(2)}) copy-start(bf16[1,1,128,4096]{3,2,1,0:T(8,128)(2,1)} %param.10) | copy-start | bytes 3145732
  4.3 2.0 %collective-permute-start = (bf16[4,544,128]{2,1,0:T(8,128)(2,1)S(1)}, bf16[4,544,128]{2,1,0:T(8,128)(2,1)S(1)}, u32[]{:S(2)}, u32[]{:S(2)}) collective-permute-start(bf16[4,544,128]{2,1,0:T(8,128)(2,1)S(1)} %shard_map.75), channel_id=1, source_target_pairs={{0,1},{1,0},{2,3},{3,2},{4,5},{5,4},{6,7},{7,6},{8,9},{9,8},{10,11... | collective-permute-start | bytes 1671176 | tf_op jit(solution)/shard_map/ppermute | solution.py:384
  4.4 7.7 %copy-start.3 = (bf16[1,1,128,4096]{3,2,1,0:T(8,128)(2,1)S(1)}, bf16[1,1,128,4096]{3,2,1,0:T(8,128)(2,1)}, u32[]{:S(2)}) copy-start(bf16[1,1,128,4096]{3,2,1,0:T(8,128)(2,1)} %param.10) | copy-start | bytes 3145732
  4.4 7.7 %copy-start.4 = (bf16[1,1,128,4096]{3,2,1,0:T(8,128)(2,1)S(1)}, bf16[1,1,128,4096]{3,2,1,0:T(8,128)(2,1)}, u32[]{:S(2)}) copy-start(bf16[1,1,128,4096]{3,2,1,0:T(8,128)(2,1)} %param.8) | copy-start | bytes 3145732
  5.4 6.7 %copy-start.1 = (bf16[1,1,128,4096]{3,2,1,0:T(8,128)(2,1)S(1)}, bf16[1,1,128,4096]{3,2,1,0:T(8,128)(2,1)}, u32[]{:S(2)}) copy-start(bf16[1,1,128,4096]{3,2,1,0:T(8,128)(2,1)} %param.9) | copy-start | bytes 3145732
  7.1 7.2 %collective-permute-start.1 = (bf16[544,128]{1,0:T(8,128)(2,1)S(1)}, bf16[544,128]{1,0:T(8,128)(2,1)S(1)}, u32[]{:S(2)}, u32[]{:S(2)}) collective-permute-start(bf16[544,128]{1,0:T(8,128)(2,1)S(1)} %get-tuple-element.36), channel_id=1, source_target_pairs={{0,2},{2,4},{4,6},{6,0},{1,3},{3,5},{5,7},{7,1},{8,10},{10,12},{12... | collective-permute-start | bytes 417800 | tf_op jit(solution)/shard_map/ppermute | solution.py:378
  8.7 8.1 %collective-permute-start.2 = (bf16[544,128]{1,0:T(8,128)(2,1)S(1)}, bf16[544,128]{1,0:T(8,128)(2,1)S(1)}, u32[]{:S(2)}, u32[]{:S(2)}) collective-permute-start(bf16[544,128]{1,0:T(8,128)(2,1)S(1)} %get-tuple-element.37), channel_id=1, source_target_pairs={{0,4},{2,6},{4,0},{6,2},{1,5},{3,7},{5,1},{7,3},{8,12},{10,14},{12... | collective-permute-start | bytes 417800 | tf_op jit(solution)/shard_map/ppermute | solution.py:378
  11.4 7.2 %collective-permute-start.3 = (bf16[544,128]{1,0:T(8,128)(2,1)S(1)}, bf16[544,128]{1,0:T(8,128)(2,1)S(1)}, u32[]{:S(2)}, u32[]{:S(2)}) collective-permute-start(bf16[544,128]{1,0:T(8,128)(2,1)S(1)} %get-tuple-element.38), channel_id=1, source_target_pairs={{0,6},{2,0},{4,2},{6,4},{1,7},{3,1},{5,3},{7,5},{8,14},{10,8},{12,... | collective-permute-start | bytes 417800 | tf_op jit(solution)/shard_map/ppermute | solution.py:378
  49.2 6.7 %collective-permute-start.4 = (bf16[512,128]{1,0:T(8,128)(2,1)S(1)}, bf16[512,128]{1,0:T(8,128)(2,1)S(1)}, u32[]{:S(2)}, u32[]{:S(2)}) collective-permute-start(bf16[512,128]{1,0:T(8,128)(2,1)S(1)} %get-tuple-element.41), channel_id=1, source_target_pairs={{0,2},{2,4},{4,6},{6,0},{1,3},{3,5},{5,7},{7,1},{8,10},{10,12},{12... | collective-permute-start | bytes 393224 | tf_op jit(solution)/shard_map/ppermute | solution.py:378
  50.6 6.6 %collective-permute-start.5 = (bf16[512,128]{1,0:T(8,128)(2,1)S(1)}, bf16[512,128]{1,0:T(8,128)(2,1)S(1)}, u32[]{:S(2)}, u32[]{:S(2)}) collective-permute-start(bf16[512,128]{1,0:T(8,128)(2,1)S(1)} %get-tuple-element.42), channel_id=1, source_target_pairs={{0,4},{2,6},{4,0},{6,2},{1,5},{3,7},{5,1},{7,3},{8,12},{10,14},{12... | collective-permute-start | bytes 393224 | tf_op jit(solution)/shard_map/ppermute | solution.py:378
  52.2 6.3 %collective-permute-start.6 = (bf16[512,128]{1,0:T(8,128)(2,1)S(1)}, bf16[512,128]{1,0:T(8,128)(2,1)S(1)}, u32[]{:S(2)}, u32[]{:S(2)}) collective-permute-start(bf16[512,128]{1,0:T(8,128)(2,1)S(1)} %get-tuple-element.43), channel_id=1, source_target_pairs={{0,6},{2,0},{4,2},{6,4},{1,7},{3,1},{5,3},{7,5},{8,14},{10,8},{12,... | collective-permute-start | bytes 393224 | tf_op jit(solution)/shard_map/ppermute | solution.py:378
  59.3 2.0 %copy-start.7 = (bf16[1,4096]{1,0:T(2,128)(2,1)S(1)}, bf16[1,4096]{1,0:T(2,128)(2,1)}, u32[]{:S(2)}) copy-start(bf16[1,4096]{1,0:T(2,128)(2,1)} %param.11) | copy-start | bytes 24580
  59.3 2.0 %collective-permute-start.7 = (bf16[4,512,128]{2,1,0:T(8,128)(2,1)S(1)}, bf16[4,512,128]{2,1,0:T(8,128)(2,1)S(1)}, u32[]{:S(2)}, u32[]{:S(2)}) collective-permute-start(bf16[4,512,128]{2,1,0:T(8,128)(2,1)S(1)} %shard_map.82), channel_id=1, source_target_pairs={{0,1},{1,0},{2,3},{3,2},{4,5},{5,4},{6,7},{7,6},{8,9},{9,8},{10,11... | collective-permute-start | bytes 1572872 | tf_op jit(solution)/shard_map/ppermute | solution.py:384
  62.5 8.5 %collective-permute-start.14 = (bf16[128,512]{1,0:T(8,128)(2,1)S(1)}, bf16[128,512]{1,0:T(8,128)(2,1)S(1)}, u32[]{:S(2)}, u32[]{:S(2)}) collective-permute-start(bf16[128,512]{1,0:T(8,128)(2,1)S(1)} %get-tuple-element.54), channel_id=1, source_target_pairs={{0,64},{64,128},{128,192},{192,0},{1,65},{65,129},{129,193},{193,1... | collective-permute-start | bytes 393224 | tf_op jit(solution)/shard_map/ppermute | solution.py:378
  64.1 9.9 %collective-permute-start.15 = (bf16[128,512]{1,0:T(8,128)(2,1)S(1)}, bf16[128,512]{1,0:T(8,128)(2,1)S(1)}, u32[]{:S(2)}, u32[]{:S(2)}) collective-permute-start(bf16[128,512]{1,0:T(8,128)(2,1)S(1)} %get-tuple-element.55), channel_id=1, source_target_pairs={{0,128},{64,192},{128,0},{192,64},{1,129},{65,193},{129,1},{193,65... | collective-permute-start | bytes 393224 | tf_op jit(solution)/shard_map/ppermute | solution.py:378
  66.8 7.1 %collective-permute-start.16 = (bf16[128,512]{1,0:T(8,128)(2,1)S(1)}, bf16[128,512]{1,0:T(8,128)(2,1)S(1)}, u32[]{:S(2)}, u32[]{:S(2)}) collective-permute-start(bf16[128,512]{1,0:T(8,128)(2,1)S(1)} %get-tuple-element.56), channel_id=1, source_target_pairs={{0,192},{64,0},{128,64},{192,128},{1,193},{65,1},{129,65},{193,129... | collective-permute-start | bytes 393224 | tf_op jit(solution)/shard_map/ppermute | solution.py:378
  68.3 5.7 %copy-start.5 = (bf16[1,128,1024]{2,1,0:T(8,128)(2,1)S(1)}, bf16[1,128,1024]{2,1,0:T(8,128)(2,1)}, u32[]{:S(2)}) copy-start(bf16[1,128,1024]{2,1,0:T(8,128)(2,1)} %param.7) | copy-start | bytes 786436
  69.5 8.8 %collective-permute-start.8 = (bf16[128,512]{1,0:T(8,128)(2,1)S(1)}, bf16[128,512]{1,0:T(8,128)(2,1)S(1)}, u32[]{:S(2)}, u32[]{:S(2)}) collective-permute-start(bf16[128,512]{1,0:T(8,128)(2,1)S(1)} %get-tuple-element.45), channel_id=1, source_target_pairs={{0,64},{64,128},{128,192},{192,0},{1,65},{65,129},{129,193},{193,1... | collective-permute-start | bytes 393224 | tf_op jit(solution)/shard_map/ppermute | solution.py:378
  70.2 10.2 %collective-permute-start.9 = (bf16[128,512]{1,0:T(8,128)(2,1)S(1)}, bf16[128,512]{1,0:T(8,128)(2,1)S(1)}, u32[]{:S(2)}, u32[]{:S(2)}) collective-permute-start(bf16[128,512]{1,0:T(8,128)(2,1)S(1)} %get-tuple-element.46), channel_id=1, source_target_pairs={{0,128},{64,192},{128,0},{192,64},{1,129},{65,193},{129,1},{193,65... | collective-permute-start | bytes 393224 | tf_op jit(solution)/shard_map/ppermute | solution.py:378
  71.0 9.3 %collective-permute-start.10 = (bf16[128,512]{1,0:T(8,128)(2,1)S(1)}, bf16[128,512]{1,0:T(8,128)(2,1)S(1)}, u32[]{:S(2)}, u32[]{:S(2)}) collective-permute-start(bf16[128,512]{1,0:T(8,128)(2,1)S(1)} %get-tuple-element.47), channel_id=1, source_target_pairs={{0,192},{64,0},{128,64},{192,128},{1,193},{65,1},{129,65},{193,129... | collective-permute-start | bytes 393224 | tf_op jit(solution)/shard_map/ppermute | solution.py:378
  74.7 10.7 %collective-permute-start.17 = (bf16[128,512]{1,0:T(8,128)(2,1)S(1)}, bf16[128,512]{1,0:T(8,128)(2,1)S(1)}, u32[]{:S(2)}, u32[]{:S(2)}) collective-permute-start(bf16[128,512]{1,0:T(8,128)(2,1)S(1)} %get-tuple-element.58), channel_id=1, source_target_pairs={{0,64},{64,128},{128,192},{192,0},{1,65},{65,129},{129,193},{193,1... | collective-permute-start | bytes 393224 | tf_op jit(solution)/shard_map/ppermute | solution.py:378
  75.7 10.3 %collective-permute-start.18 = (bf16[128,512]{1,0:T(8,128)(2,1)S(1)}, bf16[128,512]{1,0:T(8,128)(2,1)S(1)}, u32[]{:S(2)}, u32[]{:S(2)}) collective-permute-start(bf16[128,512]{1,0:T(8,128)(2,1)S(1)} %get-tuple-element.59), channel_id=1, source_target_pairs={{0,128},{64,192},{128,0},{192,64},{1,129},{65,193},{129,1},{193,65... | collective-permute-start | bytes 393224 | tf_op jit(solution)/shard_map/ppermute | solution.py:378
  78.2 7.8 %collective-permute-start.19 = (bf16[128,512]{1,0:T(8,128)(2,1)S(1)}, bf16[128,512]{1,0:T(8,128)(2,1)S(1)}, u32[]{:S(2)}, u32[]{:S(2)}) collective-permute-start(bf16[128,512]{1,0:T(8,128)(2,1)S(1)} %get-tuple-element.60), channel_id=1, source_target_pairs={{0,192},{64,0},{128,64},{192,128},{1,193},{65,1},{129,65},{193,129... | collective-permute-start | bytes 393224 | tf_op jit(solution)/shard_map/ppermute | solution.py:378
  81.2 7.6 %collective-permute-start.11 = (bf16[128,512]{1,0:T(8,128)(2,1)S(1)}, bf16[128,512]{1,0:T(8,128)(2,1)S(1)}, u32[]{:S(2)}, u32[]{:S(2)}) collective-permute-start(bf16[128,512]{1,0:T(8,128)(2,1)S(1)} %get-tuple-element.49), channel_id=1, source_target_pairs={{0,64},{64,128},{128,192},{192,0},{1,65},{65,129},{129,193},{193,1... | collective-permute-start | bytes 393224 | tf_op jit(solution)/shard_map/ppermute | solution.py:378
  82.8 7.4 %collective-permute-start.12 = (bf16[128,512]{1,0:T(8,128)(2,1)S(1)}, bf16[128,512]{1,0:T(8,128)(2,1)S(1)}, u32[]{:S(2)}, u32[]{:S(2)}) collective-permute-start(bf16[128,512]{1,0:T(8,128)(2,1)S(1)} %get-tuple-element.50), channel_id=1, source_target_pairs={{0,128},{64,192},{128,0},{192,64},{1,129},{65,193},{129,1},{193,65... | collective-permute-start | bytes 393224 | tf_op jit(solution)/shard_map/ppermute | solution.py:378
  85.4 5.0 %collective-permute-start.13 = (bf16[128,512]{1,0:T(8,128)(2,1)S(1)}, bf16[128,512]{1,0:T(8,128)(2,1)S(1)}, u32[]{:S(2)}, u32[]{:S(2)}) collective-permute-start(bf16[128,512]{1,0:T(8,128)(2,1)S(1)} %get-tuple-element.51), channel_id=1, source_target_pairs={{0,192},{64,0},{128,64},{192,128},{1,193},{65,1},{129,65},{193,129... | collective-permute-start | bytes 393224 | tf_op jit(solution)/shard_map/ppermute | solution.py:378

commit v4 on v3

--- a/solution.py
+++ b/solution.py
@@ -18,7 +18,8 @@
 META = 32
 ROWS = GROUP * D
 PART = ROWS + META
-PHASE, Y, CORE = 0, 1, 2
+PAIR = 2 * D + META
+PHASE, Y, CORE, Z = 0, 1, 2, 3
 VMEM_LIMIT = 16 * 1024 * 1024
 
 
@@ -220,51 +221,81 @@
 
 
 def row_kernel(index, *refs):
-    *slots, out_ref, ordered_ref = refs
+    *slots, send_ref, keep_ref, ordered_ref, state_ref = refs
     in_order(index[Y], slots, ordered_ref)
     metas = [unpack_meta(ordered_ref[c, ROWS:PART, :]) for c in range(4)]
     weights, after = [None] * 4, jnp.zeros((8, D), F32)
     for c in (3, 2, 1, 0):
         weights[c] = jnp.exp(after) * same(metas[c][2], metas[3][2])
         after = after + metas[c][0]
-    row = iota((16, D), 0)
     for i in range(GROUP):
         rows = slice(i * D, (i + 1) * D)
-        state = sum(weights[c][i : i + 1] * ordered_ref[c, rows, :].astype(F32) for c in range(4)).astype(BF16)
-        out_ref[2 * i, 0 : D // 2, :] = state[0 : D // 2]
-        out_ref[2 * i + 1, 0 : D // 2, :] = state[D // 2 :]
-        hi, mid, low = split3(after[i : i + 1])
-        meta = jnp.zeros((16, D), F32)
-        for at, value in enumerate((hi, mid, low, metas[0][1], metas[3][2])):
-            meta = jnp.where(row == at, value, meta)
-        out_ref[2 * i, D // 2 :, :] = meta.astype(BF16)
-        out_ref[2 * i + 1, D // 2 :, :] = meta.astype(BF16)
-
-
-def scan_kernel(index, in_ref, out_ref):
-    del index
-    state = jnp.zeros((D // 2, D), F32)
-    before = jnp.full((1, D), -1.0, F32)
-    for z in range(NZ):
-        meta = in_ref[z, D // 2 :, :].astype(F32)
-        decay, first, last = meta[0:1] + meta[1:2] + meta[2:3], meta[3:4], meta[4:5]
-        state = state * same(before, first)
-        out_ref[z] = state.astype(BF16)
-        state = jnp.exp(decay) * same(first, last) * state + in_ref[z, 0 : D // 2, :].astype(F32)
-        before = last
-
-
-def spread_kernel(index, state_ref, *refs):
+        state = sum(weights[c][i : i + 1] * ordered_ref[c, rows, :].astype(F32) for c in range(4))
+        state_ref[i] = state.astype(BF16)
+    odd = lax.rem(index[Z], 2)
+    turned = jnp.concatenate([after[2:4], after[0:2], after[4:8]], axis=0)
+    for out_ref, half in ((send_ref, 1 - odd), (keep_ref, odd)):
+        for i in range(2):
+            out_ref[i * D : (i + 1) * D, :] = state_ref[2 * half + i]
+        out_ref[2 * D : PAIR, :] = pack_meta(jnp.where(half == 0, after, turned), metas[0][1], metas[3][2])
+
+
+def pair_kernel(index, own_ref, other_ref, out_ref):
+    is_odd = lax.rem(index[Z], 2) == 1
+    decay_own, first_own, last_own = unpack_meta(own_ref[2 * D : PAIR, :])
+    decay_other, first_other, last_other = unpack_meta(other_ref[2 * D : PAIR, :])
+    passed = jnp.exp(jnp.where(is_odd, decay_own, decay_other)) * same(last_own, last_other)
+    weight_own = jnp.where(is_odd, 1.0, passed)
+    weight_other = jnp.where(is_odd, passed, 1.0)
+    for i in range(2):
+        rows = slice(i * D, (i + 1) * D)
+        out_ref[rows, :] = (
+            weight_own[i : i + 1] * own_ref[rows, :].astype(F32)
+            + weight_other[i : i + 1] * other_ref[rows, :].astype(F32)
+        ).astype(BF16)
+    out_ref[2 * D : PAIR, :] = pack_meta(
+        decay_own + decay_other,
+        jnp.where(is_odd, first_other, first_own),
+        jnp.where(is_odd, last_own, last_other),
+    )
+
+
+def prefix_kernel(index, own_ref, other_ref, *refs):
+    *before, mine_ref, send_ref = refs
+    is_odd = lax.rem(index[Z], 2) == 1
+    decay_own, first_own, last_own = unpack_meta(own_ref[2 * D : PAIR, :])
+    decay_other, first_other, last_other = unpack_meta(other_ref[2 * D : PAIR, :])
+    decay0 = jnp.where(is_odd, decay_other, decay_own)
+    first0, first1 = jnp.where(is_odd, first_other, first_own), jnp.where(is_odd, first_own, first_other)
+    last0 = jnp.where(is_odd, last_other, last_own)
+    joined = same(last0, first1)
+    passing = jnp.exp(decay0) * same(first0, last0) * joined
+    weights, after = [], jnp.zeros((8, D), F32)
+    for back, pair in enumerate(before, start=1):
+        decay, _, last = unpack_meta(pair[2 * D : PAIR, :])
+        weights.append(jnp.where(index[Z] >= 2 * back, jnp.exp(after) * same(last, first0), 0.0))
+        after = after + decay
+    for i in range(2):
+        rows = slice(i * D, (i + 1) * D)
+        state = sum(w[i : i + 1] * pair[rows, :].astype(F32) for w, pair in zip(weights, before))
+        earlier = jnp.where(is_odd, other_ref[rows, :], own_ref[rows, :]).astype(F32)
+        later = passing[i : i + 1] * state + joined * earlier
+        mine_ref[rows, :] = jnp.where(is_odd, later, state).astype(BF16)
+        send_ref[rows, :] = jnp.where(is_odd, state, later).astype(BF16)
+
+
+def spread_kernel(index, mine_ref, theirs_ref, *refs):
     *slots, out0, out1, out2, out3, ordered_ref, result_ref = refs
-    y = index[Y]
+    y, odd = index[Y], lax.rem(index[Z], 2)
     in_order(y, slots, ordered_ref)
     metas = [unpack_meta(ordered_ref[c, ROWS:PART, :]) for c in range(4)]
     passing = [jnp.exp(decay) * same(first, last) for decay, first, last in metas]
     joined = [None] + [same(metas[c - 1][2], metas[c][1]) for c in (1, 2, 3)]
     for i in range(GROUP):
-        rows = slice(i * D, (i + 1) * D)
-        state = state_ref[rows, :].astype(F32)
-        result_ref[0, rows, :] = state.astype(BF16)
+        rows, pair_rows = slice(i * D, (i + 1) * D), slice((i % 2) * D, (i % 2 + 1) * D)
+        state = jnp.where(odd == i // 2, mine_ref[pair_rows, :], theirs_ref[pair_rows, :])
+        result_ref[0, rows, :] = state
+        state = state.astype(F32)
         for c in (1, 2, 3):
             state = passing[c - 1][i : i + 1] * state + ordered_ref[c - 1, rows, :].astype(F32)
             state = state * joined[c]
@@ -380,12 +411,16 @@
     return [slots[0], *moved]
 
 
+def swap_rows(array):
+    return lax.ppermute(array, "z", [(i, i ^ 1) for i in range(NZ)])
+
+
 def swap_cores(array):
     return lax.ppermute(array, "core", [(0, 1), (1, 0)])
 
 
 def local(tokens, queries, keys_in, values, norm_gain, log_decay, doc_ids):
-    index = jnp.stack([lax.axis_index(name) for name in ("phase", "y", "core")]).astype(jnp.int32)
+    index = jnp.stack([lax.axis_index(name) for name in ("phase", "y", "core", "z")]).astype(jnp.int32)
     queries, keys, values, decay = queries[0, 0], keys_in[0, 0], values[0, 0], log_decay[0, 0]
     gain = norm_gain.reshape(8, 1, ROWS)
 
@@ -396,16 +431,23 @@
     slots = ring_exchange(small_call(chip_kernel, index, [own, other], [part] * 4), "y")
     intra = [intra_term(wave, queries, keys, values, decay, doc_ids) for wave in range(2)]
 
-    (parts,) = small_call(
-        row_kernel, index, slots, [((NZ, D // 2 + 16, D), BF16)], [pltpu.VMEM((4, PART, D), BF16)], intra[0][:1]
+    pair, pair_states = ((PAIR, D), BF16), ((2 * D, D), BF16)
+    send, keep = small_call(
+        row_kernel,
+        index,
+        slots,
+        [pair] * 2,
+        [pltpu.VMEM((4, PART, D), BF16), pltpu.VMEM((GROUP, D, D), BF16)],
+        intra[0][:1],
     )
-    parts = lax.all_to_all(parts, "z", split_axis=0, concat_axis=0, tiled=True)
-    (states,) = small_call(scan_kernel, index, [parts], [((NZ, D // 2, D), BF16)])
-    states = lax.all_to_all(states, "z", split_axis=0, concat_axis=0, tiled=True)
+    partner = swap_rows(send)
+    (both,) = small_call(pair_kernel, index, [keep, partner], [pair])
+    before = [lax.ppermute(both, "z", [(i, i + by) for i in range(NZ - by)]) for by in (2, 4, 6)]
+    mine, send = small_call(prefix_kernel, index, [keep, partner, *before], [pair_states] * 2)
     spread = small_call(
         spread_kernel,
         index,
-        [states.reshape(ROWS, D), *slots],
+        [mine, swap_rows(send), *slots],
         [group_states] * 4,
         [pltpu.VMEM((4, PART, D), BF16), pltpu.VMEM((4, ROWS, D), BF16)],
     )

time: 92.2 us -> 88.3 us (0.958)
  blocking collectives: 28.5 us -> 0 us
  starting transfers between devices: 28.9 us -> 45.1 us
  waiting for transfers between devices: 13.4 us -> 21 us
    all_to_all x2 -> x0, blocking collectives: 28.5 us -> none  [the longest x1 17 us: local(): parts = lax.all_to_all(parts, 'z', split_axis=0, concat_axis=0, tiled=True)]
    ppermute x0 -> x5, starting transfers between devices: none -> 16.2 us  [the longest x3 13.1 us: local(): lax.ppermute(both, 'z', [(i, i + by) for i in range(NZ - by)])]
    ppermute x0 -> x5, waiting for transfers between devices: none -> 7.61 us  [the longest x2 5.66 us: swap_rows(): return lax.ppermute(array, 'z', [(i, i ^ 1) for i in range(NZ)])]
    pallas_call x10 -> x11, Pallas kernels: 8.27 us -> 8.87 us  [small_call(): pl.pallas_call(body, out_shape=[jax.ShapeDtypeStruct(shape, dtype) for sh...]
  transfers between devices with their start and end apart: 20 -> 25, of which waited for: 11 -> 14; matrix products, arithmetic and copies ran while one was open for 0% -> 0% of each run, Pallas kernels for 11% -> 12%
where the time goes in v4:
time: 88.3 us; the launch traced here: 87.9 us
  starting transfers between devices  45.1 us (51%)
  waiting for transfers between devices  21 us (24%)
  Pallas kernels  18.2 us (21%)
  local copies, waits for them, and re-layouts  3.14 us (4%)
    ppermute x18, starting transfers between devices, ring_exchange(): lax.ppermute(slots[d], axis, [(i, (i + d) % size) for i in range(size)])  28.7 us
    ppermute x3, starting transfers between devices, local(): lax.ppermute(both, 'z', [(i, i + by) for i in range(NZ - by)])  13.1 us
    ppermute x18, waiting for transfers between devices, ring_exchange(): lax.ppermute(slots[d], axis, [(i, (i + d) % size) for i in range(size)])  11.3 us
    pallas_call x11, Pallas kernels, small_call(): pl.pallas_call(body, out_shape=[jax.ShapeDtypeStruct(shape, dtype) for sh...  8.87 us
    ppermute x2, waiting for transfers between devices, swap_rows(): return lax.ppermute(array, 'z', [(i, i ^ 1) for i in range(NZ)])  5.66 us
    pallas_call x2, Pallas kernels, intra_term(): pl.pallas_call(functools.partial(intra_kernel, wave), out_shape=[jax.Shap...  4.45 us
    unnamed x18, local copies, waits for them, and re-layouts  3.14 us
    ppermute x2, starting transfers between devices, swap_rows(): return lax.ppermute(array, 'z', [(i, i ^ 1) for i in range(NZ)])  3.13 us
  transfers between devices with their start and end apart: 25, of which 14 were waited for; matrix products, arithmetic and copies ran while one was open for 0% of the time, Pallas kernels for 12%

profile of v4, /device:TPU:8, one launch (start us, length us, event | category | flops | bytes accessed | tf_op | source)
XLA Modules:
  0.0 87.9 jit_solution(17171429431834172695)
XLA Ops:
  0.0 0.1 pad_add_fusion.index
  0.1 0.6 copy-done.6
  0.7 0.0 copy-done.8
  0.7 1.2 %copy-done = bf16[1,1,128,4096]{3,2,1,0:T(8,128)(2,1)S(1)} copy-done((bf16[1,1,128,4096]{3,2,1,0:T(8,128)(2,1)S(1)}, bf16[1,1,128,4096]{3,2,1,0:T(8,128)(2,1)}, u32[]{:S(2)}) %copy-start) | copy-done | bytes 1048600
  2.0 1.2 %copy-done.2 = bf16[1,1,128,4096]{3,2,1,0:T(8,128)(2,1)S(1)} copy-done((bf16[1,1,128,4096]{3,2,1,0:T(8,128)(2,1)S(1)}, bf16[1,1,128,4096]{3,2,1,0:T(8,128)(2,1)}, u32[]{:S(2)}) %copy-start.2) | copy-done | bytes 1048600
  3.2 1.1 %shard_map.75 = bf16[4,544,128]{2,1,0:T(8,128)(2,1)S(1)} custom-call(s32[4]{0:T(128)S(1)} %pad_add_fusion.index, bf16[128,4096]{1,0:T(8,128)(2,1)S(1)} %bitcast.11, bf16[128,4096]{1,0:T(8,128)(2,1)S(1)} %bitcast.15, f32[32,128]{1,0:T(8,128)S(1)} %bitcast.25, s32[1,128]{1,0:T(1,128)S(1)} %copy-done.8), custom_call_target="tpu_custom_call" | custom-call | flops 67108864 | bytes 1572864 | tf_op jit(solution)/shard_map/pallas_call | solution.py:93
  4.3 0.1 collective-permute-start
  4.4 0.0 copy-start.3
  4.4 0.0 copy-start.4
  4.4 1.1 %shard_map.74.refs_0_ = bf16[4,544,128]{2,1,0:T(8,128)(2,1)S(1)} custom-call(s32[4]{0:T(128)S(1)} %pad_add_fusion.index, bf16[128,4096]{1,0:T(8,128)(2,1)S(1)} %bitcast.12, bf16[128,4096]{1,0:T(8,128)(2,1)S(1)} %bitcast.16, f32[32,128]{1,0:T(8,128)S(1)} %bitcast.26, s32[1,128]{1,0:T(1,128)S(1)} %copy-done.8), custom_call_target="tpu_custom_call" | custom-call | flops 67108864 | bytes 1572864 | tf_op jit(solution)/shard_map/pallas_call | solution.py:93
  5.4 0.0 copy-start.1
  5.5 0.8 collective-permute-done.refs_1_
  6.3 0.8 shard_map.76
  7.1 1.7 %collective-permute-start.1 = (bf16[544,128]{1,0:T(8,128)(2,1)S(1)}, bf16[544,128]{1,0:T(8,128)(2,1)S(1)}, u32[]{:S(2)}, u32[]{:S(2)}) collective-permute-start(bf16[544,128]{1,0:T(8,128)(2,1)S(1)} %get-tuple-element.40), channel_id=1, source_target_pairs={{0,2},{2,4},{4,6},{6,0},{1,3},{3,5},{5,7},{7,1},{8,10},{10,12},{12... | collective-permute-start | bytes 417800 | tf_op jit(solution)/shard_map/ppermute | solution.py:409
  8.8 2.7 %collective-permute-start.2 = (bf16[544,128]{1,0:T(8,128)(2,1)S(1)}, bf16[544,128]{1,0:T(8,128)(2,1)S(1)}, u32[]{:S(2)}, u32[]{:S(2)}) collective-permute-start(bf16[544,128]{1,0:T(8,128)(2,1)S(1)} %get-tuple-element.41), channel_id=1, source_target_pairs={{0,4},{2,6},{4,0},{6,2},{1,5},{3,7},{5,1},{7,3},{8,12},{10,14},{12... | collective-permute-start | bytes 417800 | tf_op jit(solution)/shard_map/ppermute | solution.py:409
  11.4 0.7 collective-permute-start.3
  12.1 2.2 %shard_map.77 = (f32[4,128,512]{2,1,0:T(8,128)S(1)}, bf16[4,128,8]{2,1,0:T(8,128)(2,1)S(1)}) custom-call(bf16[128,4096]{1,0:T(8,128)(2,1)S(1)} %bitcast.19, bf16[128,4096]{1,0:T(8,128)(2,1)S(1)} %bitcast.13, bf16[128,4096]{1,0:T(8,128)(2,1)S(1)} %bitcast.17, f32[32,128]{1,0:T(8,128)S(1)} %bitcast.27, s32[1,128]{1,0:T(1,128)S(1)} %copy-done.8), custom_call_target="tpu_custom_call" | custom-call | flops 134217728 | bytes 2621440 | tf_op jit(solution)/shard_map/pallas_call | solution.py:147
  14.3 2.5 %collective-permute-done.2.refs_2_.refs_4_ = bf16[544,128]{1,0:T(8,128)(2,1)S(1)} collective-permute-done((bf16[544,128]{1,0:T(8,128)(2,1)S(1)}, bf16[544,128]{1,0:T(8,128)(2,1)S(1)}, u32[]{:S(2)}, u32[]{:S(2)}) %collective-permute-start.2) | collective-permute-done | bytes 139296 | tf_op jit(solution)/shard_map/ppermute | solution.py:409
  16.8 1.9 %collective-permute-done.3.refs_3_.refs_5_ = bf16[544,128]{1,0:T(8,128)(2,1)S(1)} collective-permute-done((bf16[544,128]{1,0:T(8,128)(2,1)S(1)}, bf16[544,128]{1,0:T(8,128)(2,1)S(1)}, u32[]{:S(2)}, u32[]{:S(2)}) %collective-permute-start.3) | collective-permute-done | bytes 139296 | tf_op jit(solution)/shard_map/ppermute | solution.py:409
  18.7 0.7 shard_map.78
  19.4 1.3 %collective-permute-start.4 = (bf16[288,128]{1,0:T(8,128)(2,1)S(1)}, bf16[288,128]{1,0:T(8,128)(2,1)S(1)}, u32[]{:S(2)}, u32[]{:S(2)}) collective-permute-start(bf16[288,128]{1,0:T(8,128)(2,1)S(1)} %get-tuple-element.45), channel_id=1, source_target_pairs={{0,8},{8,0},{16,24},{24,16},{32,40},{40,32},{48,56},{56,48},{1,9},... | collective-permute-start | bytes 221192 | tf_op jit(solution)/shard_map/ppermute | solution.py:415
  20.7 3.1 %collective-permute-done.4.refs_1_ = bf16[288,128]{1,0:T(8,128)(2,1)S(1)} collective-permute-done((bf16[288,128]{1,0:T(8,128)(2,1)S(1)}, bf16[288,128]{1,0:T(8,128)(2,1)S(1)}, u32[]{:S(2)}, u32[]{:S(2)}) %collective-permute-start.4) | collective-permute-done | bytes 73760 | tf_op jit(solution)/shard_map/ppermute | solution.py:415
  23.8 0.6 shard_map.79
  24.4 7.5 %collective-permute-start.7 = (bf16[288,128]{1,0:T(8,128)(2,1)S(1)}, bf16[288,128]{1,0:T(8,128)(2,1)S(1)}, u32[]{:S(2)}, u32[]{:S(2)}) collective-permute-start(bf16[288,128]{1,0:T(8,128)(2,1)S(1)} %shard_map.79), channel_id=1, source_target_pairs={{0,48},{8,56},{1,49},{9,57},{2,50},{10,58},{3,51},{11,59},{4,52},{... | collective-permute-start | bytes 221192 | tf_op jit(solution)/shard_map/ppermute | solution.py:445
  31.9 1.6 %collective-permute-start.6 = (bf16[288,128]{1,0:T(8,128)(2,1)S(1)}, bf16[288,128]{1,0:T(8,128)(2,1)S(1)}, u32[]{:S(2)}, u32[]{:S(2)}) collective-permute-start(bf16[288,128]{1,0:T(8,128)(2,1)S(1)} %shard_map.79), channel_id=1, source_target_pairs={{0,32},{8,40},{16,48},{24,56},{1,33},{9,41},{17,49},{25,57},{2,34}... | collective-permute-start | bytes 221192 | tf_op jit(solution)/shard_map/ppermute | solution.py:445
  33.5 4.0 %collective-permute-start.5 = (bf16[288,128]{1,0:T(8,128)(2,1)S(1)}, bf16[288,128]{1,0:T(8,128)(2,1)S(1)}, u32[]{:S(2)}, u32[]{:S(2)}) collective-permute-start(bf16[288,128]{1,0:T(8,128)(2,1)S(1)} %shard_map.79), channel_id=1, source_target_pairs={{0,16},{8,24},{16,32},{24,40},{32,48},{40,56},{1,17},{9,25},{17,33... | collective-permute-start | bytes 221192 | tf_op jit(solution)/shard_map/ppermute | solution.py:445
  37.5 1.9 %collective-permute-done.5.refs_2_ = bf16[288,128]{1,0:T(8,128)(2,1)S(1)} collective-permute-done((bf16[288,128]{1,0:T(8,128)(2,1)S(1)}, bf16[288,128]{1,0:T(8,128)(2,1)S(1)}, u32[]{:S(2)}, u32[]{:S(2)}) %collective-permute-start.5) | collective-permute-done | bytes 73760 | tf_op jit(solution)/shard_map/ppermute | solution.py:445
  39.5 0.6 shard_map.80
  40.1 1.8 %collective-permute-start.8 = (bf16[256,128]{1,0:T(8,128)(2,1)S(1)}, bf16[256,128]{1,0:T(8,128)(2,1)S(1)}, u32[]{:S(2)}, u32[]{:S(2)}) collective-permute-start(bf16[256,128]{1,0:T(8,128)(2,1)S(1)} %get-tuple-element.47), channel_id=1, source_target_pairs={{0,8},{8,0},{16,24},{24,16},{32,40},{40,32},{48,56},{56,48},{1,9},... | collective-permute-start | bytes 196616 | tf_op jit(solution)/shard_map/ppermute | solution.py:415
  41.9 2.5 %collective-permute-done.8.refs_1_ = bf16[256,128]{1,0:T(8,128)(2,1)S(1)} collective-permute-done((bf16[256,128]{1,0:T(8,128)(2,1)S(1)}, bf16[256,128]{1,0:T(8,128)(2,1)S(1)}, u32[]{:S(2)}, u32[]{:S(2)}) %collective-permute-start.8) | collective-permute-done | bytes 65568 | tf_op jit(solution)/shard_map/ppermute | solution.py:415
  44.5 0.8 shard_map.81
  45.2 1.4 %collective-permute-start.9 = (bf16[512,128]{1,0:T(8,128)(2,1)S(1)}, bf16[512,128]{1,0:T(8,128)(2,1)S(1)}, u32[]{:S(2)}, u32[]{:S(2)}) collective-permute-start(bf16[512,128]{1,0:T(8,128)(2,1)S(1)} %get-tuple-element.49), channel_id=1, source_target_pairs={{0,2},{2,4},{4,6},{6,0},{1,3},{3,5},{5,7},{7,1},{8,10},{10,12},{12... | collective-permute-start | bytes 393224 | tf_op jit(solution)/shard_map/ppermute | solution.py:409
  46.6 1.6 %collective-permute-start.10 = (bf16[512,128]{1,0:T(8,128)(2,1)S(1)}, bf16[512,128]{1,0:T(8,128)(2,1)S(1)}, u32[]{:S(2)}, u32[]{:S(2)}) collective-permute-start(bf16[512,128]{1,0:T(8,128)(2,1)S(1)} %get-tuple-element.50), channel_id=1, source_target_pairs={{0,4},{2,6},{4,0},{6,2},{1,5},{3,7},{5,1},{7,3},{8,12},{10,14},{12... | collective-permute-start | bytes 393224 | tf_op jit(solution)/shard_map/ppermute | solution.py:409
  48.1 1.6 %collective-permute-start.11 = (bf16[512,128]{1,0:T(8,128)(2,1)S(1)}, bf16[512,128]{1,0:T(8,128)(2,1)S(1)}, u32[]{:S(2)}, u32[]{:S(2)}) collective-permute-start(bf16[512,128]{1,0:T(8,128)(2,1)S(1)} %get-tuple-element.51), channel_id=1, source_target_pairs={{0,6},{2,0},{4,2},{6,4},{1,7},{3,1},{5,3},{7,5},{8,14},{10,8},{12,... | collective-permute-start | bytes 393224 | tf_op jit(solution)/shard_map/ppermute | solution.py:409
  49.7 2.2 %shard_map.73 = (f32[4,128,512]{2,1,0:T(8,128)S(1)}, bf16[4,128,8]{2,1,0:T(8,128)(2,1)S(1)}) custom-call(bf16[128,4096]{1,0:T(8,128)(2,1)S(1)} %bitcast.20, bf16[128,4096]{1,0:T(8,128)(2,1)S(1)} %bitcast.14, bf16[128,4096]{1,0:T(8,128)(2,1)S(1)} %bitcast.18, f32[32,128]{1,0:T(8,128)S(1)} %bitcast.28, s32[1,128]{1,0:T(1,128)S(1)} %copy-done.8), custom_call_target="tpu_custom_call" | custom-call | flops 134217728 | bytes 2621440 | tf_op jit(solution)/shard_map/pallas_call | solution.py:147
  52.0 1.2 %collective-permute-done.10.refs_4_ = bf16[512,128]{1,0:T(8,128)(2,1)S(1)} collective-permute-done((bf16[512,128]{1,0:T(8,128)(2,1)S(1)}, bf16[512,128]{1,0:T(8,128)(2,1)S(1)}, u32[]{:S(2)}, u32[]{:S(2)}) %collective-permute-start.10) | collective-permute-done | bytes 131104 | tf_op jit(solution)/shard_map/ppermute | solution.py:409
  53.2 1.3 %collective-permute-done.11.refs_5_ = bf16[512,128]{1,0:T(8,128)(2,1)S(1)} collective-permute-done((bf16[512,128]{1,0:T(8,128)(2,1)S(1)}, bf16[512,128]{1,0:T(8,128)(2,1)S(1)}, u32[]{:S(2)}, u32[]{:S(2)}) %collective-permute-start.11) | collective-permute-done | bytes 131104 | tf_op jit(solution)/shard_map/ppermute | solution.py:409
  54.5 0.8 shard_map.83
  55.3 0.1 collective-permute-start.12
  55.4 0.6 shard_map.82.refs_3_
  56.0 1.3 %collective-permute-done.12.refs_4_ = bf16[4,512,128]{2,1,0:T(8,128)(2,1)S(1)} collective-permute-done((bf16[4,512,128]{2,1,0:T(8,128)(2,1)S(1)}, bf16[4,512,128]{2,1,0:T(8,128)(2,1)S(1)}, u32[]{:S(2)}, u32[]{:S(2)}) %collective-permute-start.12) | collective-permute-done | bytes 524320 | tf_op jit(solution)/shard_map/ppermute | solution.py:419
  57.3 1.2 %shard_map.86 = (bf16[128,512]{1,0:T(8,128)(2,1)S(1)}, bf16[128,512]{1,0:T(8,128)(2,1)S(1)}, bf16[128,512]{1,0:T(8,128)(2,1)S(1)}, bf16[128,512]{1,0:T(8,128)(2,1)S(1)}) custom-call(s32[4]{0:T(128)S(1)} %pad_add_fusion.index, bf16[128,4096]{1,0:T(8,128)(2,1)S(1)} %bitcast.21, f32[4,128,512]{2,1,0:T(8,128)S(1)} %get-tuple-element.43.refs_4_.refs_1_, ...), custom_call_target="tpu_custom_call" | custom-call | flops 3162112 | bytes 6324224 | tf_op jit(solution)/shard_map/pallas_call | solution.py:203
  58.5 1.6 %collective-permute-start.19 = (bf16[128,512]{1,0:T(8,128)(2,1)S(1)}, bf16[128,512]{1,0:T(8,128)(2,1)S(1)}, u32[]{:S(2)}, u32[]{:S(2)}) collective-permute-start(bf16[128,512]{1,0:T(8,128)(2,1)S(1)} %get-tuple-element.62), channel_id=1, source_target_pairs={{0,64},{64,128},{128,192},{192,0},{1,65},{65,129},{129,193},{193,1... | collective-permute-start | bytes 393224 | tf_op jit(solution)/shard_map/ppermute | solution.py:409
  60.1 2.7 %collective-permute-start.20 = (bf16[128,512]{1,0:T(8,128)(2,1)S(1)}, bf16[128,512]{1,0:T(8,128)(2,1)S(1)}, u32[]{:S(2)}, u32[]{:S(2)}) collective-permute-start(bf16[128,512]{1,0:T(8,128)(2,1)S(1)} %get-tuple-element.63), channel_id=1, source_target_pairs={{0,128},{64,192},{128,0},{192,64},{1,129},{65,193},{129,1},{193,65... | collective-permute-start | bytes 393224 | tf_op jit(solution)/shard_map/ppermute | solution.py:409
  62.8 1.4 %collective-permute-start.21 = (bf16[128,512]{1,0:T(8,128)(2,1)S(1)}, bf16[128,512]{1,0:T(8,128)(2,1)S(1)}, u32[]{:S(2)}, u32[]{:S(2)}) collective-permute-start(bf16[128,512]{1,0:T(8,128)(2,1)S(1)} %get-tuple-element.64), channel_id=1, source_target_pairs={{0,192},{64,0},{128,64},{192,128},{1,193},{65,1},{129,65},{193,129... | collective-permute-start | bytes 393224 | tf_op jit(solution)/shard_map/ppermute | solution.py:409
  64.3 1.2 %shard_map.84 = (bf16[128,512]{1,0:T(8,128)(2,1)S(1)}, bf16[128,512]{1,0:T(8,128)(2,1)S(1)}, bf16[128,512]{1,0:T(8,128)(2,1)S(1)}, bf16[128,512]{1,0:T(8,128)(2,1)S(1)}) custom-call(s32[4]{0:T(128)S(1)} %pad_add_fusion.index, bf16[128,4096]{1,0:T(8,128)(2,1)S(1)} %bitcast.22, f32[4,128,512]{2,1,0:T(8,128)S(1)} %get-tuple-element.37.refs_6_.refs_1_, ...), custom_call_target="tpu_custom_call" | custom-call | flops 3162112 | bytes 6324224 | tf_op jit(solution)/shard_map/pallas_call | solution.py:203
  65.5 0.7 collective-permute-start.13
  66.2 0.9 collective-permute-start.14
  67.0 1.9 %collective-permute-start.15 = (bf16[128,512]{1,0:T(8,128)(2,1)S(1)}, bf16[128,512]{1,0:T(8,128)(2,1)S(1)}, u32[]{:S(2)}, u32[]{:S(2)}) collective-permute-start(bf16[128,512]{1,0:T(8,128)(2,1)S(1)} %get-tuple-element.55), channel_id=1, source_target_pairs={{0,192},{64,0},{128,64},{192,128},{1,193},{65,1},{129,65},{193,129... | collective-permute-start | bytes 393224 | tf_op jit(solution)/shard_map/ppermute | solution.py:409
  68.9 1.0 %collective-permute-done.20.refs_3_ = bf16[128,512]{1,0:T(8,128)(2,1)S(1)} collective-permute-done((bf16[128,512]{1,0:T(8,128)(2,1)S(1)}, bf16[128,512]{1,0:T(8,128)(2,1)S(1)}, u32[]{:S(2)}, u32[]{:S(2)}) %collective-permute-start.20) | collective-permute-done | bytes 131104 | tf_op jit(solution)/shard_map/ppermute | solution.py:409
  69.9 0.8 shard_map.87
  70.7 1.0 %collective-permute-start.22 = (bf16[128,512]{1,0:T(8,128)(2,1)S(1)}, bf16[128,512]{1,0:T(8,128)(2,1)S(1)}, u32[]{:S(2)}, u32[]{:S(2)}) collective-permute-start(bf16[128,512]{1,0:T(8,128)(2,1)S(1)} %get-tuple-element.66), channel_id=1, source_target_pairs={{0,64},{64,128},{128,192},{192,0},{1,65},{65,129},{129,193},{193,1... | collective-permute-start | bytes 393224 | tf_op jit(solution)/shard_map/ppermute | solution.py:409
  71.7 2.1 %collective-permute-start.23 = (bf16[128,512]{1,0:T(8,128)(2,1)S(1)}, bf16[128,512]{1,0:T(8,128)(2,1)S(1)}, u32[]{:S(2)}, u32[]{:S(2)}) collective-permute-start(bf16[128,512]{1,0:T(8,128)(2,1)S(1)} %get-tuple-element.67), channel_id=1, source_target_pairs={{0,128},{64,192},{128,0},{192,64},{1,129},{65,193},{129,1},{193,65... | collective-permute-start | bytes 393224 | tf_op jit(solution)/shard_map/ppermute | solution.py:409
  73.9 0.4 collective-permute-done.13.refs_2_
  74.3 2.1 %collective-permute-start.24 = (bf16[128,512]{1,0:T(8,128)(2,1)S(1)}, bf16[128,512]{1,0:T(8,128)(2,1)S(1)}, u32[]{:S(2)}, u32[]{:S(2)}) collective-permute-start(bf16[128,512]{1,0:T(8,128)(2,1)S(1)} %get-tuple-element.68), channel_id=1, source_target_pairs={{0,192},{64,0},{128,64},{192,128},{1,193},{65,1},{129,65},{193,129... | collective-permute-start | bytes 393224 | tf_op jit(solution)/shard_map/ppermute | solution.py:409
  76.4 0.8 shard_map.85
  77.2 1.6 %collective-permute-start.16 = (bf16[128,512]{1,0:T(8,128)(2,1)S(1)}, bf16[128,512]{1,0:T(8,128)(2,1)S(1)}, u32[]{:S(2)}, u32[]{:S(2)}) collective-permute-start(bf16[128,512]{1,0:T(8,128)(2,1)S(1)} %get-tuple-element.57), channel_id=1, source_target_pairs={{0,64},{64,128},{128,192},{192,0},{1,65},{65,129},{129,193},{193,1... | collective-permute-start | bytes 393224 | tf_op jit(solution)/shard_map/ppermute | solution.py:409
  78.8 2.6 %collective-permute-start.17 = (bf16[128,512]{1,0:T(8,128)(2,1)S(1)}, bf16[128,512]{1,0:T(8,128)(2,1)S(1)}, u32[]{:S(2)}, u32[]{:S(2)}) collective-permute-start(bf16[128,512]{1,0:T(8,128)(2,1)S(1)} %get-tuple-element.58), channel_id=1, source_target_pairs={{0,128},{64,192},{128,0},{192,64},{1,129},{65,193},{129,1},{193,65... | collective-permute-start | bytes 393224 | tf_op jit(solution)/shard_map/ppermute | solution.py:409
  81.4 0.6 collective-permute-start.18
  82.0 1.4 %shard_map.88.refs_4_ = bf16[128,4096]{1,0:T(8,128)(2,1)} custom-call(s32[4]{0:T(128)S(1)} %pad_add_fusion.index, bf16[128,512]{1,0:T(8,128)(2,1)S(1)} %get-tuple-element.65.refs_0_, bf16[128,512]{1,0:T(8,128)(2,1)S(1)} %collective-permute-done.22.refs_1_, bf16[128,512]{1,0:T(8,128)(2,1)S(1)} %collective-permute-done.23.refs_2_, ...), custom_call_target="tpu_custom_call" | custom-call | bytes 1048576 | tf_op jit(solution)/shard_map/pallas_call | solution.py:390
  83.4 1.4 %collective-permute-done.16.refs_1_ = bf16[128,512]{1,0:T(8,128)(2,1)S(1)} collective-permute-done((bf16[128,512]{1,0:T(8,128)(2,1)S(1)}, bf16[128,512]{1,0:T(8,128)(2,1)S(1)}, u32[]{:S(2)}, u32[]{:S(2)}) %collective-permute-start.16) | collective-permute-done | bytes 131104 | tf_op jit(solution)/shard_map/ppermute | solution.py:409
  84.8 1.4 %collective-permute-done.17.refs_2_ = bf16[128,512]{1,0:T(8,128)(2,1)S(1)} collective-permute-done((bf16[128,512]{1,0:T(8,128)(2,1)S(1)}, bf16[128,512]{1,0:T(8,128)(2,1)S(1)}, u32[]{:S(2)}, u32[]{:S(2)}) %collective-permute-start.17) | collective-permute-done | bytes 131104 | tf_op jit(solution)/shard_map/ppermute | solution.py:409
  86.2 0.2 collective-permute-done.18.refs_3_
  86.4 1.4 %shard_map.89 = bf16[128,4096]{1,0:T(8,128)(2,1)} custom-call(s32[4]{0:T(128)S(1)} %pad_add_fusion.index, bf16[128,512]{1,0:T(8,128)(2,1)S(1)} %get-tuple-element.56.refs_0_, bf16[128,512]{1,0:T(8,128)(2,1)S(1)} %collective-permute-done.16.refs_1_, bf16[128,512]{1,0:T(8,128)(2,1)S(1)} %collective-permute-done.17.refs_2_, ...), custom_call_target="tpu_custom_call", output_to_operand_aliasing={{}: (5, {})} | custom-call | bytes 1048576 | tf_op jit(solution)/shard_map/pallas_call | solution.py:390
  (22 shorter events, 0.1 us)
Async XLA Ops:
  0.0 0.7 copy-start.6
  0.1 0.7 copy-start.8
  0.7 1.2 %copy-start = (bf16[1,1,128,4096]{3,2,1,0:T(8,128)(2,1)S(1)}, bf16[1,1,128,4096]{3,2,1,0:T(8,128)(2,1)}, u32[]{:S(2)}) copy-start(bf16[1,1,128,4096]{3,2,1,0:T(8,128)(2,1)} %param.9) | copy-start | bytes 3145732
  2.0 1.2 %copy-start.2 = (bf16[1,1,128,4096]{3,2,1,0:T(8,128)(2,1)S(1)}, bf16[1,1,128,4096]{3,2,1,0:T(8,128)(2,1)}, u32[]{:S(2)}) copy-start(bf16[1,1,128,4096]{3,2,1,0:T(8,128)(2,1)} %param.10) | copy-start | bytes 3145732
  4.3 2.0 %collective-permute-start = (bf16[4,544,128]{2,1,0:T(8,128)(2,1)S(1)}, bf16[4,544,128]{2,1,0:T(8,128)(2,1)S(1)}, u32[]{:S(2)}, u32[]{:S(2)}) collective-permute-start(bf16[4,544,128]{2,1,0:T(8,128)(2,1)S(1)} %shard_map.75), channel_id=1, source_target_pairs={{0,1},{1,0},{2,3},{3,2},{4,5},{5,4},{6,7},{7,6},{8,9},{9,8},{10,11... | collective-permute-start | bytes 1671176 | tf_op jit(solution)/shard_map/ppermute | solution.py:419
  4.4 7.7 %copy-start.3 = (bf16[1,1,128,4096]{3,2,1,0:T(8,128)(2,1)S(1)}, bf16[1,1,128,4096]{3,2,1,0:T(8,128)(2,1)}, u32[]{:S(2)}) copy-start(bf16[1,1,128,4096]{3,2,1,0:T(8,128)(2,1)} %param.10) | copy-start | bytes 3145732
  4.4 7.7 %copy-start.4 = (bf16[1,1,128,4096]{3,2,1,0:T(8,128)(2,1)S(1)}, bf16[1,1,128,4096]{3,2,1,0:T(8,128)(2,1)}, u32[]{:S(2)}) copy-start(bf16[1,1,128,4096]{3,2,1,0:T(8,128)(2,1)} %param.8) | copy-start | bytes 3145732
  5.4 6.7 %copy-start.1 = (bf16[1,1,128,4096]{3,2,1,0:T(8,128)(2,1)S(1)}, bf16[1,1,128,4096]{3,2,1,0:T(8,128)(2,1)}, u32[]{:S(2)}) copy-start(bf16[1,1,128,4096]{3,2,1,0:T(8,128)(2,1)} %param.9) | copy-start | bytes 3145732
  7.1 7.2 %collective-permute-start.1 = (bf16[544,128]{1,0:T(8,128)(2,1)S(1)}, bf16[544,128]{1,0:T(8,128)(2,1)S(1)}, u32[]{:S(2)}, u32[]{:S(2)}) collective-permute-start(bf16[544,128]{1,0:T(8,128)(2,1)S(1)} %get-tuple-element.40), channel_id=1, source_target_pairs={{0,2},{2,4},{4,6},{6,0},{1,3},{3,5},{5,7},{7,1},{8,10},{10,12},{12... | collective-permute-start | bytes 417800 | tf_op jit(solution)/shard_map/ppermute | solution.py:409
  8.8 8.1 %collective-permute-start.2 = (bf16[544,128]{1,0:T(8,128)(2,1)S(1)}, bf16[544,128]{1,0:T(8,128)(2,1)S(1)}, u32[]{:S(2)}, u32[]{:S(2)}) collective-permute-start(bf16[544,128]{1,0:T(8,128)(2,1)S(1)} %get-tuple-element.41), channel_id=1, source_target_pairs={{0,4},{2,6},{4,0},{6,2},{1,5},{3,7},{5,1},{7,3},{8,12},{10,14},{12... | collective-permute-start | bytes 417800 | tf_op jit(solution)/shard_map/ppermute | solution.py:409
  11.4 7.2 %collective-permute-start.3 = (bf16[544,128]{1,0:T(8,128)(2,1)S(1)}, bf16[544,128]{1,0:T(8,128)(2,1)S(1)}, u32[]{:S(2)}, u32[]{:S(2)}) collective-permute-start(bf16[544,128]{1,0:T(8,128)(2,1)S(1)} %get-tuple-element.42), channel_id=1, source_target_pairs={{0,6},{2,0},{4,2},{6,4},{1,7},{3,1},{5,3},{7,5},{8,14},{10,8},{12,... | collective-permute-start | bytes 417800 | tf_op jit(solution)/shard_map/ppermute | solution.py:409
  19.4 4.4 %collective-permute-start.4 = (bf16[288,128]{1,0:T(8,128)(2,1)S(1)}, bf16[288,128]{1,0:T(8,128)(2,1)S(1)}, u32[]{:S(2)}, u32[]{:S(2)}) collective-permute-start(bf16[288,128]{1,0:T(8,128)(2,1)S(1)} %get-tuple-element.45), channel_id=1, source_target_pairs={{0,8},{8,0},{16,24},{24,16},{32,40},{40,32},{48,56},{56,48},{1,9},... | collective-permute-start | bytes 221192 | tf_op jit(solution)/shard_map/ppermute | solution.py:415
  24.4 13.1 %collective-permute-start.7 = (bf16[288,128]{1,0:T(8,128)(2,1)S(1)}, bf16[288,128]{1,0:T(8,128)(2,1)S(1)}, u32[]{:S(2)}, u32[]{:S(2)}) collective-permute-start(bf16[288,128]{1,0:T(8,128)(2,1)S(1)} %shard_map.79), channel_id=1, source_target_pairs={{0,48},{8,56},{1,49},{9,57},{2,50},{10,58},{3,51},{11,59},{4,52},{... | collective-permute-start | bytes 221192 | tf_op jit(solution)/shard_map/ppermute | solution.py:445
  31.9 5.6 %collective-permute-start.6 = (bf16[288,128]{1,0:T(8,128)(2,1)S(1)}, bf16[288,128]{1,0:T(8,128)(2,1)S(1)}, u32[]{:S(2)}, u32[]{:S(2)}) collective-permute-start(bf16[288,128]{1,0:T(8,128)(2,1)S(1)} %shard_map.79), channel_id=1, source_target_pairs={{0,32},{8,40},{16,48},{24,56},{1,33},{9,41},{17,49},{25,57},{2,34}... | collective-permute-start | bytes 221192 | tf_op jit(solution)/shard_map/ppermute | solution.py:445
  33.5 6.0 %collective-permute-start.5 = (bf16[288,128]{1,0:T(8,128)(2,1)S(1)}, bf16[288,128]{1,0:T(8,128)(2,1)S(1)}, u32[]{:S(2)}, u32[]{:S(2)}) collective-permute-start(bf16[288,128]{1,0:T(8,128)(2,1)S(1)} %shard_map.79), channel_id=1, source_target_pairs={{0,16},{8,24},{16,32},{24,40},{32,48},{40,56},{1,17},{9,25},{17,33... | collective-permute-start | bytes 221192 | tf_op jit(solution)/shard_map/ppermute | solution.py:445
  40.1 4.4 %collective-permute-start.8 = (bf16[256,128]{1,0:T(8,128)(2,1)S(1)}, bf16[256,128]{1,0:T(8,128)(2,1)S(1)}, u32[]{:S(2)}, u32[]{:S(2)}) collective-permute-start(bf16[256,128]{1,0:T(8,128)(2,1)S(1)} %get-tuple-element.47), channel_id=1, source_target_pairs={{0,8},{8,0},{16,24},{24,16},{32,40},{40,32},{48,56},{56,48},{1,9},... | collective-permute-start | bytes 196616 | tf_op jit(solution)/shard_map/ppermute | solution.py:415
  45.2 6.7 %collective-permute-start.9 = (bf16[512,128]{1,0:T(8,128)(2,1)S(1)}, bf16[512,128]{1,0:T(8,128)(2,1)S(1)}, u32[]{:S(2)}, u32[]{:S(2)}) collective-permute-start(bf16[512,128]{1,0:T(8,128)(2,1)S(1)} %get-tuple-element.49), channel_id=1, source_target_pairs={{0,2},{2,4},{4,6},{6,0},{1,3},{3,5},{5,7},{7,1},{8,10},{10,12},{12... | collective-permute-start | bytes 393224 | tf_op jit(solution)/shard_map/ppermute | solution.py:409
  46.6 6.6 %collective-permute-start.10 = (bf16[512,128]{1,0:T(8,128)(2,1)S(1)}, bf16[512,128]{1,0:T(8,128)(2,1)S(1)}, u32[]{:S(2)}, u32[]{:S(2)}) collective-permute-start(bf16[512,128]{1,0:T(8,128)(2,1)S(1)} %get-tuple-element.50), channel_id=1, source_target_pairs={{0,4},{2,6},{4,0},{6,2},{1,5},{3,7},{5,1},{7,3},{8,12},{10,14},{12... | collective-permute-start | bytes 393224 | tf_op jit(solution)/shard_map/ppermute | solution.py:409
  48.1 6.3 %collective-permute-start.11 = (bf16[512,128]{1,0:T(8,128)(2,1)S(1)}, bf16[512,128]{1,0:T(8,128)(2,1)S(1)}, u32[]{:S(2)}, u32[]{:S(2)}) collective-permute-start(bf16[512,128]{1,0:T(8,128)(2,1)S(1)} %get-tuple-element.51), channel_id=1, source_target_pairs={{0,6},{2,0},{4,2},{6,4},{1,7},{3,1},{5,3},{7,5},{8,14},{10,8},{12,... | collective-permute-start | bytes 393224 | tf_op jit(solution)/shard_map/ppermute | solution.py:409
  55.3 2.0 %copy-start.7 = (bf16[1,4096]{1,0:T(2,128)(2,1)S(1)}, bf16[1,4096]{1,0:T(2,128)(2,1)}, u32[]{:S(2)}) copy-start(bf16[1,4096]{1,0:T(2,128)(2,1)} %param.11) | copy-start | bytes 24580
  55.3 2.0 %collective-permute-start.12 = (bf16[4,512,128]{2,1,0:T(8,128)(2,1)S(1)}, bf16[4,512,128]{2,1,0:T(8,128)(2,1)S(1)}, u32[]{:S(2)}, u32[]{:S(2)}) collective-permute-start(bf16[4,512,128]{2,1,0:T(8,128)(2,1)S(1)} %shard_map.83), channel_id=1, source_target_pairs={{0,1},{1,0},{2,3},{3,2},{4,5},{5,4},{6,7},{7,6},{8,9},{9,8},{10,11... | collective-permute-start | bytes 1572872 | tf_op jit(solution)/shard_map/ppermute | solution.py:419
  58.5 8.5 %collective-permute-start.19 = (bf16[128,512]{1,0:T(8,128)(2,1)S(1)}, bf16[128,512]{1,0:T(8,128)(2,1)S(1)}, u32[]{:S(2)}, u32[]{:S(2)}) collective-permute-start(bf16[128,512]{1,0:T(8,128)(2,1)S(1)} %get-tuple-element.62), channel_id=1, source_target_pairs={{0,64},{64,128},{128,192},{192,0},{1,65},{65,129},{129,193},{193,1... | collective-permute-start | bytes 393224 | tf_op jit(solution)/shard_map/ppermute | solution.py:409
  60.1 9.9 %collective-permute-start.20 = (bf16[128,512]{1,0:T(8,128)(2,1)S(1)}, bf16[128,512]{1,0:T(8,128)(2,1)S(1)}, u32[]{:S(2)}, u32[]{:S(2)}) collective-permute-start(bf16[128,512]{1,0:T(8,128)(2,1)S(1)} %get-tuple-element.63), channel_id=1, source_target_pairs={{0,128},{64,192},{128,0},{192,64},{1,129},{65,193},{129,1},{193,65... | collective-permute-start | bytes 393224 | tf_op jit(solution)/shard_map/ppermute | solution.py:409
  62.8 7.1 %collective-permute-start.21 = (bf16[128,512]{1,0:T(8,128)(2,1)S(1)}, bf16[128,512]{1,0:T(8,128)(2,1)S(1)}, u32[]{:S(2)}, u32[]{:S(2)}) collective-permute-start(bf16[128,512]{1,0:T(8,128)(2,1)S(1)} %get-tuple-element.64), channel_id=1, source_target_pairs={{0,192},{64,0},{128,64},{192,128},{1,193},{65,1},{129,65},{193,129... | collective-permute-start | bytes 393224 | tf_op jit(solution)/shard_map/ppermute | solution.py:409
  64.3 5.7 %copy-start.5 = (bf16[1,128,1024]{2,1,0:T(8,128)(2,1)S(1)}, bf16[1,128,1024]{2,1,0:T(8,128)(2,1)}, u32[]{:S(2)}) copy-start(bf16[1,128,1024]{2,1,0:T(8,128)(2,1)} %param.7) | copy-start | bytes 786436
  65.5 8.8 %collective-permute-start.13 = (bf16[128,512]{1,0:T(8,128)(2,1)S(1)}, bf16[128,512]{1,0:T(8,128)(2,1)S(1)}, u32[]{:S(2)}, u32[]{:S(2)}) collective-permute-start(bf16[128,512]{1,0:T(8,128)(2,1)S(1)} %get-tuple-element.53), channel_id=1, source_target_pairs={{0,64},{64,128},{128,192},{192,0},{1,65},{65,129},{129,193},{193,1... | collective-permute-start | bytes 393224 | tf_op jit(solution)/shard_map/ppermute | solution.py:409
  66.2 10.2 %collective-permute-start.14 = (bf16[128,512]{1,0:T(8,128)(2,1)S(1)}, bf16[128,512]{1,0:T(8,128)(2,1)S(1)}, u32[]{:S(2)}, u32[]{:S(2)}) collective-permute-start(bf16[128,512]{1,0:T(8,128)(2,1)S(1)} %get-tuple-element.54), channel_id=1, source_target_pairs={{0,128},{64,192},{128,0},{192,64},{1,129},{65,193},{129,1},{193,65... | collective-permute-start | bytes 393224 | tf_op jit(solution)/shard_map/ppermute | solution.py:409
  67.0 9.4 %collective-permute-start.15 = (bf16[128,512]{1,0:T(8,128)(2,1)S(1)}, bf16[128,512]{1,0:T(8,128)(2,1)S(1)}, u32[]{:S(2)}, u32[]{:S(2)}) collective-permute-start(bf16[128,512]{1,0:T(8,128)(2,1)S(1)} %get-tuple-element.55), channel_id=1, source_target_pairs={{0,192},{64,0},{128,64},{192,128},{1,193},{65,1},{129,65},{193,129... | collective-permute-start | bytes 393224 | tf_op jit(solution)/shard_map/ppermute | solution.py:409
  70.7 10.7 %collective-permute-start.22 = (bf16[128,512]{1,0:T(8,128)(2,1)S(1)}, bf16[128,512]{1,0:T(8,128)(2,1)S(1)}, u32[]{:S(2)}, u32[]{:S(2)}) collective-permute-start(bf16[128,512]{1,0:T(8,128)(2,1)S(1)} %get-tuple-element.66), channel_id=1, source_target_pairs={{0,64},{64,128},{128,192},{192,0},{1,65},{65,129},{129,193},{193,1... | collective-permute-start | bytes 393224 | tf_op jit(solution)/shard_map/ppermute | solution.py:409
  71.7 10.3 %collective-permute-start.23 = (bf16[128,512]{1,0:T(8,128)(2,1)S(1)}, bf16[128,512]{1,0:T(8,128)(2,1)S(1)}, u32[]{:S(2)}, u32[]{:S(2)}) collective-permute-start(bf16[128,512]{1,0:T(8,128)(2,1)S(1)} %get-tuple-element.67), channel_id=1, source_target_pairs={{0,128},{64,192},{128,0},{192,64},{1,129},{65,193},{129,1},{193,65... | collective-permute-start | bytes 393224 | tf_op jit(solution)/shard_map/ppermute | solution.py:409
  74.3 7.8 %collective-permute-start.24 = (bf16[128,512]{1,0:T(8,128)(2,1)S(1)}, bf16[128,512]{1,0:T(8,128)(2,1)S(1)}, u32[]{:S(2)}, u32[]{:S(2)}) collective-permute-start(bf16[128,512]{1,0:T(8,128)(2,1)S(1)} %get-tuple-element.68), channel_id=1, source_target_pairs={{0,192},{64,0},{128,64},{192,128},{1,193},{65,1},{129,65},{193,129... | collective-permute-start | bytes 393224 | tf_op jit(solution)/shard_map/ppermute | solution.py:409
  77.2 7.6 %collective-permute-start.16 = (bf16[128,512]{1,0:T(8,128)(2,1)S(1)}, bf16[128,512]{1,0:T(8,128)(2,1)S(1)}, u32[]{:S(2)}, u32[]{:S(2)}) collective-permute-start(bf16[128,512]{1,0:T(8,128)(2,1)S(1)} %get-tuple-element.57), channel_id=1, source_target_pairs={{0,64},{64,128},{128,192},{192,0},{1,65},{65,129},{129,193},{193,1... | collective-permute-start | bytes 393224 | tf_op jit(solution)/shard_map/ppermute | solution.py:409
  78.8 7.4 %collective-permute-start.17 = (bf16[128,512]{1,0:T(8,128)(2,1)S(1)}, bf16[128,512]{1,0:T(8,128)(2,1)S(1)}, u32[]{:S(2)}, u32[]{:S(2)}) collective-permute-start(bf16[128,512]{1,0:T(8,128)(2,1)S(1)} %get-tuple-element.58), channel_id=1, source_target_pairs={{0,128},{64,192},{128,0},{192,64},{1,129},{65,193},{129,1},{193,65... | collective-permute-start | bytes 393224 | tf_op jit(solution)/shard_map/ppermute | solution.py:409
  81.4 5.0 %collective-permute-start.18 = (bf16[128,512]{1,0:T(8,128)(2,1)S(1)}, bf16[128,512]{1,0:T(8,128)(2,1)S(1)}, u32[]{:S(2)}, u32[]{:S(2)}) collective-permute-start(bf16[128,512]{1,0:T(8,128)(2,1)S(1)} %get-tuple-element.59), channel_id=1, source_target_pairs={{0,192},{64,0},{128,64},{192,128},{1,193},{65,1},{129,65},{193,129... | collective-permute-start | bytes 393224 | tf_op jit(solution)/shard_map/ppermute | solution.py:409

commit v5 on v4

--- a/solution.py
+++ b/solution.py
@@ -89,7 +89,7 @@
 
 def summaries(of_other, index, keys, values, decay, ids):
     whole = lambda shape: pl.BlockSpec(shape, lambda i, s: (0,) * len(shape))
-    block = pl.BlockSpec((D, HALF * D), lambda i, s: (0, 1 - s[CORE] if of_other else s[CORE]))
+    block = pl.BlockSpec((D, HALF * D), lambda i, s: (0, 0 if of_other else s[CORE]))
     return pl.pallas_call(
         functools.partial(summary_kernel, of_other),
         out_shape=jax.ShapeDtypeStruct((4, PART, D), BF16),
@@ -424,7 +424,9 @@
     queries, keys, values, decay = queries[0, 0], keys_in[0, 0], values[0, 0], log_decay[0, 0]
     gain = norm_gain.reshape(8, 1, ROWS)
 
-    other = swap_cores(summaries(True, index, keys, values, decay, doc_ids))
+    others_lanes = (1 - index[CORE]) * HALF * D
+    others = [lax.dynamic_slice_in_dim(array, others_lanes, HALF * D, 1) for array in (keys, values)]
+    other = swap_cores(summaries(True, index, *others, decay, doc_ids))
     own = summaries(False, index, keys, values, decay, doc_ids)
 
     part, group_states = ((PART, D), BF16), ((ROWS, D), BF16)
@@ -442,7 +444,7 @@
     )
     partner = swap_rows(send)
     (both,) = small_call(pair_kernel, index, [keep, partner], [pair])
-    before = [lax.ppermute(both, "z", [(i, i + by) for i in range(NZ - by)]) for by in (2, 4, 6)]
+    before = [lax.ppermute(both, "z", [(i, (i + by) % NZ) for i in range(NZ)]) for by in (2, 4, 6)]
     mine, send = small_call(prefix_kernel, index, [keep, partner, *before], [pair_states] * 2)
     spread = small_call(
         spread_kernel,

time: 88.3 us -> 86.1 us (0.975)
  starting transfers between devices: 45.1 us -> 40.1 us
  waiting for transfers between devices: 21 us -> 25.6 us
  local copies, waits for them, and re-layouts: 3.14 us -> 1.41 us
    ppermute x3, starting transfers between devices: 13.1 us -> 9.5 us  [local(): lax.ppermute(both, 'z', [(i, (i + by) % NZ) for i in range(NZ)])]
    ppermute x3, waiting for transfers between devices: 1.95 us -> 5.45 us  [local(): lax.ppermute(both, 'z', [(i, (i + by) % NZ) for i in range(NZ)])]
    unnamed x18 -> x14, local copies, waits for them, and re-layouts: 3.14 us -> 0.05 us
    dynamic_slice x0 -> x1, local copies, waits for them, and re-layouts: none -> 1.36 us  [local(): lax.dynamic_slice_in_dim(array, others_lanes, HALF * D, 1)]
    ppermute x2, starting transfers between devices: 3.13 us -> 1.79 us  [swap_rows(): return lax.ppermute(array, 'z', [(i, i ^ 1) for i in range(NZ)])]
    ppermute x2, waiting for transfers between devices: 5.66 us -> 7 us  [swap_rows(): return lax.ppermute(array, 'z', [(i, i ^ 1) for i in range(NZ)])]
  transfers between devices with their start and end apart: 25 -> 25, of which waited for: 14 -> 16; matrix products, arithmetic and copies ran while one was open for 0% -> 0% of each run, Pallas kernels for 12% -> 12%
where the time goes in v5:
time: 86.1 us; the launch traced here: 86 us
  starting transfers between devices  40.1 us (47%)
  waiting for transfers between devices  25.6 us (30%)
  Pallas kernels  18.3 us (21%)
  local copies, waits for them, and re-layouts  1.41 us (2%)
    ppermute x18, starting transfers between devices, ring_exchange(): lax.ppermute(slots[d], axis, [(i, (i + d) % size) for i in range(size)])  28.7 us
    ppermute x18, waiting for transfers between devices, ring_exchange(): lax.ppermute(slots[d], axis, [(i, (i + d) % size) for i in range(size)])  11.2 us
    ppermute x3, starting transfers between devices, local(): lax.ppermute(both, 'z', [(i, (i + by) % NZ) for i in range(NZ)])  9.5 us
    pallas_call x11, Pallas kernels, small_call(): pl.pallas_call(body, out_shape=[jax.ShapeDtypeStruct(shape, dtype) for sh...  9.05 us
    ppermute x2, waiting for transfers between devices, swap_rows(): return lax.ppermute(array, 'z', [(i, i ^ 1) for i in range(NZ)])  7 us
    ppermute x3, waiting for transfers between devices, local(): lax.ppermute(both, 'z', [(i, (i + by) % NZ) for i in range(NZ)])  5.45 us
    pallas_call x2, Pallas kernels, intra_term(): pl.pallas_call(functools.partial(intra_kernel, wave), out_shape=[jax.Shap...  4.44 us
    pallas_call x2, Pallas kernels, place(): pl.pallas_call(functools.partial(place_kernel, wave), out_shape=jax.Shape...  2.73 us
  transfers between devices with their start and end apart: 25, of which 16 were waited for; matrix products, arithmetic and copies ran while one was open for 0% of the time, Pallas kernels for 12%

profile of v5, /device:TPU:8, one launch (start us, length us, event | category | flops | bytes accessed | tf_op | source)
XLA Modules:
  0.0 86.0 jit_solution(13851575540081586289)
XLA Ops:
  0.0 1.4 %dynamic-slice_bitcast_fusion = (bf16[128,2048]{1,0:T(8,128)(2,1)S(1)}, bf16[128,2048]{1,0:T(8,128)(2,1)S(1)}) fusion(bf16[1,1,128,4096]{3,2,1,0:T(8,128)(2,1)} %param.10, s32[]{:T(128)S(6)} %select_n.4, bf16[1,1,128,4096]{3,2,1,0:T(8,128)(2,1)} %param.9), kind=kLoop, calls=%fused_computation | loop fusion | bytes 2097156 | tf_op jit(solution)/shard_map/dynamic_slice | solution.py:428
  1.4 0.0 copy-start.1
  1.4 0.1 pad_add_fusion.index
  1.5 1.0 %shard_map.75 = bf16[4,544,128]{2,1,0:T(8,128)(2,1)S(1)} custom-call(s32[4]{0:T(128)S(1)} %pad_add_fusion.index, bf16[128,2048]{1,0:T(8,128)(2,1)S(1)} %get-tuple-element.70.k_ref, bf16[128,2048]{1,0:T(8,128)(2,1)S(1)} %get-tuple-element.69.v_ref, f32[32,128]{1,0:T(8,128)S(1)} %bitcast.27, s32[1,128]{1,0:T(1,128)S(1)} %copy-done.6), custom_call_target="tpu_custom_call" | custom-call | flops 67108864 | bytes 1572864 | tf_op jit(solution)/shard_map/pallas_call | solution.py:93
  2.5 0.1 collective-permute-start
  2.6 0.0 copy-done.1
  2.7 1.1 %shard_map.74.refs_0_ = bf16[4,544,128]{2,1,0:T(8,128)(2,1)S(1)} custom-call(s32[4]{0:T(128)S(1)} %pad_add_fusion.index, bf16[128,4096]{1,0:T(8,128)(2,1)S(1)} %bitcast.19, bf16[128,4096]{1,0:T(8,128)(2,1)S(1)} %bitcast.22, f32[32,128]{1,0:T(8,128)S(1)} %bitcast.28, s32[1,128]{1,0:T(1,128)S(1)} %copy-done.6), custom_call_target="tpu_custom_call" | custom-call | flops 67108864 | bytes 1572864 | tf_op jit(solution)/shard_map/pallas_call | solution.py:93
  3.7 0.0 copy-start
  3.7 0.8 collective-permute-done.refs_1_
  4.6 0.8 shard_map.76
  5.4 1.7 %collective-permute-start.1 = (bf16[544,128]{1,0:T(8,128)(2,1)S(1)}, bf16[544,128]{1,0:T(8,128)(2,1)S(1)}, u32[]{:S(2)}, u32[]{:S(2)}) collective-permute-start(bf16[544,128]{1,0:T(8,128)(2,1)S(1)} %get-tuple-element.40), channel_id=1, source_target_pairs={{0,2},{2,4},{4,6},{6,0},{1,3},{3,5},{5,7},{7,1},{8,10},{10,12},{12... | collective-permute-start | bytes 417800 | tf_op jit(solution)/shard_map/ppermute | solution.py:409
  7.0 2.7 %collective-permute-start.2 = (bf16[544,128]{1,0:T(8,128)(2,1)S(1)}, bf16[544,128]{1,0:T(8,128)(2,1)S(1)}, u32[]{:S(2)}, u32[]{:S(2)}) collective-permute-start(bf16[544,128]{1,0:T(8,128)(2,1)S(1)} %get-tuple-element.41), channel_id=1, source_target_pairs={{0,4},{2,6},{4,0},{6,2},{1,5},{3,7},{5,1},{7,3},{8,12},{10,14},{12... | collective-permute-start | bytes 417800 | tf_op jit(solution)/shard_map/ppermute | solution.py:409
  9.7 0.7 collective-permute-start.3
  10.4 2.2 %shard_map.77 = (f32[4,128,512]{2,1,0:T(8,128)S(1)}, bf16[4,128,8]{2,1,0:T(8,128)(2,1)S(1)}) custom-call(bf16[128,4096]{1,0:T(8,128)(2,1)S(1)} %bitcast.15, bf16[128,4096]{1,0:T(8,128)(2,1)S(1)} %bitcast.20, bf16[128,4096]{1,0:T(8,128)(2,1)S(1)} %bitcast.23, f32[32,128]{1,0:T(8,128)S(1)} %bitcast.29, s32[1,128]{1,0:T(1,128)S(1)} %copy-done.6), custom_call_target="tpu_custom_call" | custom-call | flops 134217728 | bytes 2621440 | tf_op jit(solution)/shard_map/pallas_call | solution.py:147
  12.6 2.5 %collective-permute-done.2.refs_2_.refs_4_ = bf16[544,128]{1,0:T(8,128)(2,1)S(1)} collective-permute-done((bf16[544,128]{1,0:T(8,128)(2,1)S(1)}, bf16[544,128]{1,0:T(8,128)(2,1)S(1)}, u32[]{:S(2)}, u32[]{:S(2)}) %collective-permute-start.2) | collective-permute-done | bytes 139296 | tf_op jit(solution)/shard_map/ppermute | solution.py:409
  15.1 1.9 %collective-permute-done.3.refs_3_.refs_5_ = bf16[544,128]{1,0:T(8,128)(2,1)S(1)} collective-permute-done((bf16[544,128]{1,0:T(8,128)(2,1)S(1)}, bf16[544,128]{1,0:T(8,128)(2,1)S(1)}, u32[]{:S(2)}, u32[]{:S(2)}) %collective-permute-start.3) | collective-permute-done | bytes 139296 | tf_op jit(solution)/shard_map/ppermute | solution.py:409
  16.9 0.7 shard_map.78
  17.7 1.3 %collective-permute-start.4 = (bf16[288,128]{1,0:T(8,128)(2,1)S(1)}, bf16[288,128]{1,0:T(8,128)(2,1)S(1)}, u32[]{:S(2)}, u32[]{:S(2)}) collective-permute-start(bf16[288,128]{1,0:T(8,128)(2,1)S(1)} %get-tuple-element.45), channel_id=1, source_target_pairs={{0,8},{8,0},{16,24},{24,16},{32,40},{40,32},{48,56},{56,48},{1,9},... | collective-permute-start | bytes 221192 | tf_op jit(solution)/shard_map/ppermute | solution.py:415
  19.0 3.1 %collective-permute-done.4.refs_1_ = bf16[288,128]{1,0:T(8,128)(2,1)S(1)} collective-permute-done((bf16[288,128]{1,0:T(8,128)(2,1)S(1)}, bf16[288,128]{1,0:T(8,128)(2,1)S(1)}, u32[]{:S(2)}, u32[]{:S(2)}) %collective-permute-start.4) | collective-permute-done | bytes 73760 | tf_op jit(solution)/shard_map/ppermute | solution.py:415
  22.1 0.6 shard_map.79
  22.7 5.7 %collective-permute-start.7 = (bf16[288,128]{1,0:T(8,128)(2,1)S(1)}, bf16[288,128]{1,0:T(8,128)(2,1)S(1)}, u32[]{:S(2)}, u32[]{:S(2)}) collective-permute-start(bf16[288,128]{1,0:T(8,128)(2,1)S(1)} %shard_map.79), channel_id=1, source_target_pairs={{0,48},{8,56},{16,0},{24,8},{32,16},{40,24},{48,32},{56,40},{1,49}... | collective-permute-start | bytes 221192 | tf_op jit(solution)/shard_map/ppermute | solution.py:447
  28.4 1.0 %collective-permute-start.6 = (bf16[288,128]{1,0:T(8,128)(2,1)S(1)}, bf16[288,128]{1,0:T(8,128)(2,1)S(1)}, u32[]{:S(2)}, u32[]{:S(2)}) collective-permute-start(bf16[288,128]{1,0:T(8,128)(2,1)S(1)} %shard_map.79), channel_id=1, source_target_pairs={{0,32},{8,40},{16,48},{24,56},{32,0},{40,8},{48,16},{56,24},{1,33}... | collective-permute-start | bytes 221192 | tf_op jit(solution)/shard_map/ppermute | solution.py:447
  29.4 2.8 %collective-permute-start.5 = (bf16[288,128]{1,0:T(8,128)(2,1)S(1)}, bf16[288,128]{1,0:T(8,128)(2,1)S(1)}, u32[]{:S(2)}, u32[]{:S(2)}) collective-permute-start(bf16[288,128]{1,0:T(8,128)(2,1)S(1)} %shard_map.79), channel_id=1, source_target_pairs={{0,16},{8,24},{16,32},{24,40},{32,48},{40,56},{48,0},{56,8},{1,17}... | collective-permute-start | bytes 221192 | tf_op jit(solution)/shard_map/ppermute | solution.py:447
  32.2 0.5 collective-permute-done.7.refs_4_
  32.6 4.5 %collective-permute-done.6.refs_3_ = bf16[288,128]{1,0:T(8,128)(2,1)S(1)} collective-permute-done((bf16[288,128]{1,0:T(8,128)(2,1)S(1)}, bf16[288,128]{1,0:T(8,128)(2,1)S(1)}, u32[]{:S(2)}, u32[]{:S(2)}) %collective-permute-start.6) | collective-permute-done | bytes 73760 | tf_op jit(solution)/shard_map/ppermute | solution.py:447
  37.1 0.5 collective-permute-done.5.refs_2_
  37.6 0.6 shard_map.80
  38.3 0.5 collective-permute-start.8
  38.7 3.9 %collective-permute-done.8.refs_1_ = bf16[256,128]{1,0:T(8,128)(2,1)S(1)} collective-permute-done((bf16[256,128]{1,0:T(8,128)(2,1)S(1)}, bf16[256,128]{1,0:T(8,128)(2,1)S(1)}, u32[]{:S(2)}, u32[]{:S(2)}) %collective-permute-start.8) | collective-permute-done | bytes 65568 | tf_op jit(solution)/shard_map/ppermute | solution.py:415
  42.6 0.8 shard_map.81
  43.4 1.3 %collective-permute-start.9 = (bf16[512,128]{1,0:T(8,128)(2,1)S(1)}, bf16[512,128]{1,0:T(8,128)(2,1)S(1)}, u32[]{:S(2)}, u32[]{:S(2)}) collective-permute-start(bf16[512,128]{1,0:T(8,128)(2,1)S(1)} %get-tuple-element.49), channel_id=1, source_target_pairs={{0,2},{2,4},{4,6},{6,0},{1,3},{3,5},{5,7},{7,1},{8,10},{10,12},{12... | collective-permute-start | bytes 393224 | tf_op jit(solution)/shard_map/ppermute | solution.py:409
  44.7 1.6 %collective-permute-start.10 = (bf16[512,128]{1,0:T(8,128)(2,1)S(1)}, bf16[512,128]{1,0:T(8,128)(2,1)S(1)}, u32[]{:S(2)}, u32[]{:S(2)}) collective-permute-start(bf16[512,128]{1,0:T(8,128)(2,1)S(1)} %get-tuple-element.50), channel_id=1, source_target_pairs={{0,4},{2,6},{4,0},{6,2},{1,5},{3,7},{5,1},{7,3},{8,12},{10,14},{12... | collective-permute-start | bytes 393224 | tf_op jit(solution)/shard_map/ppermute | solution.py:409
  46.3 1.5 %collective-permute-start.11 = (bf16[512,128]{1,0:T(8,128)(2,1)S(1)}, bf16[512,128]{1,0:T(8,128)(2,1)S(1)}, u32[]{:S(2)}, u32[]{:S(2)}) collective-permute-start(bf16[512,128]{1,0:T(8,128)(2,1)S(1)} %get-tuple-element.51), channel_id=1, source_target_pairs={{0,6},{2,0},{4,2},{6,4},{1,7},{3,1},{5,3},{7,5},{8,14},{10,8},{12,... | collective-permute-start | bytes 393224 | tf_op jit(solution)/shard_map/ppermute | solution.py:409
  47.8 2.2 %shard_map.73 = (f32[4,128,512]{2,1,0:T(8,128)S(1)}, bf16[4,128,8]{2,1,0:T(8,128)(2,1)S(1)}) custom-call(bf16[128,4096]{1,0:T(8,128)(2,1)S(1)} %bitcast.16, bf16[128,4096]{1,0:T(8,128)(2,1)S(1)} %bitcast.21, bf16[128,4096]{1,0:T(8,128)(2,1)S(1)} %bitcast.24, f32[32,128]{1,0:T(8,128)S(1)} %bitcast.30, s32[1,128]{1,0:T(1,128)S(1)} %copy-done.6), custom_call_target="tpu_custom_call" | custom-call | flops 134217728 | bytes 2621440 | tf_op jit(solution)/shard_map/pallas_call | solution.py:147
  50.1 1.2 %collective-permute-done.10.refs_4_ = bf16[512,128]{1,0:T(8,128)(2,1)S(1)} collective-permute-done((bf16[512,128]{1,0:T(8,128)(2,1)S(1)}, bf16[512,128]{1,0:T(8,128)(2,1)S(1)}, u32[]{:S(2)}, u32[]{:S(2)}) %collective-permute-start.10) | collective-permute-done | bytes 131104 | tf_op jit(solution)/shard_map/ppermute | solution.py:409
  51.2 1.3 %collective-permute-done.11.refs_5_ = bf16[512,128]{1,0:T(8,128)(2,1)S(1)} collective-permute-done((bf16[512,128]{1,0:T(8,128)(2,1)S(1)}, bf16[512,128]{1,0:T(8,128)(2,1)S(1)}, u32[]{:S(2)}, u32[]{:S(2)}) %collective-permute-start.11) | collective-permute-done | bytes 131104 | tf_op jit(solution)/shard_map/ppermute | solution.py:409
  52.5 0.8 shard_map.83
  53.3 0.0 copy-start.5
  53.4 0.1 collective-permute-start.12
  53.5 0.8 shard_map.82.refs_3_
  54.2 1.1 %collective-permute-done.12.refs_4_ = bf16[4,512,128]{2,1,0:T(8,128)(2,1)S(1)} collective-permute-done((bf16[4,512,128]{2,1,0:T(8,128)(2,1)S(1)}, bf16[4,512,128]{2,1,0:T(8,128)(2,1)S(1)}, u32[]{:S(2)}, u32[]{:S(2)}) %collective-permute-start.12) | collective-permute-done | bytes 524320 | tf_op jit(solution)/shard_map/ppermute | solution.py:419
  55.4 1.2 %shard_map.86 = (bf16[128,512]{1,0:T(8,128)(2,1)S(1)}, bf16[128,512]{1,0:T(8,128)(2,1)S(1)}, bf16[128,512]{1,0:T(8,128)(2,1)S(1)}, bf16[128,512]{1,0:T(8,128)(2,1)S(1)}) custom-call(s32[4]{0:T(128)S(1)} %pad_add_fusion.index, bf16[128,4096]{1,0:T(8,128)(2,1)S(1)} %bitcast.17, f32[4,128,512]{2,1,0:T(8,128)S(1)} %get-tuple-element.43.refs_4_.refs_1_, ...), custom_call_target="tpu_custom_call" | custom-call | flops 3162112 | bytes 6324224 | tf_op jit(solution)/shard_map/pallas_call | solution.py:203
  56.6 1.6 %collective-permute-start.19 = (bf16[128,512]{1,0:T(8,128)(2,1)S(1)}, bf16[128,512]{1,0:T(8,128)(2,1)S(1)}, u32[]{:S(2)}, u32[]{:S(2)}) collective-permute-start(bf16[128,512]{1,0:T(8,128)(2,1)S(1)} %get-tuple-element.62), channel_id=1, source_target_pairs={{0,64},{64,128},{128,192},{192,0},{1,65},{65,129},{129,193},{193,1... | collective-permute-start | bytes 393224 | tf_op jit(solution)/shard_map/ppermute | solution.py:409
  58.2 2.7 %collective-permute-start.20 = (bf16[128,512]{1,0:T(8,128)(2,1)S(1)}, bf16[128,512]{1,0:T(8,128)(2,1)S(1)}, u32[]{:S(2)}, u32[]{:S(2)}) collective-permute-start(bf16[128,512]{1,0:T(8,128)(2,1)S(1)} %get-tuple-element.63), channel_id=1, source_target_pairs={{0,128},{64,192},{128,0},{192,64},{1,129},{65,193},{129,1},{193,65... | collective-permute-start | bytes 393224 | tf_op jit(solution)/shard_map/ppermute | solution.py:409
  60.9 1.4 %collective-permute-start.21 = (bf16[128,512]{1,0:T(8,128)(2,1)S(1)}, bf16[128,512]{1,0:T(8,128)(2,1)S(1)}, u32[]{:S(2)}, u32[]{:S(2)}) collective-permute-start(bf16[128,512]{1,0:T(8,128)(2,1)S(1)} %get-tuple-element.64), channel_id=1, source_target_pairs={{0,192},{64,0},{128,64},{192,128},{1,193},{65,1},{129,65},{193,129... | collective-permute-start | bytes 393224 | tf_op jit(solution)/shard_map/ppermute | solution.py:409
  62.3 1.2 %shard_map.84 = (bf16[128,512]{1,0:T(8,128)(2,1)S(1)}, bf16[128,512]{1,0:T(8,128)(2,1)S(1)}, bf16[128,512]{1,0:T(8,128)(2,1)S(1)}, bf16[128,512]{1,0:T(8,128)(2,1)S(1)}) custom-call(s32[4]{0:T(128)S(1)} %pad_add_fusion.index, bf16[128,4096]{1,0:T(8,128)(2,1)S(1)} %bitcast.18, f32[4,128,512]{2,1,0:T(8,128)S(1)} %get-tuple-element.37.refs_6_.refs_1_, ...), custom_call_target="tpu_custom_call" | custom-call | flops 3162112 | bytes 6324224 | tf_op jit(solution)/shard_map/pallas_call | solution.py:203
  63.5 0.7 collective-permute-start.13
  64.2 0.9 %collective-permute-start.14 = (bf16[128,512]{1,0:T(8,128)(2,1)S(1)}, bf16[128,512]{1,0:T(8,128)(2,1)S(1)}, u32[]{:S(2)}, u32[]{:S(2)}) collective-permute-start(bf16[128,512]{1,0:T(8,128)(2,1)S(1)} %get-tuple-element.54), channel_id=1, source_target_pairs={{0,128},{64,192},{128,0},{192,64},{1,129},{65,193},{129,1},{193,65... | collective-permute-start | bytes 393224 | tf_op jit(solution)/shard_map/ppermute | solution.py:409
  65.1 1.9 %collective-permute-start.15 = (bf16[128,512]{1,0:T(8,128)(2,1)S(1)}, bf16[128,512]{1,0:T(8,128)(2,1)S(1)}, u32[]{:S(2)}, u32[]{:S(2)}) collective-permute-start(bf16[128,512]{1,0:T(8,128)(2,1)S(1)} %get-tuple-element.55), channel_id=1, source_target_pairs={{0,192},{64,0},{128,64},{192,128},{1,193},{65,1},{129,65},{193,129... | collective-permute-start | bytes 393224 | tf_op jit(solution)/shard_map/ppermute | solution.py:409
  67.0 1.0 %collective-permute-done.20.refs_3_ = bf16[128,512]{1,0:T(8,128)(2,1)S(1)} collective-permute-done((bf16[128,512]{1,0:T(8,128)(2,1)S(1)}, bf16[128,512]{1,0:T(8,128)(2,1)S(1)}, u32[]{:S(2)}, u32[]{:S(2)}) %collective-permute-start.20) | collective-permute-done | bytes 131104 | tf_op jit(solution)/shard_map/ppermute | solution.py:409
  68.0 0.8 shard_map.87
  68.8 0.9 %collective-permute-start.22 = (bf16[128,512]{1,0:T(8,128)(2,1)S(1)}, bf16[128,512]{1,0:T(8,128)(2,1)S(1)}, u32[]{:S(2)}, u32[]{:S(2)}) collective-permute-start(bf16[128,512]{1,0:T(8,128)(2,1)S(1)} %get-tuple-element.66), channel_id=1, source_target_pairs={{0,64},{64,128},{128,192},{192,0},{1,65},{65,129},{129,193},{193,1... | collective-permute-start | bytes 393224 | tf_op jit(solution)/shard_map/ppermute | solution.py:409
  69.8 2.2 %collective-permute-start.23 = (bf16[128,512]{1,0:T(8,128)(2,1)S(1)}, bf16[128,512]{1,0:T(8,128)(2,1)S(1)}, u32[]{:S(2)}, u32[]{:S(2)}) collective-permute-start(bf16[128,512]{1,0:T(8,128)(2,1)S(1)} %get-tuple-element.67), channel_id=1, source_target_pairs={{0,128},{64,192},{128,0},{192,64},{1,129},{65,193},{129,1},{193,65... | collective-permute-start | bytes 393224 | tf_op jit(solution)/shard_map/ppermute | solution.py:409
  71.9 0.4 collective-permute-done.13.refs_2_
  72.3 2.1 %collective-permute-start.24 = (bf16[128,512]{1,0:T(8,128)(2,1)S(1)}, bf16[128,512]{1,0:T(8,128)(2,1)S(1)}, u32[]{:S(2)}, u32[]{:S(2)}) collective-permute-start(bf16[128,512]{1,0:T(8,128)(2,1)S(1)} %get-tuple-element.68), channel_id=1, source_target_pairs={{0,192},{64,0},{128,64},{192,128},{1,193},{65,1},{129,65},{193,129... | collective-permute-start | bytes 393224 | tf_op jit(solution)/shard_map/ppermute | solution.py:409
  74.5 0.8 shard_map.85
  75.3 1.6 %collective-permute-start.16 = (bf16[128,512]{1,0:T(8,128)(2,1)S(1)}, bf16[128,512]{1,0:T(8,128)(2,1)S(1)}, u32[]{:S(2)}, u32[]{:S(2)}) collective-permute-start(bf16[128,512]{1,0:T(8,128)(2,1)S(1)} %get-tuple-element.57), channel_id=1, source_target_pairs={{0,64},{64,128},{128,192},{192,0},{1,65},{65,129},{129,193},{193,1... | collective-permute-start | bytes 393224 | tf_op jit(solution)/shard_map/ppermute | solution.py:409
  76.9 2.6 %collective-permute-start.17 = (bf16[128,512]{1,0:T(8,128)(2,1)S(1)}, bf16[128,512]{1,0:T(8,128)(2,1)S(1)}, u32[]{:S(2)}, u32[]{:S(2)}) collective-permute-start(bf16[128,512]{1,0:T(8,128)(2,1)S(1)} %get-tuple-element.58), channel_id=1, source_target_pairs={{0,128},{64,192},{128,0},{192,64},{1,129},{65,193},{129,1},{193,65... | collective-permute-start | bytes 393224 | tf_op jit(solution)/shard_map/ppermute | solution.py:409
  79.5 0.6 collective-permute-start.18
  80.1 1.4 %shard_map.88.refs_4_ = bf16[128,4096]{1,0:T(8,128)(2,1)} custom-call(s32[4]{0:T(128)S(1)} %pad_add_fusion.index, bf16[128,512]{1,0:T(8,128)(2,1)S(1)} %get-tuple-element.65.refs_0_, bf16[128,512]{1,0:T(8,128)(2,1)S(1)} %collective-permute-done.22.refs_1_, bf16[128,512]{1,0:T(8,128)(2,1)S(1)} %collective-permute-done.23.refs_2_, ...), custom_call_target="tpu_custom_call" | custom-call | bytes 1048576 | tf_op jit(solution)/shard_map/pallas_call | solution.py:390
  81.4 1.4 %collective-permute-done.16.refs_1_ = bf16[128,512]{1,0:T(8,128)(2,1)S(1)} collective-permute-done((bf16[128,512]{1,0:T(8,128)(2,1)S(1)}, bf16[128,512]{1,0:T(8,128)(2,1)S(1)}, u32[]{:S(2)}, u32[]{:S(2)}) %collective-permute-start.16) | collective-permute-done | bytes 131104 | tf_op jit(solution)/shard_map/ppermute | solution.py:409
  82.8 1.4 %collective-permute-done.17.refs_2_ = bf16[128,512]{1,0:T(8,128)(2,1)S(1)} collective-permute-done((bf16[128,512]{1,0:T(8,128)(2,1)S(1)}, bf16[128,512]{1,0:T(8,128)(2,1)S(1)}, u32[]{:S(2)}, u32[]{:S(2)}) %collective-permute-start.17) | collective-permute-done | bytes 131104 | tf_op jit(solution)/shard_map/ppermute | solution.py:409
  84.2 0.2 collective-permute-done.18.refs_3_
  84.4 1.4 %shard_map.89 = bf16[128,4096]{1,0:T(8,128)(2,1)} custom-call(s32[4]{0:T(128)S(1)} %pad_add_fusion.index, bf16[128,512]{1,0:T(8,128)(2,1)S(1)} %get-tuple-element.56.refs_0_, bf16[128,512]{1,0:T(8,128)(2,1)S(1)} %collective-permute-done.16.refs_1_, bf16[128,512]{1,0:T(8,128)(2,1)S(1)} %collective-permute-done.17.refs_2_, ...), custom_call_target="tpu_custom_call", output_to_operand_aliasing={{}: (5, {})} | custom-call | bytes 1048576 | tf_op jit(solution)/shard_map/pallas_call | solution.py:390
  (19 shorter events, 0.0 us)
Async XLA Ops:
  0.0 1.5 %copy-start.4 = (f32[1,1,32,128]{3,2,1,0:T(8,128)S(1)}, f32[1,1,32,128]{3,2,1,0:T(8,128)}, u32[]{:S(2)}) copy-start(f32[1,1,32,128]{3,2,1,0:T(8,128)} %param.12) | copy-start | bytes 49156
  0.0 1.5 %copy-start.6 = (s32[1,128]{1,0:T(1,128)S(1)}, s32[1,128]{1,0:T(1,128)}, u32[]{:S(2)}) copy-start(s32[1,128]{1,0:T(1,128)} %ids_ref.7) | copy-start | bytes 1540
  0.0 2.6 %copy-start.2 = (bf16[1,1,128,4096]{3,2,1,0:T(8,128)(2,1)S(1)}, bf16[1,1,128,4096]{3,2,1,0:T(8,128)(2,1)}, u32[]{:S(2)}) copy-start(bf16[1,1,128,4096]{3,2,1,0:T(8,128)(2,1)} %param.10) | copy-start | bytes 3145732
  1.4 1.3 %copy-start.1 = (bf16[1,1,128,4096]{3,2,1,0:T(8,128)(2,1)S(1)}, bf16[1,1,128,4096]{3,2,1,0:T(8,128)(2,1)}, u32[]{:S(2)}) copy-start(bf16[1,1,128,4096]{3,2,1,0:T(8,128)(2,1)} %param.9) | copy-start | bytes 3145732
  2.5 2.0 %collective-permute-start = (bf16[4,544,128]{2,1,0:T(8,128)(2,1)S(1)}, bf16[4,544,128]{2,1,0:T(8,128)(2,1)S(1)}, u32[]{:S(2)}, u32[]{:S(2)}) collective-permute-start(bf16[4,544,128]{2,1,0:T(8,128)(2,1)S(1)} %shard_map.75), channel_id=1, source_target_pairs={{0,1},{1,0},{2,3},{3,2},{4,5},{5,4},{6,7},{7,6},{8,9},{9,8},{10,11... | collective-permute-start | bytes 1671176 | tf_op jit(solution)/shard_map/ppermute | solution.py:419
  3.7 6.6 %copy-start = (bf16[1,1,128,4096]{3,2,1,0:T(8,128)(2,1)S(1)}, bf16[1,1,128,4096]{3,2,1,0:T(8,128)(2,1)}, u32[]{:S(2)}) copy-start(bf16[1,1,128,4096]{3,2,1,0:T(8,128)(2,1)} %param.8) | copy-start | bytes 3145732
  5.4 7.2 %collective-permute-start.1 = (bf16[544,128]{1,0:T(8,128)(2,1)S(1)}, bf16[544,128]{1,0:T(8,128)(2,1)S(1)}, u32[]{:S(2)}, u32[]{:S(2)}) collective-permute-start(bf16[544,128]{1,0:T(8,128)(2,1)S(1)} %get-tuple-element.40), channel_id=1, source_target_pairs={{0,2},{2,4},{4,6},{6,0},{1,3},{3,5},{5,7},{7,1},{8,10},{10,12},{12... | collective-permute-start | bytes 417800 | tf_op jit(solution)/shard_map/ppermute | solution.py:409
  7.0 8.1 %collective-permute-start.2 = (bf16[544,128]{1,0:T(8,128)(2,1)S(1)}, bf16[544,128]{1,0:T(8,128)(2,1)S(1)}, u32[]{:S(2)}, u32[]{:S(2)}) collective-permute-start(bf16[544,128]{1,0:T(8,128)(2,1)S(1)} %get-tuple-element.41), channel_id=1, source_target_pairs={{0,4},{2,6},{4,0},{6,2},{1,5},{3,7},{5,1},{7,3},{8,12},{10,14},{12... | collective-permute-start | bytes 417800 | tf_op jit(solution)/shard_map/ppermute | solution.py:409
  9.7 7.3 %collective-permute-start.3 = (bf16[544,128]{1,0:T(8,128)(2,1)S(1)}, bf16[544,128]{1,0:T(8,128)(2,1)S(1)}, u32[]{:S(2)}, u32[]{:S(2)}) collective-permute-start(bf16[544,128]{1,0:T(8,128)(2,1)S(1)} %get-tuple-element.42), channel_id=1, source_target_pairs={{0,6},{2,0},{4,2},{6,4},{1,7},{3,1},{5,3},{7,5},{8,14},{10,8},{12,... | collective-permute-start | bytes 417800 | tf_op jit(solution)/shard_map/ppermute | solution.py:409
  17.7 4.4 %collective-permute-start.4 = (bf16[288,128]{1,0:T(8,128)(2,1)S(1)}, bf16[288,128]{1,0:T(8,128)(2,1)S(1)}, u32[]{:S(2)}, u32[]{:S(2)}) collective-permute-start(bf16[288,128]{1,0:T(8,128)(2,1)S(1)} %get-tuple-element.45), channel_id=1, source_target_pairs={{0,8},{8,0},{16,24},{24,16},{32,40},{40,32},{48,56},{56,48},{1,9},... | collective-permute-start | bytes 221192 | tf_op jit(solution)/shard_map/ppermute | solution.py:415
  22.7 10.0 %collective-permute-start.7 = (bf16[288,128]{1,0:T(8,128)(2,1)S(1)}, bf16[288,128]{1,0:T(8,128)(2,1)S(1)}, u32[]{:S(2)}, u32[]{:S(2)}) collective-permute-start(bf16[288,128]{1,0:T(8,128)(2,1)S(1)} %shard_map.79), channel_id=1, source_target_pairs={{0,48},{8,56},{16,0},{24,8},{32,16},{40,24},{48,32},{56,40},{1,49}... | collective-permute-start | bytes 221192 | tf_op jit(solution)/shard_map/ppermute | solution.py:447
  28.4 8.8 %collective-permute-start.6 = (bf16[288,128]{1,0:T(8,128)(2,1)S(1)}, bf16[288,128]{1,0:T(8,128)(2,1)S(1)}, u32[]{:S(2)}, u32[]{:S(2)}) collective-permute-start(bf16[288,128]{1,0:T(8,128)(2,1)S(1)} %shard_map.79), channel_id=1, source_target_pairs={{0,32},{8,40},{16,48},{24,56},{32,0},{40,8},{48,16},{56,24},{1,33}... | collective-permute-start | bytes 221192 | tf_op jit(solution)/shard_map/ppermute | solution.py:447
  29.4 8.3 %collective-permute-start.5 = (bf16[288,128]{1,0:T(8,128)(2,1)S(1)}, bf16[288,128]{1,0:T(8,128)(2,1)S(1)}, u32[]{:S(2)}, u32[]{:S(2)}) collective-permute-start(bf16[288,128]{1,0:T(8,128)(2,1)S(1)} %shard_map.79), channel_id=1, source_target_pairs={{0,16},{8,24},{16,32},{24,40},{32,48},{40,56},{48,0},{56,8},{1,17}... | collective-permute-start | bytes 221192 | tf_op jit(solution)/shard_map/ppermute | solution.py:447
  38.3 4.4 %collective-permute-start.8 = (bf16[256,128]{1,0:T(8,128)(2,1)S(1)}, bf16[256,128]{1,0:T(8,128)(2,1)S(1)}, u32[]{:S(2)}, u32[]{:S(2)}) collective-permute-start(bf16[256,128]{1,0:T(8,128)(2,1)S(1)} %get-tuple-element.47), channel_id=1, source_target_pairs={{0,8},{8,0},{16,24},{24,16},{32,40},{40,32},{48,56},{56,48},{1,9},... | collective-permute-start | bytes 196616 | tf_op jit(solution)/shard_map/ppermute | solution.py:415
  43.4 6.7 %collective-permute-start.9 = (bf16[512,128]{1,0:T(8,128)(2,1)S(1)}, bf16[512,128]{1,0:T(8,128)(2,1)S(1)}, u32[]{:S(2)}, u32[]{:S(2)}) collective-permute-start(bf16[512,128]{1,0:T(8,128)(2,1)S(1)} %get-tuple-element.49), channel_id=1, source_target_pairs={{0,2},{2,4},{4,6},{6,0},{1,3},{3,5},{5,7},{7,1},{8,10},{10,12},{12... | collective-permute-start | bytes 393224 | tf_op jit(solution)/shard_map/ppermute | solution.py:409
  44.7 6.6 %collective-permute-start.10 = (bf16[512,128]{1,0:T(8,128)(2,1)S(1)}, bf16[512,128]{1,0:T(8,128)(2,1)S(1)}, u32[]{:S(2)}, u32[]{:S(2)}) collective-permute-start(bf16[512,128]{1,0:T(8,128)(2,1)S(1)} %get-tuple-element.50), channel_id=1, source_target_pairs={{0,4},{2,6},{4,0},{6,2},{1,5},{3,7},{5,1},{7,3},{8,12},{10,14},{12... | collective-permute-start | bytes 393224 | tf_op jit(solution)/shard_map/ppermute | solution.py:409
  46.3 6.2 %collective-permute-start.11 = (bf16[512,128]{1,0:T(8,128)(2,1)S(1)}, bf16[512,128]{1,0:T(8,128)(2,1)S(1)}, u32[]{:S(2)}, u32[]{:S(2)}) collective-permute-start(bf16[512,128]{1,0:T(8,128)(2,1)S(1)} %get-tuple-element.51), channel_id=1, source_target_pairs={{0,6},{2,0},{4,2},{6,4},{1,7},{3,1},{5,3},{7,5},{8,14},{10,8},{12,... | collective-permute-start | bytes 393224 | tf_op jit(solution)/shard_map/ppermute | solution.py:409
  53.3 2.0 %copy-start.5 = (bf16[1,4096]{1,0:T(2,128)(2,1)S(1)}, bf16[1,4096]{1,0:T(2,128)(2,1)}, u32[]{:S(2)}) copy-start(bf16[1,4096]{1,0:T(2,128)(2,1)} %param.11) | copy-start | bytes 24580
  53.4 2.0 %collective-permute-start.12 = (bf16[4,512,128]{2,1,0:T(8,128)(2,1)S(1)}, bf16[4,512,128]{2,1,0:T(8,128)(2,1)S(1)}, u32[]{:S(2)}, u32[]{:S(2)}) collective-permute-start(bf16[4,512,128]{2,1,0:T(8,128)(2,1)S(1)} %shard_map.83), channel_id=1, source_target_pairs={{0,1},{1,0},{2,3},{3,2},{4,5},{5,4},{6,7},{7,6},{8,9},{9,8},{10,11... | collective-permute-start | bytes 1572872 | tf_op jit(solution)/shard_map/ppermute | solution.py:419
  56.6 8.5 %collective-permute-start.19 = (bf16[128,512]{1,0:T(8,128)(2,1)S(1)}, bf16[128,512]{1,0:T(8,128)(2,1)S(1)}, u32[]{:S(2)}, u32[]{:S(2)}) collective-permute-start(bf16[128,512]{1,0:T(8,128)(2,1)S(1)} %get-tuple-element.62), channel_id=1, source_target_pairs={{0,64},{64,128},{128,192},{192,0},{1,65},{65,129},{129,193},{193,1... | collective-permute-start | bytes 393224 | tf_op jit(solution)/shard_map/ppermute | solution.py:409
  58.2 9.9 %collective-permute-start.20 = (bf16[128,512]{1,0:T(8,128)(2,1)S(1)}, bf16[128,512]{1,0:T(8,128)(2,1)S(1)}, u32[]{:S(2)}, u32[]{:S(2)}) collective-permute-start(bf16[128,512]{1,0:T(8,128)(2,1)S(1)} %get-tuple-element.63), channel_id=1, source_target_pairs={{0,128},{64,192},{128,0},{192,64},{1,129},{65,193},{129,1},{193,65... | collective-permute-start | bytes 393224 | tf_op jit(solution)/shard_map/ppermute | solution.py:409
  60.9 7.1 %collective-permute-start.21 = (bf16[128,512]{1,0:T(8,128)(2,1)S(1)}, bf16[128,512]{1,0:T(8,128)(2,1)S(1)}, u32[]{:S(2)}, u32[]{:S(2)}) collective-permute-start(bf16[128,512]{1,0:T(8,128)(2,1)S(1)} %get-tuple-element.64), channel_id=1, source_target_pairs={{0,192},{64,0},{128,64},{192,128},{1,193},{65,1},{129,65},{193,129... | collective-permute-start | bytes 393224 | tf_op jit(solution)/shard_map/ppermute | solution.py:409
  62.3 5.7 %copy-start.3 = (bf16[1,128,1024]{2,1,0:T(8,128)(2,1)S(1)}, bf16[1,128,1024]{2,1,0:T(8,128)(2,1)}, u32[]{:S(2)}) copy-start(bf16[1,128,1024]{2,1,0:T(8,128)(2,1)} %param.7) | copy-start | bytes 786436
  63.5 8.8 %collective-permute-start.13 = (bf16[128,512]{1,0:T(8,128)(2,1)S(1)}, bf16[128,512]{1,0:T(8,128)(2,1)S(1)}, u32[]{:S(2)}, u32[]{:S(2)}) collective-permute-start(bf16[128,512]{1,0:T(8,128)(2,1)S(1)} %get-tuple-element.53), channel_id=1, source_target_pairs={{0,64},{64,128},{128,192},{192,0},{1,65},{65,129},{129,193},{193,1... | collective-permute-start | bytes 393224 | tf_op jit(solution)/shard_map/ppermute | solution.py:409
  64.2 10.2 %collective-permute-start.14 = (bf16[128,512]{1,0:T(8,128)(2,1)S(1)}, bf16[128,512]{1,0:T(8,128)(2,1)S(1)}, u32[]{:S(2)}, u32[]{:S(2)}) collective-permute-start(bf16[128,512]{1,0:T(8,128)(2,1)S(1)} %get-tuple-element.54), channel_id=1, source_target_pairs={{0,128},{64,192},{128,0},{192,64},{1,129},{65,193},{129,1},{193,65... | collective-permute-start | bytes 393224 | tf_op jit(solution)/shard_map/ppermute | solution.py:409
  65.1 9.4 %collective-permute-start.15 = (bf16[128,512]{1,0:T(8,128)(2,1)S(1)}, bf16[128,512]{1,0:T(8,128)(2,1)S(1)}, u32[]{:S(2)}, u32[]{:S(2)}) collective-permute-start(bf16[128,512]{1,0:T(8,128)(2,1)S(1)} %get-tuple-element.55), channel_id=1, source_target_pairs={{0,192},{64,0},{128,64},{192,128},{1,193},{65,1},{129,65},{193,129... | collective-permute-start | bytes 393224 | tf_op jit(solution)/shard_map/ppermute | solution.py:409
  68.8 10.7 %collective-permute-start.22 = (bf16[128,512]{1,0:T(8,128)(2,1)S(1)}, bf16[128,512]{1,0:T(8,128)(2,1)S(1)}, u32[]{:S(2)}, u32[]{:S(2)}) collective-permute-start(bf16[128,512]{1,0:T(8,128)(2,1)S(1)} %get-tuple-element.66), channel_id=1, source_target_pairs={{0,64},{64,128},{128,192},{192,0},{1,65},{65,129},{129,193},{193,1... | collective-permute-start | bytes 393224 | tf_op jit(solution)/shard_map/ppermute | solution.py:409
  69.8 10.3 %collective-permute-start.23 = (bf16[128,512]{1,0:T(8,128)(2,1)S(1)}, bf16[128,512]{1,0:T(8,128)(2,1)S(1)}, u32[]{:S(2)}, u32[]{:S(2)}) collective-permute-start(bf16[128,512]{1,0:T(8,128)(2,1)S(1)} %get-tuple-element.67), channel_id=1, source_target_pairs={{0,128},{64,192},{128,0},{192,64},{1,129},{65,193},{129,1},{193,65... | collective-permute-start | bytes 393224 | tf_op jit(solution)/shard_map/ppermute | solution.py:409
  72.3 7.8 %collective-permute-start.24 = (bf16[128,512]{1,0:T(8,128)(2,1)S(1)}, bf16[128,512]{1,0:T(8,128)(2,1)S(1)}, u32[]{:S(2)}, u32[]{:S(2)}) collective-permute-start(bf16[128,512]{1,0:T(8,128)(2,1)S(1)} %get-tuple-element.68), channel_id=1, source_target_pairs={{0,192},{64,0},{128,64},{192,128},{1,193},{65,1},{129,65},{193,129... | collective-permute-start | bytes 393224 | tf_op jit(solution)/shard_map/ppermute | solution.py:409
  75.3 7.6 %collective-permute-start.16 = (bf16[128,512]{1,0:T(8,128)(2,1)S(1)}, bf16[128,512]{1,0:T(8,128)(2,1)S(1)}, u32[]{:S(2)}, u32[]{:S(2)}) collective-permute-start(bf16[128,512]{1,0:T(8,128)(2,1)S(1)} %get-tuple-element.57), channel_id=1, source_target_pairs={{0,64},{64,128},{128,192},{192,0},{1,65},{65,129},{129,193},{193,1... | collective-permute-start | bytes 393224 | tf_op jit(solution)/shard_map/ppermute | solution.py:409
  76.9 7.4 %collective-permute-start.17 = (bf16[128,512]{1,0:T(8,128)(2,1)S(1)}, bf16[128,512]{1,0:T(8,128)(2,1)S(1)}, u32[]{:S(2)}, u32[]{:S(2)}) collective-permute-start(bf16[128,512]{1,0:T(8,128)(2,1)S(1)} %get-tuple-element.58), channel_id=1, source_target_pairs={{0,128},{64,192},{128,0},{192,64},{1,129},{65,193},{129,1},{193,65... | collective-permute-start | bytes 393224 | tf_op jit(solution)/shard_map/ppermute | solution.py:409
  79.5 5.0 %collective-permute-start.18 = (bf16[128,512]{1,0:T(8,128)(2,1)S(1)}, bf16[128,512]{1,0:T(8,128)(2,1)S(1)}, u32[]{:S(2)}, u32[]{:S(2)}) collective-permute-start(bf16[128,512]{1,0:T(8,128)(2,1)S(1)} %get-tuple-element.59), channel_id=1, source_target_pairs={{0,192},{64,0},{128,64},{192,128},{1,193},{65,1},{129,65},{193,129... | collective-permute-start | bytes 393224 | tf_op jit(solution)/shard_map/ppermute | solution.py:409

commit v6 on v5

--- a/solution.py
+++ b/solution.py
@@ -74,11 +74,13 @@
     total = nt(three_parts(decay), jnp.ones((D, 3 * D), BF16))
     carried = jnp.exp(total - running_sums(decay)) * same(ids, last)
     for group in range(4):
+        group_lanes = slice(group * ROWS, (group + 1) * ROWS)
+        keys, values = k_ref[:, group_lanes], v_ref[:, group_lanes]
         for i in range(GROUP):
             h = group * GROUP + i
-            lanes = slice(h * D, (h + 1) * D)
-            keyed = (jnp.transpose(k_ref[:, lanes].astype(F32)) * carried[h : h + 1]).astype(BF16)
-            state = jnp.dot(keyed, v_ref[:, lanes], preferred_element_type=F32)
+            lanes = slice(i * D, (i + 1) * D)
+            keyed = (jnp.transpose(keys[:, lanes].astype(F32)) * carried[h : h + 1]).astype(BF16)
+            state = jnp.dot(keyed, values[:, lanes], preferred_element_type=F32)
             out_ref[group, i * D : (i + 1) * D, :] = state.astype(BF16)
         cut_ref[0:GROUP, :] = total[group * GROUP : (group + 1) * GROUP, :]
         cut_ref[GROUP:8, :] = jnp.zeros((8 - GROUP, D), F32)

time: 86.1 us -> 86.1 us (level)
  no operation moved by 1% of the time
where the time goes in v6:
time: 86.1 us; the launch traced here: 86 us
  starting transfers between devices  40.2 us (47%)
  waiting for transfers between devices  25.6 us (30%)
  Pallas kernels  18.3 us (21%)
  local copies, waits for them, and re-layouts  1.42 us (2%)
    ppermute x18, starting transfers between devices, ring_exchange(): lax.ppermute(slots[d], axis, [(i, (i + d) % size) for i in range(size)])  28.7 us
    ppermute x18, waiting for transfers between devices, ring_exchange(): lax.ppermute(slots[d], axis, [(i, (i + d) % size) for i in range(size)])  11.2 us
    ppermute x3, starting transfers between devices, local(): lax.ppermute(both, 'z', [(i, (i + by) % NZ) for i in range(NZ)])  9.51 us
    pallas_call x11, Pallas kernels, small_call(): pl.pallas_call(body, out_shape=[jax.ShapeDtypeStruct(shape, dtype) for sh...  9.06 us
    ppermute x2, waiting for transfers between devices, swap_rows(): return lax.ppermute(array, 'z', [(i, i ^ 1) for i in range(NZ)])  6.99 us
    ppermute x3, waiting for transfers between devices, local(): lax.ppermute(both, 'z', [(i, (i + by) % NZ) for i in range(NZ)])  5.45 us
    pallas_call x2, Pallas kernels, intra_term(): pl.pallas_call(functools.partial(intra_kernel, wave), out_shape=[jax.Shap...  4.44 us
    pallas_call x2, Pallas kernels, place(): pl.pallas_call(functools.partial(place_kernel, wave), out_shape=jax.Shape...  2.73 us
  transfers between devices with their start and end apart: 25, of which 16 were waited for; matrix products, arithmetic and copies ran while one was open for 0% of the time, Pallas kernels for 12%

profile of v6, /device:TPU:8, one launch (start us, length us, event | category | flops | bytes accessed | tf_op | source)
XLA Modules:
  0.0 86.0 jit_solution(13501272734721770266)
XLA Ops:
  0.0 1.4 %dynamic-slice_bitcast_fusion = (bf16[128,2048]{1,0:T(8,128)(2,1)S(1)}, bf16[128,2048]{1,0:T(8,128)(2,1)S(1)}) fusion(bf16[1,1,128,4096]{3,2,1,0:T(8,128)(2,1)} %param.10, s32[]{:T(128)S(6)} %select_n.4, bf16[1,1,128,4096]{3,2,1,0:T(8,128)(2,1)} %param.9), kind=kLoop, calls=%fused_computation | loop fusion | bytes 2097156 | tf_op jit(solution)/shard_map/dynamic_slice | solution.py:430
  1.4 0.0 copy-start.1
  1.4 0.1 pad_add_fusion.index
  1.5 1.0 %shard_map.75 = bf16[4,544,128]{2,1,0:T(8,128)(2,1)S(1)} custom-call(s32[4]{0:T(128)S(1)} %pad_add_fusion.index, bf16[128,2048]{1,0:T(8,128)(2,1)S(1)} %get-tuple-element.70.k_ref, bf16[128,2048]{1,0:T(8,128)(2,1)S(1)} %get-tuple-element.69.v_ref, f32[32,128]{1,0:T(8,128)S(1)} %bitcast.27, s32[1,128]{1,0:T(1,128)S(1)} %copy-done.6), custom_call_target="tpu_custom_call" | custom-call | flops 67108864 | bytes 1572864 | tf_op jit(solution)/shard_map/pallas_call | solution.py:95
  2.5 0.1 collective-permute-start
  2.6 0.0 copy-done.1
  2.7 1.0 %shard_map.74.refs_0_ = bf16[4,544,128]{2,1,0:T(8,128)(2,1)S(1)} custom-call(s32[4]{0:T(128)S(1)} %pad_add_fusion.index, bf16[128,4096]{1,0:T(8,128)(2,1)S(1)} %bitcast.19, bf16[128,4096]{1,0:T(8,128)(2,1)S(1)} %bitcast.22, f32[32,128]{1,0:T(8,128)S(1)} %bitcast.28, s32[1,128]{1,0:T(1,128)S(1)} %copy-done.6), custom_call_target="tpu_custom_call" | custom-call | flops 67108864 | bytes 1572864 | tf_op jit(solution)/shard_map/pallas_call | solution.py:95
  3.7 0.0 copy-start
  3.7 0.9 collective-permute-done.refs_1_
  4.6 0.8 shard_map.76
  5.4 1.7 %collective-permute-start.1 = (bf16[544,128]{1,0:T(8,128)(2,1)S(1)}, bf16[544,128]{1,0:T(8,128)(2,1)S(1)}, u32[]{:S(2)}, u32[]{:S(2)}) collective-permute-start(bf16[544,128]{1,0:T(8,128)(2,1)S(1)} %get-tuple-element.40), channel_id=1, source_target_pairs={{0,2},{2,4},{4,6},{6,0},{1,3},{3,5},{5,7},{7,1},{8,10},{10,12},{12... | collective-permute-start | bytes 417800 | tf_op jit(solution)/shard_map/ppermute | solution.py:411
  7.0 2.7 %collective-permute-start.2 = (bf16[544,128]{1,0:T(8,128)(2,1)S(1)}, bf16[544,128]{1,0:T(8,128)(2,1)S(1)}, u32[]{:S(2)}, u32[]{:S(2)}) collective-permute-start(bf16[544,128]{1,0:T(8,128)(2,1)S(1)} %get-tuple-element.41), channel_id=1, source_target_pairs={{0,4},{2,6},{4,0},{6,2},{1,5},{3,7},{5,1},{7,3},{8,12},{10,14},{12... | collective-permute-start | bytes 417800 | tf_op jit(solution)/shard_map/ppermute | solution.py:411
  9.7 0.7 collective-permute-start.3
  10.4 2.2 %shard_map.77 = (f32[4,128,512]{2,1,0:T(8,128)S(1)}, bf16[4,128,8]{2,1,0:T(8,128)(2,1)S(1)}) custom-call(bf16[128,4096]{1,0:T(8,128)(2,1)S(1)} %bitcast.15, bf16[128,4096]{1,0:T(8,128)(2,1)S(1)} %bitcast.20, bf16[128,4096]{1,0:T(8,128)(2,1)S(1)} %bitcast.23, f32[32,128]{1,0:T(8,128)S(1)} %bitcast.29, s32[1,128]{1,0:T(1,128)S(1)} %copy-done.6), custom_call_target="tpu_custom_call" | custom-call | flops 134217728 | bytes 2621440 | tf_op jit(solution)/shard_map/pallas_call | solution.py:149
  12.6 2.5 %collective-permute-done.2.refs_2_.refs_4_ = bf16[544,128]{1,0:T(8,128)(2,1)S(1)} collective-permute-done((bf16[544,128]{1,0:T(8,128)(2,1)S(1)}, bf16[544,128]{1,0:T(8,128)(2,1)S(1)}, u32[]{:S(2)}, u32[]{:S(2)}) %collective-permute-start.2) | collective-permute-done | bytes 139296 | tf_op jit(solution)/shard_map/ppermute | solution.py:411
  15.1 1.9 %collective-permute-done.3.refs_3_.refs_5_ = bf16[544,128]{1,0:T(8,128)(2,1)S(1)} collective-permute-done((bf16[544,128]{1,0:T(8,128)(2,1)S(1)}, bf16[544,128]{1,0:T(8,128)(2,1)S(1)}, u32[]{:S(2)}, u32[]{:S(2)}) %collective-permute-start.3) | collective-permute-done | bytes 139296 | tf_op jit(solution)/shard_map/ppermute | solution.py:411
  16.9 0.7 shard_map.78
  17.6 1.3 %collective-permute-start.4 = (bf16[288,128]{1,0:T(8,128)(2,1)S(1)}, bf16[288,128]{1,0:T(8,128)(2,1)S(1)}, u32[]{:S(2)}, u32[]{:S(2)}) collective-permute-start(bf16[288,128]{1,0:T(8,128)(2,1)S(1)} %get-tuple-element.45), channel_id=1, source_target_pairs={{0,8},{8,0},{16,24},{24,16},{32,40},{40,32},{48,56},{56,48},{1,9},... | collective-permute-start | bytes 221192 | tf_op jit(solution)/shard_map/ppermute | solution.py:417
  19.0 3.1 %collective-permute-done.4.refs_1_ = bf16[288,128]{1,0:T(8,128)(2,1)S(1)} collective-permute-done((bf16[288,128]{1,0:T(8,128)(2,1)S(1)}, bf16[288,128]{1,0:T(8,128)(2,1)S(1)}, u32[]{:S(2)}, u32[]{:S(2)}) %collective-permute-start.4) | collective-permute-done | bytes 73760 | tf_op jit(solution)/shard_map/ppermute | solution.py:417
  22.1 0.6 shard_map.79
  22.7 5.7 %collective-permute-start.7 = (bf16[288,128]{1,0:T(8,128)(2,1)S(1)}, bf16[288,128]{1,0:T(8,128)(2,1)S(1)}, u32[]{:S(2)}, u32[]{:S(2)}) collective-permute-start(bf16[288,128]{1,0:T(8,128)(2,1)S(1)} %shard_map.79), channel_id=1, source_target_pairs={{0,48},{8,56},{16,0},{24,8},{32,16},{40,24},{48,32},{56,40},{1,49}... | collective-permute-start | bytes 221192 | tf_op jit(solution)/shard_map/ppermute | solution.py:449
  28.4 1.0 %collective-permute-start.6 = (bf16[288,128]{1,0:T(8,128)(2,1)S(1)}, bf16[288,128]{1,0:T(8,128)(2,1)S(1)}, u32[]{:S(2)}, u32[]{:S(2)}) collective-permute-start(bf16[288,128]{1,0:T(8,128)(2,1)S(1)} %shard_map.79), channel_id=1, source_target_pairs={{0,32},{8,40},{16,48},{24,56},{32,0},{40,8},{48,16},{56,24},{1,33}... | collective-permute-start | bytes 221192 | tf_op jit(solution)/shard_map/ppermute | solution.py:449
  29.4 2.8 %collective-permute-start.5 = (bf16[288,128]{1,0:T(8,128)(2,1)S(1)}, bf16[288,128]{1,0:T(8,128)(2,1)S(1)}, u32[]{:S(2)}, u32[]{:S(2)}) collective-permute-start(bf16[288,128]{1,0:T(8,128)(2,1)S(1)} %shard_map.79), channel_id=1, source_target_pairs={{0,16},{8,24},{16,32},{24,40},{32,48},{40,56},{48,0},{56,8},{1,17}... | collective-permute-start | bytes 221192 | tf_op jit(solution)/shard_map/ppermute | solution.py:449
  32.2 0.5 collective-permute-done.7.refs_4_
  32.6 4.5 %collective-permute-done.6.refs_3_ = bf16[288,128]{1,0:T(8,128)(2,1)S(1)} collective-permute-done((bf16[288,128]{1,0:T(8,128)(2,1)S(1)}, bf16[288,128]{1,0:T(8,128)(2,1)S(1)}, u32[]{:S(2)}, u32[]{:S(2)}) %collective-permute-start.6) | collective-permute-done | bytes 73760 | tf_op jit(solution)/shard_map/ppermute | solution.py:449
  37.1 0.5 collective-permute-done.5.refs_2_
  37.6 0.6 shard_map.80
  38.3 0.5 collective-permute-start.8
  38.7 3.9 %collective-permute-done.8.refs_1_ = bf16[256,128]{1,0:T(8,128)(2,1)S(1)} collective-permute-done((bf16[256,128]{1,0:T(8,128)(2,1)S(1)}, bf16[256,128]{1,0:T(8,128)(2,1)S(1)}, u32[]{:S(2)}, u32[]{:S(2)}) %collective-permute-start.8) | collective-permute-done | bytes 65568 | tf_op jit(solution)/shard_map/ppermute | solution.py:417
  42.6 0.8 shard_map.81
  43.4 1.3 %collective-permute-start.9 = (bf16[512,128]{1,0:T(8,128)(2,1)S(1)}, bf16[512,128]{1,0:T(8,128)(2,1)S(1)}, u32[]{:S(2)}, u32[]{:S(2)}) collective-permute-start(bf16[512,128]{1,0:T(8,128)(2,1)S(1)} %get-tuple-element.49), channel_id=1, source_target_pairs={{0,2},{2,4},{4,6},{6,0},{1,3},{3,5},{5,7},{7,1},{8,10},{10,12},{12... | collective-permute-start | bytes 393224 | tf_op jit(solution)/shard_map/ppermute | solution.py:411
  44.7 1.7 %collective-permute-start.10 = (bf16[512,128]{1,0:T(8,128)(2,1)S(1)}, bf16[512,128]{1,0:T(8,128)(2,1)S(1)}, u32[]{:S(2)}, u32[]{:S(2)}) collective-permute-start(bf16[512,128]{1,0:T(8,128)(2,1)S(1)} %get-tuple-element.50), channel_id=1, source_target_pairs={{0,4},{2,6},{4,0},{6,2},{1,5},{3,7},{5,1},{7,3},{8,12},{10,14},{12... | collective-permute-start | bytes 393224 | tf_op jit(solution)/shard_map/ppermute | solution.py:411
  46.3 1.5 %collective-permute-start.11 = (bf16[512,128]{1,0:T(8,128)(2,1)S(1)}, bf16[512,128]{1,0:T(8,128)(2,1)S(1)}, u32[]{:S(2)}, u32[]{:S(2)}) collective-permute-start(bf16[512,128]{1,0:T(8,128)(2,1)S(1)} %get-tuple-element.51), channel_id=1, source_target_pairs={{0,6},{2,0},{4,2},{6,4},{1,7},{3,1},{5,3},{7,5},{8,14},{10,8},{12,... | collective-permute-start | bytes 393224 | tf_op jit(solution)/shard_map/ppermute | solution.py:411
  47.8 2.2 %shard_map.73 = (f32[4,128,512]{2,1,0:T(8,128)S(1)}, bf16[4,128,8]{2,1,0:T(8,128)(2,1)S(1)}) custom-call(bf16[128,4096]{1,0:T(8,128)(2,1)S(1)} %bitcast.16, bf16[128,4096]{1,0:T(8,128)(2,1)S(1)} %bitcast.21, bf16[128,4096]{1,0:T(8,128)(2,1)S(1)} %bitcast.24, f32[32,128]{1,0:T(8,128)S(1)} %bitcast.30, s32[1,128]{1,0:T(1,128)S(1)} %copy-done.6), custom_call_target="tpu_custom_call" | custom-call | flops 134217728 | bytes 2621440 | tf_op jit(solution)/shard_map/pallas_call | solution.py:149
  50.1 1.2 %collective-permute-done.10.refs_4_ = bf16[512,128]{1,0:T(8,128)(2,1)S(1)} collective-permute-done((bf16[512,128]{1,0:T(8,128)(2,1)S(1)}, bf16[512,128]{1,0:T(8,128)(2,1)S(1)}, u32[]{:S(2)}, u32[]{:S(2)}) %collective-permute-start.10) | collective-permute-done | bytes 131104 | tf_op jit(solution)/shard_map/ppermute | solution.py:411
  51.2 1.3 %collective-permute-done.11.refs_5_ = bf16[512,128]{1,0:T(8,128)(2,1)S(1)} collective-permute-done((bf16[512,128]{1,0:T(8,128)(2,1)S(1)}, bf16[512,128]{1,0:T(8,128)(2,1)S(1)}, u32[]{:S(2)}, u32[]{:S(2)}) %collective-permute-start.11) | collective-permute-done | bytes 131104 | tf_op jit(solution)/shard_map/ppermute | solution.py:411
  52.5 0.8 shard_map.83
  53.3 0.0 copy-start.5
  53.3 0.1 collective-permute-start.12
  53.4 0.8 shard_map.82.refs_3_
  54.2 1.1 %collective-permute-done.12.refs_4_ = bf16[4,512,128]{2,1,0:T(8,128)(2,1)S(1)} collective-permute-done((bf16[4,512,128]{2,1,0:T(8,128)(2,1)S(1)}, bf16[4,512,128]{2,1,0:T(8,128)(2,1)S(1)}, u32[]{:S(2)}, u32[]{:S(2)}) %collective-permute-start.12) | collective-permute-done | bytes 524320 | tf_op jit(solution)/shard_map/ppermute | solution.py:421
  55.3 1.2 %shard_map.86 = (bf16[128,512]{1,0:T(8,128)(2,1)S(1)}, bf16[128,512]{1,0:T(8,128)(2,1)S(1)}, bf16[128,512]{1,0:T(8,128)(2,1)S(1)}, bf16[128,512]{1,0:T(8,128)(2,1)S(1)}) custom-call(s32[4]{0:T(128)S(1)} %pad_add_fusion.index, bf16[128,4096]{1,0:T(8,128)(2,1)S(1)} %bitcast.17, f32[4,128,512]{2,1,0:T(8,128)S(1)} %get-tuple-element.43.refs_4_.refs_1_, ...), custom_call_target="tpu_custom_call" | custom-call | flops 3162112 | bytes 6324224 | tf_op jit(solution)/shard_map/pallas_call | solution.py:205
  56.6 1.6 %collective-permute-start.19 = (bf16[128,512]{1,0:T(8,128)(2,1)S(1)}, bf16[128,512]{1,0:T(8,128)(2,1)S(1)}, u32[]{:S(2)}, u32[]{:S(2)}) collective-permute-start(bf16[128,512]{1,0:T(8,128)(2,1)S(1)} %get-tuple-element.62), channel_id=1, source_target_pairs={{0,64},{64,128},{128,192},{192,0},{1,65},{65,129},{129,193},{193,1... | collective-permute-start | bytes 393224 | tf_op jit(solution)/shard_map/ppermute | solution.py:411
  58.2 2.7 %collective-permute-start.20 = (bf16[128,512]{1,0:T(8,128)(2,1)S(1)}, bf16[128,512]{1,0:T(8,128)(2,1)S(1)}, u32[]{:S(2)}, u32[]{:S(2)}) collective-permute-start(bf16[128,512]{1,0:T(8,128)(2,1)S(1)} %get-tuple-element.63), channel_id=1, source_target_pairs={{0,128},{64,192},{128,0},{192,64},{1,129},{65,193},{129,1},{193,65... | collective-permute-start | bytes 393224 | tf_op jit(solution)/shard_map/ppermute | solution.py:411
  60.9 1.4 %collective-permute-start.21 = (bf16[128,512]{1,0:T(8,128)(2,1)S(1)}, bf16[128,512]{1,0:T(8,128)(2,1)S(1)}, u32[]{:S(2)}, u32[]{:S(2)}) collective-permute-start(bf16[128,512]{1,0:T(8,128)(2,1)S(1)} %get-tuple-element.64), channel_id=1, source_target_pairs={{0,192},{64,0},{128,64},{192,128},{1,193},{65,1},{129,65},{193,129... | collective-permute-start | bytes 393224 | tf_op jit(solution)/shard_map/ppermute | solution.py:411
  62.3 1.2 %shard_map.84 = (bf16[128,512]{1,0:T(8,128)(2,1)S(1)}, bf16[128,512]{1,0:T(8,128)(2,1)S(1)}, bf16[128,512]{1,0:T(8,128)(2,1)S(1)}, bf16[128,512]{1,0:T(8,128)(2,1)S(1)}) custom-call(s32[4]{0:T(128)S(1)} %pad_add_fusion.index, bf16[128,4096]{1,0:T(8,128)(2,1)S(1)} %bitcast.18, f32[4,128,512]{2,1,0:T(8,128)S(1)} %get-tuple-element.37.refs_6_.refs_1_, ...), custom_call_target="tpu_custom_call" | custom-call | flops 3162112 | bytes 6324224 | tf_op jit(solution)/shard_map/pallas_call | solution.py:205
  63.5 0.7 collective-permute-start.13
  64.2 0.9 %collective-permute-start.14 = (bf16[128,512]{1,0:T(8,128)(2,1)S(1)}, bf16[128,512]{1,0:T(8,128)(2,1)S(1)}, u32[]{:S(2)}, u32[]{:S(2)}) collective-permute-start(bf16[128,512]{1,0:T(8,128)(2,1)S(1)} %get-tuple-element.54), channel_id=1, source_target_pairs={{0,128},{64,192},{128,0},{192,64},{1,129},{65,193},{129,1},{193,65... | collective-permute-start | bytes 393224 | tf_op jit(solution)/shard_map/ppermute | solution.py:411
  65.1 1.9 %collective-permute-start.15 = (bf16[128,512]{1,0:T(8,128)(2,1)S(1)}, bf16[128,512]{1,0:T(8,128)(2,1)S(1)}, u32[]{:S(2)}, u32[]{:S(2)}) collective-permute-start(bf16[128,512]{1,0:T(8,128)(2,1)S(1)} %get-tuple-element.55), channel_id=1, source_target_pairs={{0,192},{64,0},{128,64},{192,128},{1,193},{65,1},{129,65},{193,129... | collective-permute-start | bytes 393224 | tf_op jit(solution)/shard_map/ppermute | solution.py:411
  67.0 1.0 %collective-permute-done.20.refs_3_ = bf16[128,512]{1,0:T(8,128)(2,1)S(1)} collective-permute-done((bf16[128,512]{1,0:T(8,128)(2,1)S(1)}, bf16[128,512]{1,0:T(8,128)(2,1)S(1)}, u32[]{:S(2)}, u32[]{:S(2)}) %collective-permute-start.20) | collective-permute-done | bytes 131104 | tf_op jit(solution)/shard_map/ppermute | solution.py:411
  68.0 0.8 shard_map.87
  68.8 1.0 %collective-permute-start.22 = (bf16[128,512]{1,0:T(8,128)(2,1)S(1)}, bf16[128,512]{1,0:T(8,128)(2,1)S(1)}, u32[]{:S(2)}, u32[]{:S(2)}) collective-permute-start(bf16[128,512]{1,0:T(8,128)(2,1)S(1)} %get-tuple-element.66), channel_id=1, source_target_pairs={{0,64},{64,128},{128,192},{192,0},{1,65},{65,129},{129,193},{193,1... | collective-permute-start | bytes 393224 | tf_op jit(solution)/shard_map/ppermute | solution.py:411
  69.8 2.1 %collective-permute-start.23 = (bf16[128,512]{1,0:T(8,128)(2,1)S(1)}, bf16[128,512]{1,0:T(8,128)(2,1)S(1)}, u32[]{:S(2)}, u32[]{:S(2)}) collective-permute-start(bf16[128,512]{1,0:T(8,128)(2,1)S(1)} %get-tuple-element.67), channel_id=1, source_target_pairs={{0,128},{64,192},{128,0},{192,64},{1,129},{65,193},{129,1},{193,65... | collective-permute-start | bytes 393224 | tf_op jit(solution)/shard_map/ppermute | solution.py:411
  71.9 0.4 collective-permute-done.13.refs_2_
  72.3 2.1 %collective-permute-start.24 = (bf16[128,512]{1,0:T(8,128)(2,1)S(1)}, bf16[128,512]{1,0:T(8,128)(2,1)S(1)}, u32[]{:S(2)}, u32[]{:S(2)}) collective-permute-start(bf16[128,512]{1,0:T(8,128)(2,1)S(1)} %get-tuple-element.68), channel_id=1, source_target_pairs={{0,192},{64,0},{128,64},{192,128},{1,193},{65,1},{129,65},{193,129... | collective-permute-start | bytes 393224 | tf_op jit(solution)/shard_map/ppermute | solution.py:411
  74.5 0.8 shard_map.85
  75.3 1.6 %collective-permute-start.16 = (bf16[128,512]{1,0:T(8,128)(2,1)S(1)}, bf16[128,512]{1,0:T(8,128)(2,1)S(1)}, u32[]{:S(2)}, u32[]{:S(2)}) collective-permute-start(bf16[128,512]{1,0:T(8,128)(2,1)S(1)} %get-tuple-element.57), channel_id=1, source_target_pairs={{0,64},{64,128},{128,192},{192,0},{1,65},{65,129},{129,193},{193,1... | collective-permute-start | bytes 393224 | tf_op jit(solution)/shard_map/ppermute | solution.py:411
  76.9 2.6 %collective-permute-start.17 = (bf16[128,512]{1,0:T(8,128)(2,1)S(1)}, bf16[128,512]{1,0:T(8,128)(2,1)S(1)}, u32[]{:S(2)}, u32[]{:S(2)}) collective-permute-start(bf16[128,512]{1,0:T(8,128)(2,1)S(1)} %get-tuple-element.58), channel_id=1, source_target_pairs={{0,128},{64,192},{128,0},{192,64},{1,129},{65,193},{129,1},{193,65... | collective-permute-start | bytes 393224 | tf_op jit(solution)/shard_map/ppermute | solution.py:411
  79.5 0.6 collective-permute-start.18
  80.1 1.4 %shard_map.88.refs_4_ = bf16[128,4096]{1,0:T(8,128)(2,1)} custom-call(s32[4]{0:T(128)S(1)} %pad_add_fusion.index, bf16[128,512]{1,0:T(8,128)(2,1)S(1)} %get-tuple-element.65.refs_0_, bf16[128,512]{1,0:T(8,128)(2,1)S(1)} %collective-permute-done.22.refs_1_, bf16[128,512]{1,0:T(8,128)(2,1)S(1)} %collective-permute-done.23.refs_2_, ...), custom_call_target="tpu_custom_call" | custom-call | bytes 1048576 | tf_op jit(solution)/shard_map/pallas_call | solution.py:392
  81.4 1.4 %collective-permute-done.16.refs_1_ = bf16[128,512]{1,0:T(8,128)(2,1)S(1)} collective-permute-done((bf16[128,512]{1,0:T(8,128)(2,1)S(1)}, bf16[128,512]{1,0:T(8,128)(2,1)S(1)}, u32[]{:S(2)}, u32[]{:S(2)}) %collective-permute-start.16) | collective-permute-done | bytes 131104 | tf_op jit(solution)/shard_map/ppermute | solution.py:411
  82.8 1.4 %collective-permute-done.17.refs_2_ = bf16[128,512]{1,0:T(8,128)(2,1)S(1)} collective-permute-done((bf16[128,512]{1,0:T(8,128)(2,1)S(1)}, bf16[128,512]{1,0:T(8,128)(2,1)S(1)}, u32[]{:S(2)}, u32[]{:S(2)}) %collective-permute-start.17) | collective-permute-done | bytes 131104 | tf_op jit(solution)/shard_map/ppermute | solution.py:411
  84.2 0.2 collective-permute-done.18.refs_3_
  84.4 1.4 %shard_map.89 = bf16[128,4096]{1,0:T(8,128)(2,1)} custom-call(s32[4]{0:T(128)S(1)} %pad_add_fusion.index, bf16[128,512]{1,0:T(8,128)(2,1)S(1)} %get-tuple-element.56.refs_0_, bf16[128,512]{1,0:T(8,128)(2,1)S(1)} %collective-permute-done.16.refs_1_, bf16[128,512]{1,0:T(8,128)(2,1)S(1)} %collective-permute-done.17.refs_2_, ...), custom_call_target="tpu_custom_call", output_to_operand_aliasing={{}: (5, {})} | custom-call | bytes 1048576 | tf_op jit(solution)/shard_map/pallas_call | solution.py:392
  (19 shorter events, 0.0 us)
Async XLA Ops:
  0.0 1.5 %copy-start.4 = (f32[1,1,32,128]{3,2,1,0:T(8,128)S(1)}, f32[1,1,32,128]{3,2,1,0:T(8,128)}, u32[]{:S(2)}) copy-start(f32[1,1,32,128]{3,2,1,0:T(8,128)} %param.12) | copy-start | bytes 49156
  0.0 1.5 %copy-start.6 = (s32[1,128]{1,0:T(1,128)S(1)}, s32[1,128]{1,0:T(1,128)}, u32[]{:S(2)}) copy-start(s32[1,128]{1,0:T(1,128)} %ids_ref.7) | copy-start | bytes 1540
  0.0 2.6 %copy-start.2 = (bf16[1,1,128,4096]{3,2,1,0:T(8,128)(2,1)S(1)}, bf16[1,1,128,4096]{3,2,1,0:T(8,128)(2,1)}, u32[]{:S(2)}) copy-start(bf16[1,1,128,4096]{3,2,1,0:T(8,128)(2,1)} %param.10) | copy-start | bytes 3145732
  1.4 1.3 %copy-start.1 = (bf16[1,1,128,4096]{3,2,1,0:T(8,128)(2,1)S(1)}, bf16[1,1,128,4096]{3,2,1,0:T(8,128)(2,1)}, u32[]{:S(2)}) copy-start(bf16[1,1,128,4096]{3,2,1,0:T(8,128)(2,1)} %param.9) | copy-start | bytes 3145732
  2.5 2.0 %collective-permute-start = (bf16[4,544,128]{2,1,0:T(8,128)(2,1)S(1)}, bf16[4,544,128]{2,1,0:T(8,128)(2,1)S(1)}, u32[]{:S(2)}, u32[]{:S(2)}) collective-permute-start(bf16[4,544,128]{2,1,0:T(8,128)(2,1)S(1)} %shard_map.75), channel_id=1, source_target_pairs={{0,1},{1,0},{2,3},{3,2},{4,5},{5,4},{6,7},{7,6},{8,9},{9,8},{10,11... | collective-permute-start | bytes 1671176 | tf_op jit(solution)/shard_map/ppermute | solution.py:421
  3.7 6.7 %copy-start = (bf16[1,1,128,4096]{3,2,1,0:T(8,128)(2,1)S(1)}, bf16[1,1,128,4096]{3,2,1,0:T(8,128)(2,1)}, u32[]{:S(2)}) copy-start(bf16[1,1,128,4096]{3,2,1,0:T(8,128)(2,1)} %param.8) | copy-start | bytes 3145732
  5.4 7.2 %collective-permute-start.1 = (bf16[544,128]{1,0:T(8,128)(2,1)S(1)}, bf16[544,128]{1,0:T(8,128)(2,1)S(1)}, u32[]{:S(2)}, u32[]{:S(2)}) collective-permute-start(bf16[544,128]{1,0:T(8,128)(2,1)S(1)} %get-tuple-element.40), channel_id=1, source_target_pairs={{0,2},{2,4},{4,6},{6,0},{1,3},{3,5},{5,7},{7,1},{8,10},{10,12},{12... | collective-permute-start | bytes 417800 | tf_op jit(solution)/shard_map/ppermute | solution.py:411
  7.0 8.1 %collective-permute-start.2 = (bf16[544,128]{1,0:T(8,128)(2,1)S(1)}, bf16[544,128]{1,0:T(8,128)(2,1)S(1)}, u32[]{:S(2)}, u32[]{:S(2)}) collective-permute-start(bf16[544,128]{1,0:T(8,128)(2,1)S(1)} %get-tuple-element.41), channel_id=1, source_target_pairs={{0,4},{2,6},{4,0},{6,2},{1,5},{3,7},{5,1},{7,3},{8,12},{10,14},{12... | collective-permute-start | bytes 417800 | tf_op jit(solution)/shard_map/ppermute | solution.py:411
  9.7 7.3 %collective-permute-start.3 = (bf16[544,128]{1,0:T(8,128)(2,1)S(1)}, bf16[544,128]{1,0:T(8,128)(2,1)S(1)}, u32[]{:S(2)}, u32[]{:S(2)}) collective-permute-start(bf16[544,128]{1,0:T(8,128)(2,1)S(1)} %get-tuple-element.42), channel_id=1, source_target_pairs={{0,6},{2,0},{4,2},{6,4},{1,7},{3,1},{5,3},{7,5},{8,14},{10,8},{12,... | collective-permute-start | bytes 417800 | tf_op jit(solution)/shard_map/ppermute | solution.py:411
  17.6 4.4 %collective-permute-start.4 = (bf16[288,128]{1,0:T(8,128)(2,1)S(1)}, bf16[288,128]{1,0:T(8,128)(2,1)S(1)}, u32[]{:S(2)}, u32[]{:S(2)}) collective-permute-start(bf16[288,128]{1,0:T(8,128)(2,1)S(1)} %get-tuple-element.45), channel_id=1, source_target_pairs={{0,8},{8,0},{16,24},{24,16},{32,40},{40,32},{48,56},{56,48},{1,9},... | collective-permute-start | bytes 221192 | tf_op jit(solution)/shard_map/ppermute | solution.py:417
  22.7 10.0 %collective-permute-start.7 = (bf16[288,128]{1,0:T(8,128)(2,1)S(1)}, bf16[288,128]{1,0:T(8,128)(2,1)S(1)}, u32[]{:S(2)}, u32[]{:S(2)}) collective-permute-start(bf16[288,128]{1,0:T(8,128)(2,1)S(1)} %shard_map.79), channel_id=1, source_target_pairs={{0,48},{8,56},{16,0},{24,8},{32,16},{40,24},{48,32},{56,40},{1,49}... | collective-permute-start | bytes 221192 | tf_op jit(solution)/shard_map/ppermute | solution.py:449
  28.4 8.8 %collective-permute-start.6 = (bf16[288,128]{1,0:T(8,128)(2,1)S(1)}, bf16[288,128]{1,0:T(8,128)(2,1)S(1)}, u32[]{:S(2)}, u32[]{:S(2)}) collective-permute-start(bf16[288,128]{1,0:T(8,128)(2,1)S(1)} %shard_map.79), channel_id=1, source_target_pairs={{0,32},{8,40},{16,48},{24,56},{32,0},{40,8},{48,16},{56,24},{1,33}... | collective-permute-start | bytes 221192 | tf_op jit(solution)/shard_map/ppermute | solution.py:449
  29.4 8.3 %collective-permute-start.5 = (bf16[288,128]{1,0:T(8,128)(2,1)S(1)}, bf16[288,128]{1,0:T(8,128)(2,1)S(1)}, u32[]{:S(2)}, u32[]{:S(2)}) collective-permute-start(bf16[288,128]{1,0:T(8,128)(2,1)S(1)} %shard_map.79), channel_id=1, source_target_pairs={{0,16},{8,24},{16,32},{24,40},{32,48},{40,56},{48,0},{56,8},{1,17}... | collective-permute-start | bytes 221192 | tf_op jit(solution)/shard_map/ppermute | solution.py:449
  38.3 4.4 %collective-permute-start.8 = (bf16[256,128]{1,0:T(8,128)(2,1)S(1)}, bf16[256,128]{1,0:T(8,128)(2,1)S(1)}, u32[]{:S(2)}, u32[]{:S(2)}) collective-permute-start(bf16[256,128]{1,0:T(8,128)(2,1)S(1)} %get-tuple-element.47), channel_id=1, source_target_pairs={{0,8},{8,0},{16,24},{24,16},{32,40},{40,32},{48,56},{56,48},{1,9},... | collective-permute-start | bytes 196616 | tf_op jit(solution)/shard_map/ppermute | solution.py:417
  43.4 6.7 %collective-permute-start.9 = (bf16[512,128]{1,0:T(8,128)(2,1)S(1)}, bf16[512,128]{1,0:T(8,128)(2,1)S(1)}, u32[]{:S(2)}, u32[]{:S(2)}) collective-permute-start(bf16[512,128]{1,0:T(8,128)(2,1)S(1)} %get-tuple-element.49), channel_id=1, source_target_pairs={{0,2},{2,4},{4,6},{6,0},{1,3},{3,5},{5,7},{7,1},{8,10},{10,12},{12... | collective-permute-start | bytes 393224 | tf_op jit(solution)/shard_map/ppermute | solution.py:411
  44.7 6.6 %collective-permute-start.10 = (bf16[512,128]{1,0:T(8,128)(2,1)S(1)}, bf16[512,128]{1,0:T(8,128)(2,1)S(1)}, u32[]{:S(2)}, u32[]{:S(2)}) collective-permute-start(bf16[512,128]{1,0:T(8,128)(2,1)S(1)} %get-tuple-element.50), channel_id=1, source_target_pairs={{0,4},{2,6},{4,0},{6,2},{1,5},{3,7},{5,1},{7,3},{8,12},{10,14},{12... | collective-permute-start | bytes 393224 | tf_op jit(solution)/shard_map/ppermute | solution.py:411
  46.3 6.2 %collective-permute-start.11 = (bf16[512,128]{1,0:T(8,128)(2,1)S(1)}, bf16[512,128]{1,0:T(8,128)(2,1)S(1)}, u32[]{:S(2)}, u32[]{:S(2)}) collective-permute-start(bf16[512,128]{1,0:T(8,128)(2,1)S(1)} %get-tuple-element.51), channel_id=1, source_target_pairs={{0,6},{2,0},{4,2},{6,4},{1,7},{3,1},{5,3},{7,5},{8,14},{10,8},{12,... | collective-permute-start | bytes 393224 | tf_op jit(solution)/shard_map/ppermute | solution.py:411
  53.3 2.0 %copy-start.5 = (bf16[1,4096]{1,0:T(2,128)(2,1)S(1)}, bf16[1,4096]{1,0:T(2,128)(2,1)}, u32[]{:S(2)}) copy-start(bf16[1,4096]{1,0:T(2,128)(2,1)} %param.11) | copy-start | bytes 24580
  53.3 2.0 %collective-permute-start.12 = (bf16[4,512,128]{2,1,0:T(8,128)(2,1)S(1)}, bf16[4,512,128]{2,1,0:T(8,128)(2,1)S(1)}, u32[]{:S(2)}, u32[]{:S(2)}) collective-permute-start(bf16[4,512,128]{2,1,0:T(8,128)(2,1)S(1)} %shard_map.83), channel_id=1, source_target_pairs={{0,1},{1,0},{2,3},{3,2},{4,5},{5,4},{6,7},{7,6},{8,9},{9,8},{10,11... | collective-permute-start | bytes 1572872 | tf_op jit(solution)/shard_map/ppermute | solution.py:421
  56.6 8.5 %collective-permute-start.19 = (bf16[128,512]{1,0:T(8,128)(2,1)S(1)}, bf16[128,512]{1,0:T(8,128)(2,1)S(1)}, u32[]{:S(2)}, u32[]{:S(2)}) collective-permute-start(bf16[128,512]{1,0:T(8,128)(2,1)S(1)} %get-tuple-element.62), channel_id=1, source_target_pairs={{0,64},{64,128},{128,192},{192,0},{1,65},{65,129},{129,193},{193,1... | collective-permute-start | bytes 393224 | tf_op jit(solution)/shard_map/ppermute | solution.py:411
  58.2 9.9 %collective-permute-start.20 = (bf16[128,512]{1,0:T(8,128)(2,1)S(1)}, bf16[128,512]{1,0:T(8,128)(2,1)S(1)}, u32[]{:S(2)}, u32[]{:S(2)}) collective-permute-start(bf16[128,512]{1,0:T(8,128)(2,1)S(1)} %get-tuple-element.63), channel_id=1, source_target_pairs={{0,128},{64,192},{128,0},{192,64},{1,129},{65,193},{129,1},{193,65... | collective-permute-start | bytes 393224 | tf_op jit(solution)/shard_map/ppermute | solution.py:411
  60.9 7.1 %collective-permute-start.21 = (bf16[128,512]{1,0:T(8,128)(2,1)S(1)}, bf16[128,512]{1,0:T(8,128)(2,1)S(1)}, u32[]{:S(2)}, u32[]{:S(2)}) collective-permute-start(bf16[128,512]{1,0:T(8,128)(2,1)S(1)} %get-tuple-element.64), channel_id=1, source_target_pairs={{0,192},{64,0},{128,64},{192,128},{1,193},{65,1},{129,65},{193,129... | collective-permute-start | bytes 393224 | tf_op jit(solution)/shard_map/ppermute | solution.py:411
  62.3 5.7 %copy-start.3 = (bf16[1,128,1024]{2,1,0:T(8,128)(2,1)S(1)}, bf16[1,128,1024]{2,1,0:T(8,128)(2,1)}, u32[]{:S(2)}) copy-start(bf16[1,128,1024]{2,1,0:T(8,128)(2,1)} %param.7) | copy-start | bytes 786436
  63.5 8.8 %collective-permute-start.13 = (bf16[128,512]{1,0:T(8,128)(2,1)S(1)}, bf16[128,512]{1,0:T(8,128)(2,1)S(1)}, u32[]{:S(2)}, u32[]{:S(2)}) collective-permute-start(bf16[128,512]{1,0:T(8,128)(2,1)S(1)} %get-tuple-element.53), channel_id=1, source_target_pairs={{0,64},{64,128},{128,192},{192,0},{1,65},{65,129},{129,193},{193,1... | collective-permute-start | bytes 393224 | tf_op jit(solution)/shard_map/ppermute | solution.py:411
  64.2 10.2 %collective-permute-start.14 = (bf16[128,512]{1,0:T(8,128)(2,1)S(1)}, bf16[128,512]{1,0:T(8,128)(2,1)S(1)}, u32[]{:S(2)}, u32[]{:S(2)}) collective-permute-start(bf16[128,512]{1,0:T(8,128)(2,1)S(1)} %get-tuple-element.54), channel_id=1, source_target_pairs={{0,128},{64,192},{128,0},{192,64},{1,129},{65,193},{129,1},{193,65... | collective-permute-start | bytes 393224 | tf_op jit(solution)/shard_map/ppermute | solution.py:411
  65.1 9.4 %collective-permute-start.15 = (bf16[128,512]{1,0:T(8,128)(2,1)S(1)}, bf16[128,512]{1,0:T(8,128)(2,1)S(1)}, u32[]{:S(2)}, u32[]{:S(2)}) collective-permute-start(bf16[128,512]{1,0:T(8,128)(2,1)S(1)} %get-tuple-element.55), channel_id=1, source_target_pairs={{0,192},{64,0},{128,64},{192,128},{1,193},{65,1},{129,65},{193,129... | collective-permute-start | bytes 393224 | tf_op jit(solution)/shard_map/ppermute | solution.py:411
  68.8 10.7 %collective-permute-start.22 = (bf16[128,512]{1,0:T(8,128)(2,1)S(1)}, bf16[128,512]{1,0:T(8,128)(2,1)S(1)}, u32[]{:S(2)}, u32[]{:S(2)}) collective-permute-start(bf16[128,512]{1,0:T(8,128)(2,1)S(1)} %get-tuple-element.66), channel_id=1, source_target_pairs={{0,64},{64,128},{128,192},{192,0},{1,65},{65,129},{129,193},{193,1... | collective-permute-start | bytes 393224 | tf_op jit(solution)/shard_map/ppermute | solution.py:411
  69.8 10.3 %collective-permute-start.23 = (bf16[128,512]{1,0:T(8,128)(2,1)S(1)}, bf16[128,512]{1,0:T(8,128)(2,1)S(1)}, u32[]{:S(2)}, u32[]{:S(2)}) collective-permute-start(bf16[128,512]{1,0:T(8,128)(2,1)S(1)} %get-tuple-element.67), channel_id=1, source_target_pairs={{0,128},{64,192},{128,0},{192,64},{1,129},{65,193},{129,1},{193,65... | collective-permute-start | bytes 393224 | tf_op jit(solution)/shard_map/ppermute | solution.py:411
  72.3 7.8 %collective-permute-start.24 = (bf16[128,512]{1,0:T(8,128)(2,1)S(1)}, bf16[128,512]{1,0:T(8,128)(2,1)S(1)}, u32[]{:S(2)}, u32[]{:S(2)}) collective-permute-start(bf16[128,512]{1,0:T(8,128)(2,1)S(1)} %get-tuple-element.68), channel_id=1, source_target_pairs={{0,192},{64,0},{128,64},{192,128},{1,193},{65,1},{129,65},{193,129... | collective-permute-start | bytes 393224 | tf_op jit(solution)/shard_map/ppermute | solution.py:411
  75.3 7.6 %collective-permute-start.16 = (bf16[128,512]{1,0:T(8,128)(2,1)S(1)}, bf16[128,512]{1,0:T(8,128)(2,1)S(1)}, u32[]{:S(2)}, u32[]{:S(2)}) collective-permute-start(bf16[128,512]{1,0:T(8,128)(2,1)S(1)} %get-tuple-element.57), channel_id=1, source_target_pairs={{0,64},{64,128},{128,192},{192,0},{1,65},{65,129},{129,193},{193,1... | collective-permute-start | bytes 393224 | tf_op jit(solution)/shard_map/ppermute | solution.py:411
  76.9 7.4 %collective-permute-start.17 = (bf16[128,512]{1,0:T(8,128)(2,1)S(1)}, bf16[128,512]{1,0:T(8,128)(2,1)S(1)}, u32[]{:S(2)}, u32[]{:S(2)}) collective-permute-start(bf16[128,512]{1,0:T(8,128)(2,1)S(1)} %get-tuple-element.58), channel_id=1, source_target_pairs={{0,128},{64,192},{128,0},{192,64},{1,129},{65,193},{129,1},{193,65... | collective-permute-start | bytes 393224 | tf_op jit(solution)/shard_map/ppermute | solution.py:411
  79.5 5.0 %collective-permute-start.18 = (bf16[128,512]{1,0:T(8,128)(2,1)S(1)}, bf16[128,512]{1,0:T(8,128)(2,1)S(1)}, u32[]{:S(2)}, u32[]{:S(2)}) collective-permute-start(bf16[128,512]{1,0:T(8,128)(2,1)S(1)} %get-tuple-element.59), channel_id=1, source_target_pairs={{0,192},{64,0},{128,64},{192,128},{1,193},{65,1},{129,65},{193,129... | collective-permute-start | bytes 393224 | tf_op jit(solution)/shard_map/ppermute | solution.py:411
